TPU v7x, 128 devices: a whole 4x4x4 slice. The times are simulated.
128 devices in a mesh: row: 8 (over z, core), col: 16 (over y, x).
Axes of the slice: x: 4, y: 4, z: 4, core: 2. Of those that a mesh axis runs over, the one named last changes fastest.
Arguments:
- noise: float32 [4096, 2048], P(('row', 'col')), may hold values from -22 to 22
- data: float32 [16384, 2048], P(('col', 'row')), may hold values from -22 to 22
- times: float32 [4096], P(('row', 'col')), may hold values from 0 to 1
Outputs:
- path: float32 [4096, 2048], P(('row', 'col'))
- velocity: float32 [4096, 2048], P(('row', 'col'))
All inputs are finite; a program needn't handle non-finite values.
Results may differ from a plain program's by a relative error of at most 0.0003.
Values sent between devices are 32-bit elements; how exact they have to be, the bound alone decides.
No kernel may reach another device: no remote copies, remote signals or barrier semaphores. Data moves between devices by JAX's collectives and lax.ppermute only.
A program may use at most 192 MiB of HBM per device.

v0:
```python
import math

import jax
import jax.numpy as jnp
from jax import lax
from jax.sharding import PartitionSpec as P

ITERS = 2


epsilon = 0.05
highest = lax.Precision.HIGHEST


def cost_block(rows, row_norms, cols, col_norms):
    cross = lax.dot_general(rows, cols, (((1,), (1,)), ((), ())), precision=highest)
    return (row_norms[:, None] + col_norms[None, :] - 2.0 * cross) / rows.shape[1]


def per_device(noise, data, times):
    rows_all = lax.all_gather(noise, "col", axis=0, tiled=True)
    cols_all = lax.all_gather(data, "row", axis=0, tiled=True)
    features = noise.shape[1]
    row_count = rows_all.shape[0]
    col_count = cols_all.shape[0]
    total_noise = row_count * lax.axis_size("row")
    total_data = col_count * lax.axis_size("col")
    block_rows = min(512, row_count)
    block_count = row_count // block_rows
    row_norms = jnp.sum(rows_all * rows_all, axis=1)
    col_norms = jnp.sum(cols_all * cols_all, axis=1)
    row_blocks = rows_all.reshape(block_count, block_rows, features)
    norm_blocks = row_norms.reshape(block_count, block_rows)

    def scores_rows(rows, norms, col_pot):
        return (col_pot[None, :] - cost_block(rows, norms, cols_all, col_norms)) / epsilon

    def scores_cols(rows, norms, pot_piece):
        return (pot_piece[:, None] - cost_block(rows, norms, cols_all, col_norms)) / epsilon

    col_pot = jnp.zeros((col_count,), jnp.float32)
    for step in range(ITERS):
        row_peaks = lax.map(
            lambda args: jnp.max(scores_rows(args[0], args[1], col_pot), axis=1),
            (row_blocks, norm_blocks),
        ).reshape(row_count)
        row_peaks = lax.pmax(row_peaks, "col")
        row_totals = lax.map(
            lambda args: jnp.sum(
                jnp.exp(scores_rows(args[0], args[1], col_pot) - args[2][:, None]), axis=1
            ),
            (row_blocks, norm_blocks, row_peaks.reshape(block_count, block_rows)),
        ).reshape(row_count)
        row_totals = lax.psum(row_totals, "col")
        row_pot = epsilon * math.log(total_data) - epsilon * (row_peaks + jnp.log(row_totals))
        pot_blocks = row_pot.reshape(block_count, block_rows)
        lowest = jnp.full((col_count,), -jnp.inf, jnp.float32)
        nothing = jnp.zeros((col_count,), jnp.float32)

        def peak_step(carry, args):
            return (
                jnp.maximum(carry, jnp.max(scores_cols(args[0], args[1], args[2]), axis=0)),
                None,
            )

        col_peaks, _ = lax.scan(peak_step, lowest, (row_blocks, norm_blocks, pot_blocks))
        col_peaks = lax.pmax(col_peaks, "row")

        def total_step(carry, args):
            scores = scores_cols(args[0], args[1], args[2])
            return (carry + jnp.sum(jnp.exp(scores - col_peaks[None, :]), axis=0), None)

        totals, _ = lax.scan(total_step, nothing, (row_blocks, norm_blocks, pot_blocks))
        totals = lax.psum(totals, "row")
        col_pot = epsilon * math.log(total_noise) - epsilon * (col_peaks + jnp.log(totals))

    def shifted_sums(rows, norms, shift):
        weights = jnp.exp(scores_rows(rows, norms, col_pot) - shift[:, None])
        denom = jnp.sum(weights, axis=1)
        numer = jnp.dot(weights, cols_all, precision=highest)
        return (denom, numer)

    peaks = lax.map(
        lambda args: jnp.max(scores_rows(args[0], args[1], col_pot), axis=1),
        (row_blocks, norm_blocks),
    ).reshape(row_count)
    peaks = lax.pmax(peaks, "col")
    denoms, numers = lax.map(
        lambda args: shifted_sums(args[0], args[1], args[2]),
        (row_blocks, norm_blocks, peaks.reshape(block_count, block_rows)),
    )
    denoms = denoms.reshape(row_count)
    numers = numers.reshape(row_count, features)
    denoms, numers = (
        lax.psum_scatter(denoms, "col", scatter_dimension=0, tiled=True),
        lax.psum_scatter(numers, "col", scatter_dimension=0, tiled=True),
    )
    targets = numers / denoms[:, None]
    path = (1.0 - times)[:, None] * noise + times[:, None] * targets
    velocity = targets - noise
    return (path, velocity)


def solution(mesh):
    in_specs = (P(("row", "col"), None), P(("col", "row"), None), P(("row", "col")))
    out_specs = (P(("row", "col"), None), P(("row", "col"), None))
    return jax.shard_map(
        per_device, mesh=mesh, in_specs=in_specs, out_specs=out_specs, check_vma=False
    )
```

profile of v0, /device:TPU:0, one launch (start us, length us, event | category | flops | bytes accessed | tf_op | source)
XLA Modules:
  0.0 474.4 jit_solution(9857244743818793593)
XLA Ops:
  7.2 0.7 all-gather.3.cloned.1.call-update
  7.9 0.7 all-gather.5.cloned.1.call-update
  8.7 55.3 %all-gather.3.cloned.1.call-done = f32[512,2048]{1,0:T(8,128)} async-done(((f32[32,2048]{1,0:T(8,128)}), f32[512,2048]{1,0:T(8,128)}) %all-gather.3.cloned.1.call-update) | async-done | bytes 4194320 | tf_op jit(solution)/shard_map/all_gather | solution.py:21
  64.0 2.5 multiply_reduce_fusion.1
  66.6 48.9 %all-gather.5.cloned.1.call-done = f32[1024,2048]{1,0:T(8,128)} async-done(((f32[128,2048]{1,0:T(8,128)}), f32[1024,2048]{1,0:T(8,128)}) %all-gather.5.cloned.1.call-update) | async-done | bytes 8388624 | tf_op jit(solution)/shard_map/all_gather | solution.py:22
  115.4 4.1 multiply_reduce_fusion
  119.6 1.6 copy-done
  121.2 16.5 %fusion = (f32[512]{0:T(512)S(1)}, f32[512,1024]{1,0:T(8,128)S(1)}) fusion(f32[512,2048]{1,0:T(8,128)} %all-gather.3.cloned.1.call-done, f32[1024,2048]{1,0:T(8,128)S(1)} %copy-done, f32[1024]{0:T(1024)S(1)} %multiply_reduce_fusion, f32[512]{0:T(512)S(1)} %multiply_reduce_fusion.1), kind=kOutput, calls=%fused_computation.13 | convolution fusion | flops 12888571904 | bytes 14688256 | tf_op jit(solution)/shard_map/while/body/eval_jaxpr/dot_general | solution.py:16
  137.7 40.3 %pmax.35 = f32[512]{0:T(512)S(1)} all-reduce(f32[512]{0:T(512)S(1)} %get-tuple-element.156), channel_id=1, replica_groups=mesh['row'=8,'col'=16] {'col'}, use_global_device_ids=true, to_apply=%region_3.4 | all-reduce | flops 512 | bytes 4096 | tf_op jit(solution)/shard_map/pmax | solution.py:47
  178.6 35.5 %psum.28 = f32[512]{0:T(512)S(1)} all-reduce(f32[512]{0:T(512)S(1)} %exponential_reduce_fusion.3), channel_id=1, replica_groups=mesh['row'=8,'col'=16] {'col'}, use_global_device_ids=true, to_apply=%region_5.6 | all-reduce | flops 512 | bytes 4096 | tf_op jit(solution)/shard_map/psum | solution.py:54
  214.4 12.4 %pmax.36 = f32[1024]{0:T(1024)S(1)} all-reduce(f32[1024]{0:T(1024)S(1)} %fusion.1), channel_id=1, replica_groups=mesh['row'=8,'col'=16] {'row'}, use_global_device_ids=true, to_apply=%region_7.8 | all-reduce | flops 1024 | bytes 8192 | tf_op jit(solution)/shard_map/pmax | solution.py:67
  227.3 12.4 %psum.29 = f32[1024]{0:T(1024)S(1)} all-reduce(f32[1024]{0:T(1024)S(1)} %exponential_reduce_fusion.2), channel_id=1, replica_groups=mesh['row'=8,'col'=16] {'row'}, use_global_device_ids=true, to_apply=%region_9.10 | all-reduce | flops 1024 | bytes 8192 | tf_op jit(solution)/shard_map/psum | solution.py:74
  240.0 37.5 %pmax.37 = f32[512]{0:T(512)S(1)} all-reduce(f32[512]{0:T(512)S(1)} %fusion.2), channel_id=1, replica_groups=mesh['row'=8,'col'=16] {'col'}, use_global_device_ids=true, to_apply=%region_11.12 | all-reduce | flops 512 | bytes 4096 | tf_op jit(solution)/shard_map/pmax | solution.py:47
  277.5 0.6 exponential_reduce_fusion.1
  278.1 35.5 %psum.30 = f32[512]{0:T(512)S(1)} all-reduce(f32[512]{0:T(512)S(1)} %exponential_reduce_fusion.1), channel_id=1, replica_groups=mesh['row'=8,'col'=16] {'col'}, use_global_device_ids=true, to_apply=%region_13.14 | all-reduce | flops 512 | bytes 4096 | tf_op jit(solution)/shard_map/psum | solution.py:54
  313.8 12.6 %pmax.38 = f32[1024]{0:T(1024)S(1)} all-reduce(f32[1024]{0:T(1024)S(1)} %fusion.3), channel_id=1, replica_groups=mesh['row'=8,'col'=16] {'row'}, use_global_device_ids=true, to_apply=%region_15.16 | all-reduce | flops 1024 | bytes 8192 | tf_op jit(solution)/shard_map/pmax | solution.py:67
  326.9 12.4 %psum.31 = f32[1024]{0:T(1024)S(1)} all-reduce(f32[1024]{0:T(1024)S(1)} %exponential_reduce_fusion), channel_id=1, replica_groups=mesh['row'=8,'col'=16] {'row'}, use_global_device_ids=true, to_apply=%region_17.18 | all-reduce | flops 1024 | bytes 8192 | tf_op jit(solution)/shard_map/psum | solution.py:74
  339.7 37.5 %pmax.39 = f32[512]{0:T(512)S(1)} all-reduce(f32[512]{0:T(512)S(1)} %fusion.4), channel_id=1, replica_groups=mesh['row'=8,'col'=16] {'col'}, use_global_device_ids=true, to_apply=%region_19.20 | all-reduce | flops 512 | bytes 4096 | tf_op jit(solution)/shard_map/pmax | solution.py:87
  377.1 17.9 %fusion.6 = f32[512,2048]{1,0:T(8,128)} fusion(f32[1024,2048]{1,0:T(8,128)} %all-gather.5.cloned.1.call-done, f32[512,1024]{1,0:T(8,128)S(1)} %get-tuple-element.157, f32[512]{0:T(512)S(1)} %pmax.39, f32[1024]{0:T(1024)S(1)} %multiply_subtract_fusion), kind=kOutput, calls=%fused_computation.19 | convolution fusion | flops 12886474752 | bytes 14686208 | tf_op jit(solution)/shard_map/while/body/eval_jaxpr/dot_general | solution.py:80
  395.0 0.6 copy-done.3
  395.6 0.6 dynamic-slice.7
  397.5 35.7 %all-reduce = f32[512]{0:T(512)S(1)} all-reduce(f32[512]{0:T(512)S(1)} %fusion.5), channel_id=3, replica_groups=mesh['row'=8,'col'=16] {'col'}, use_global_device_ids=true, to_apply=%region_22.23.clone | all-reduce | flops 512 | bytes 4096
  433.3 32.7 %reduce-scatter.2.cloned.1.call-done = f32[32,2048]{1,0:T(8,128)} async-done(((f32[512,2048]{1,0:T(8,128)}), f32[32,2048]{1,0:T(8,128)}) %reduce-scatter.2.cloned.1.call-update) | async-done | bytes 262160 | tf_op jit(solution)/shard_map/reduce_scatter | solution.py:96
  466.0 1.9 fusion.10
  (24 shorter events, 3.5 us)
Async XLA Ops:
  7.2 56.9 %all-gather.3.cloned.1.call-start = ((), (), s32[]{:S(2)}) async-start(), calls=%async_computation.1 | async-start | bytes 4456448 | tf_op jit(solution)/shard_map/all_gather | solution.py:21
  7.9 107.5 %all-gather.5.cloned.1.call-start = ((), (), s32[]{:S(2)}) async-start(), calls=%async_computation.2 | async-start | bytes 9437184 | tf_op jit(solution)/shard_map/all_gather | solution.py:22
  8.6 457.3 %reduce-scatter.2.cloned.1.call-start = ((), (), s32[]{:S(2)}) async-start(), calls=%async_computation.3 | async-start | bytes 4456448 | tf_op jit(solution)/shard_map/reduce_scatter | solution.py:96
  115.4 5.8 %copy-start = (f32[1024,2048]{1,0:T(8,128)S(1)}, f32[1024,2048]{1,0:T(8,128)}, u32[]{:S(2)}) copy-start(f32[1024,2048]{1,0:T(8,128)} %all-gather.5.cloned.1.call-done) | copy-start | bytes 25165828
  395.0 0.7 copy-start.3
  395.0 1.9 copy-start.2
  395.0 71.0 %copy-start.1 = (f32[32,2048]{1,0:T(8,128)S(1)}, f32[32,2048]{1,0:T(8,128)}, u32[]{:S(2)}) copy-start(f32[32,2048]{1,0:T(8,128)} %param.3) | copy-start | bytes 786436
Sparse Core Ops, SparseCore 0:
  10.1 53.8 all-gather.2
  65.7 49.6 all-gather.4
  395.1 70.8 reduce-scatter.1
where the time goes:
time: 475 us; the launch traced here: 474 us
  blocking collectives  272 us (57%)
  waiting for transfers between devices  138 us (29%)
  matrix products  34.4 us (7%)
  between operations  14.5 us (3%)
  other arithmetic  12.4 us (3%)
    pmax x2, blocking collectives, per_device(): row_peaks = lax.pmax(row_peaks, 'col')  77.8 us
    psum x2, blocking collectives, per_device(): row_totals = lax.psum(row_totals, 'col')  70.9 us
    all_gather x1, waiting for transfers between devices, per_device(): rows_all = lax.all_gather(noise, 'col', axis=0, tiled=True)  55.3 us
    all_gather x1, waiting for transfers between devices, per_device(): cols_all = lax.all_gather(data, 'row', axis=0, tiled=True)  48.9 us
    pmax x1, blocking collectives, per_device(): peaks = lax.pmax(peaks, 'col')  37.5 us
    unnamed x1, blocking collectives  35.7 us
    reduce_scatter x1, waiting for transfers between devices, per_device(): lax.psum_scatter(numers, 'col', scatter_dimension=0, tiled=True)  32.7 us
    pmax x2, blocking collectives, per_device(): col_peaks = lax.pmax(col_peaks, 'row')  25 us
  transfers between devices with their start and end apart: 3, of which 3 were waited for; matrix products, arithmetic and copies ran while one was open for 1% of the time, Pallas kernels for 0%

commit v1 on v0

v1 whole, which is shorter than its diff:
```python
import math

import jax
import jax.numpy as jnp
from jax import lax
from jax.sharding import PartitionSpec as P

EPS = 0.05
BOTH = ("row", "col")


def swap_col(value, masks):
    pairs = [
        (row * 16 + col, row * 16 + (col ^ masks[row % 2])) for row in range(8) for col in range(16)
    ]
    return lax.ppermute(value, BOTH, pairs)


def swap_z(value, masks):
    pairs = [
        (row * 16 + col, (row ^ (2 * masks[row % 2])) * 16 + col)
        for row in range(8)
        for col in range(16)
    ]
    return lax.ppermute(value, BOTH, pairs)


def swap_core(value):
    return lax.ppermute(value, "row", [(row, row ^ 1) for row in range(8)])


XA, XB, YA, YB = (1, 3), (3, 1), (4, 12), (12, 4)
ZA, ZB = (1, 3), (3, 1)
HIGH = lax.Precision.HIGH


def join(parts, axis=0):
    return jnp.concatenate(parts, axis=axis)


def gather_noise(part, steps):
    for masks in steps:
        part = join([part, swap_col(part, masks)])
    return part


def turn(rows):
    width = rows.shape[1:]
    return rows.reshape((4, 4, 32) + width).swapaxes(0, 1).reshape((512,) + width)


def row_exchange(value, combine):
    keep = value.shape[0]
    for bit, masks in enumerate((XA, XB, YA, YB)):
        other = swap_col(value, masks)
        other = other.reshape(keep, 2 ** (3 - bit), 2, 2**bit * 32)
        other = other[:, :, ::-1].reshape(keep, 512)
        value = combine(value, other)
    return value


def col_exchange(value, combine):
    orders = ([1, 0, 3, 2, 6, 7, 4, 5], [2, 3, 0, 1, 5, 4, 7, 6], [4, 5, 6, 7, 0, 1, 2, 3])
    swaps = (lambda v: swap_z(v, ZA), lambda v: swap_z(v, ZB), swap_core)
    for order, swap in zip(orders, swaps):
        other = swap(value)
        other = join([other[:, i : i + 1] for i in order], axis=1)
        value = combine(value, other)
    return value


def join_lse(one, two):
    peak = jnp.maximum(one[0], two[0])
    total = one[1] * jnp.exp(one[0] - peak) + two[1] * jnp.exp(two[0] - peak)
    return jnp.stack([peak, total])


def add(one, two):
    return one + two


def scatter_sum(half, steps):
    for masks in steps:
        rows = half.shape[0] // 2
        half = half[:rows] + swap_col(half[rows:], masks)
    return half


def per_device(noise, data, times):
    features = noise.shape[1]
    middle = features // 2
    noise_count, data_count = 4096, 16384
    scale = 1.0 / (features * EPS)

    own = [data, swap_z(data, ZA), swap_z(data, ZB)]
    own.append(swap_z(own[1], ZB))
    cols = [join([piece, swap_core(piece)]) for piece in own]

    first = gather_noise(noise[:, :middle], (XA, XB, YA, YB))
    second = turn(gather_noise(noise[:, middle:], (YA, YB, XA, XB)))
    rows = join([first, second], axis=1)
    row_sq = jnp.sum(rows * rows, axis=1)

    blocks = []
    for piece in cols:
        col_sq = jnp.sum(piece * piece, axis=1)
        cross = lax.dot_general(rows, piece, (((1,), (1,)), ((), ())), precision=HIGH)
        blocks.append((2.0 * cross - row_sq[:, None] - col_sq[None, :]) * scale)
    score = join([block[:, :128] for block in blocks] + [block[:, 128:] for block in blocks], 1)
    order_cols = join([piece[:128] for piece in cols] + [piece[128:] for piece in cols])

    peak = jnp.max(score, axis=1)
    total = jnp.sum(jnp.exp(score - peak[:, None]), axis=1)
    peak, total = row_exchange(jnp.stack([peak, total]), join_lse)
    row_pot = math.log(data_count) - (peak + jnp.log(total))

    shifted = score + row_pot[:, None]
    low = jnp.max(shifted, axis=0)
    plan = jnp.exp(shifted - low[None, :])
    total = jnp.sum(plan, axis=0)
    top, total = col_exchange(jnp.stack([low, total]).reshape(2, 8, 128), join_lse)
    gain = noise_count * jnp.exp(low - top.reshape(-1)) / total.reshape(-1)

    totals = jnp.sum(plan * gain[None, :], axis=1)
    totals = row_exchange(totals[None], add)[0]
    scale_rows = data_count / totals
    totals = jnp.sum(plan * scale_rows[:, None], axis=0) * gain
    totals = col_exchange(totals.reshape(1, 8, 128), add).reshape(-1)
    gain = gain * (noise_count / totals)

    weights = plan * gain[None, :]
    denom = scatter_sum(jnp.sum(weights, axis=1)[:, None], (YB, YA, XB, XA))
    left = scatter_sum(
        jnp.dot(weights, order_cols[:, :middle], precision=HIGH), (YB, YA, XB, XA)
    )
    right = scatter_sum(
        jnp.dot(turn(weights), order_cols[:, middle:], precision=HIGH), (XB, XA, YB, YA)
    )
    targets = join([left, right], axis=1) / denom
    path = (1.0 - times)[:, None] * noise + times[:, None] * targets
    velocity = targets - noise
    return path, velocity


def solution(mesh):
    in_specs = (P(("row", "col"), None), P(("col", "row"), None), P(("row", "col")))
    out_specs = (P(("row", "col"), None), P(("row", "col"), None))
    return jax.shard_map(
        per_device, mesh=mesh, in_specs=in_specs, out_specs=out_specs, check_vma=False
    )
```

time: 475 us -> 194 us (0.41)
  blocking collectives: 272 us -> 0 us
  starting transfers between devices: 0.11 us -> 31.2 us
  waiting for transfers between devices: 138 us -> 112 us
  matrix products: 34.4 us -> 18.9 us
  local copies, waits for them, and re-layouts: 2.9 us -> 16.9 us
  between operations: 14.5 us -> 1.47 us
    pmax x5 -> x0, blocking collectives: 140 us -> none  [the longest x2 77.8 us: per_device(): row_peaks = lax.pmax(row_peaks, 'col')]
    ppermute x0 -> x41, waiting for transfers between devices: none -> 112 us  [the longest x28 79.9 us: swap_col(): return lax.ppermute(value, BOTH, pairs)]
    all_gather x2 -> x0, waiting for transfers between devices: 104 us -> none  [the longest x1 55.3 us: per_device(): rows_all = lax.all_gather(noise, 'col', axis=0, tiled=True)]
    psum x4 -> x0, blocking collectives: 95.8 us -> none  [the longest x2 70.9 us: per_device(): row_totals = lax.psum(row_totals, 'col')]
    unnamed x1 -> x0, blocking collectives: 35.7 us -> none
    reduce_scatter x1 -> x0, waiting for transfers between devices: 32.7 us -> none  [per_device(): lax.psum_scatter(numers, 'col', scatter_dimension=0, tiled=True)]
    ppermute x0 -> x41, starting transfers between devices: none -> 31.2 us  [the longest x28 23.5 us: swap_col(): return lax.ppermute(value, BOTH, pairs)]
    dot_general x2 -> x6, matrix products: 34.4 us -> 18.9 us  [the longest x4 7.44 us: per_device(): lax.dot_general(rows, piece, (((1,), (1,)), ((), ())), precision=HIGH)]
  transfers between devices with their start and end apart: 3 -> 41, of which waited for: 3 -> 28; matrix products, arithmetic and copies ran while one was open for 1% -> 12% of each run, Pallas kernels for 0% -> 0%
where the time goes in v1:
time: 194 us
  waiting for transfers between devices  112 us (58%)
  starting transfers between devices  31.2 us (16%)
  matrix products  18.9 us (10%)
  local copies, waits for them, and re-layouts  16.9 us (9%)
  other arithmetic  12.8 us (7%)
    ppermute x28, waiting for transfers between devices, swap_col(): return lax.ppermute(value, BOTH, pairs)  79.9 us
    ppermute x7, waiting for transfers between devices, swap_z(): return lax.ppermute(value, BOTH, pairs)  31.4 us
    ppermute x28, starting transfers between devices, swap_col(): return lax.ppermute(value, BOTH, pairs)  23.5 us
    unnamed x37, local copies, waits for them, and re-layouts  10.4 us
    dot_general x4, matrix products, per_device(): lax.dot_general(rows, piece, (((1,), (1,)), ((), ())), precision=HIGH)  7.44 us
    ppermute x7, starting transfers between devices, swap_z(): return lax.ppermute(value, BOTH, pairs)  7.14 us
    dot_general x1, matrix products, per_device(): jnp.dot(weights, order_cols[:, :middle], precision=HIGH)  5.74 us
    dot_general x1, matrix products, per_device(): jnp.dot(turn(weights), order_cols[:, middle:], precision=HIGH)  5.73 us
  transfers between devices with their start and end apart: 41, of which 28 were waited for; matrix products, arithmetic and copies ran while one was open for 12% of the time, Pallas kernels for 0%

profile of v1, /device:TPU:0, one launch (start us, length us, event | category | flops | bytes accessed | tf_op | source)
XLA Modules:
  0.0 193.6 jit_solution(9019573962641252885)
XLA Ops:
  6.8 3.2 %collective-permute-start.5 = (f32[64,1024]{1,0:T(8,128)S(1)}, f32[64,1024]{1,0:T(8,128)S(1)}, u32[]{:S(2)}, u32[]{:S(2)}) collective-permute-start(f32[64,1024]{1,0:T(8,128)S(1)} %pad_maximum_fusion.10), channel_id=1, source_target_pairs={{0,12},{1,13},{2,14},{3,15},{4,8},{5,9},{6,10},{7,11},{8,4},{9,5},... | collective-permute-start | bytes 786440 | tf_op jit(solution)/shard_map/ppermute | solution.py:16
  10.0 2.8 %collective-permute-start.1 = (f32[64,1024]{1,0:T(8,128)S(1)}, f32[64,1024]{1,0:T(8,128)S(1)}, u32[]{:S(2)}, u32[]{:S(2)}) collective-permute-start(f32[64,1024]{1,0:T(8,128)S(1)} %pad_maximum_fusion.9), channel_id=1, source_target_pairs={{0,3},{1,2},{2,1},{3,0},{4,7},{5,6},{6,5},{7,4},{8,11},{9,10},{10,... | collective-permute-start | bytes 786440 | tf_op jit(solution)/shard_map/ppermute | solution.py:16
  18.3 8.4 %collective-permute-done.6 = f32[128,1024]{1,0:T(8,128)S(1)} collective-permute-done((f32[128,1024]{1,0:T(8,128)S(1)}, f32[128,1024]{1,0:T(8,128)S(1)}, u32[]{:S(2)}, u32[]{:S(2)}) %collective-permute-start.6) | collective-permute-done | bytes 524320 | tf_op jit(solution)/shard_map/ppermute | solution.py:16
  30.1 9.0 %collective-permute-done.9 = f32[128,2048]{1,0:T(8,128)S(1)} collective-permute-done((f32[128,2048]{1,0:T(8,128)}, f32[128,2048]{1,0:T(8,128)S(1)}, u32[]{:S(2)}, u32[]{:S(2)}) %collective-permute-start.9) | collective-permute-done | bytes 1048608 | tf_op jit(solution)/shard_map/ppermute | solution.py:25
  43.9 11.2 %collective-permute-done.13 = f32[128,2048]{1,0:T(8,128)S(1)} collective-permute-done((f32[128,2048]{1,0:T(8,128)S(1)}, f32[128,2048]{1,0:T(8,128)S(1)}, u32[]{:S(2)}, u32[]{:S(2)}) %collective-permute-start.13) | collective-permute-done | bytes 1048608 | tf_op jit(solution)/shard_map/ppermute | solution.py:25
  69.4 3.6 %collective-permute-done.15 = f32[2,512]{1,0:T(2,128)S(1)} collective-permute-done((f32[2,512]{1,0:T(2,128)S(1)}, f32[2,512]{1,0:T(2,128)S(1)}, u32[]{:S(2)}, u32[]{:S(2)}) %collective-permute-start.15) | collective-permute-done | bytes 4128 | tf_op jit(solution)/shard_map/ppermute | solution.py:16
  73.6 4.8 %collective-permute-done.16 = f32[2,512]{1,0:T(2,128)S(1)} collective-permute-done((f32[2,512]{1,0:T(2,128)S(1)}, f32[2,512]{1,0:T(2,128)S(1)}, u32[]{:S(2)}, u32[]{:S(2)}) %collective-permute-start.16) | collective-permute-done | bytes 4128 | tf_op jit(solution)/shard_map/ppermute | solution.py:16
  79.1 3.5 %collective-permute-done.17 = f32[2,512]{1,0:T(2,128)S(1)} collective-permute-done((f32[2,512]{1,0:T(2,128)S(1)}, f32[2,512]{1,0:T(2,128)S(1)}, u32[]{:S(2)}, u32[]{:S(2)}) %collective-permute-start.17) | collective-permute-done | bytes 4128 | tf_op jit(solution)/shard_map/ppermute | solution.py:16
  83.2 4.3 %collective-permute-done.18 = f32[2,512]{1,0:T(2,128)S(1)} collective-permute-done((f32[2,512]{1,0:T(2,128)S(1)}, f32[2,512]{1,0:T(2,128)S(1)}, u32[]{:S(2)}, u32[]{:S(2)}) %collective-permute-start.18) | collective-permute-done | bytes 4128 | tf_op jit(solution)/shard_map/ppermute | solution.py:16
  89.3 2.9 %collective-permute-done.19 = f32[2,8,128]{2,1,0:T(8,128)S(1)} collective-permute-done((f32[2,8,128]{2,1,0:T(8,128)S(1)}, f32[2,8,128]{2,1,0:T(8,128)S(1)}, u32[]{:S(2)}, u32[]{:S(2)}) %collective-permute-start.19) | collective-permute-done | bytes 8224 | tf_op jit(solution)/shard_map/ppermute | solution.py:25
  100.6 2.8 %collective-permute-done.22 = f32[1,512]{1,0:T(1,128)S(1)} collective-permute-done((f32[1,512]{1,0:T(1,128)S(1)}, f32[1,512]{1,0:T(1,128)S(1)}, u32[]{:S(2)}, u32[]{:S(2)}) %collective-permute-start.22) | collective-permute-done | bytes 2080 | tf_op jit(solution)/shard_map/ppermute | solution.py:16
  105.6 4.0 %collective-permute-done.23 = f32[1,512]{1,0:T(1,128)S(1)} collective-permute-done((f32[1,512]{1,0:T(1,128)S(1)}, f32[1,512]{1,0:T(1,128)S(1)}, u32[]{:S(2)}, u32[]{:S(2)}) %collective-permute-start.23) | collective-permute-done | bytes 2080 | tf_op jit(solution)/shard_map/ppermute | solution.py:16
  115.6 3.7 %collective-permute-done.25 = f32[1,512]{1,0:T(1,128)S(1)} collective-permute-done((f32[1,512]{1,0:T(1,128)S(1)}, f32[1,512]{1,0:T(1,128)S(1)}, u32[]{:S(2)}, u32[]{:S(2)}) %collective-permute-start.25) | collective-permute-done | bytes 2080 | tf_op jit(solution)/shard_map/ppermute | solution.py:16
  121.5 2.8 %collective-permute-done.26 = f32[1,8,128]{2,1,0:T(8,128)S(1)} collective-permute-done((f32[1,8,128]{2,1,0:T(8,128)S(1)}, f32[1,8,128]{2,1,0:T(8,128)S(1)}, u32[]{:S(2)}, u32[]{:S(2)}) %collective-permute-start.26) | collective-permute-done | bytes 4128 | tf_op jit(solution)/shard_map/ppermute | solution.py:25
  126.4 2.9 %collective-permute-done.27 = f32[1,8,128]{2,1,0:T(8,128)S(1)} collective-permute-done((f32[1,8,128]{2,1,0:T(8,128)S(1)}, f32[1,8,128]{2,1,0:T(8,128)S(1)}, u32[]{:S(2)}, u32[]{:S(2)}) %collective-permute-start.27) | collective-permute-done | bytes 4128 | tf_op jit(solution)/shard_map/ppermute | solution.py:25
  132.6 5.7 %fusion = f32[512,1024]{1,0:T(8,128)S(1)} fusion(f32[512,1024]{1,0:T(8,128)S(1)} %bitcast.149, f32[1024,2048]{1,0:T(8,128)} %copy-done), kind=kOutput, calls=%fused_computation | convolution fusion | flops 3221225472 | bytes 8388608 | tf_op jit(solution)/shard_map/dot_general | solution.py:137
  138.5 5.7 %fusion.2 = f32[512,1024]{1,0:T(8,128)S(1)} fusion(f32[1024,2048]{1,0:T(8,128)} %copy-done, f32[1024]{0:T(1024)S(1)} %fusion.32, f32[512,1024]{1,0:T(8,128)S(1)} %get-tuple-element.55, f32[1024]{0:T(1024)S(1)} %add_reduce_fusion, f32[512]{0:T(512)S(1)} %add_subtract_fusion.1), kind=kOutput, calls=%fused_computation.2 | convolution fusion | flops 3222798336 | bytes 8398848 | tf_op jit(solution)/shard_map/dot_general | solution.py:134
  145.4 3.0 %collective-permute-start.37 = (f32[256,1]{0,1:T(1,128)S(1)}, f32[256,1]{0,1:T(1,128)S(1)}, u32[]{:S(2)}, u32[]{:S(2)}) collective-permute-start(f32[256,1]{0,1:T(1,128)S(1)} %bitcast.185), channel_id=1, source_target_pairs={{0,12},{1,13},{2,14},{3,15},{4,8},{5,9},{6,10},{7,11},{8,4},{9,5},... | collective-permute-start | bytes 3080 | tf_op jit(solution)/shard_map/ppermute | solution.py:16
  148.3 12.1 %collective-permute-done.37 = f32[256,1]{0,1:T(1,128)S(1)} collective-permute-done((f32[256,1]{0,1:T(1,128)S(1)}, f32[256,1]{0,1:T(1,128)S(1)}, u32[]{:S(2)}, u32[]{:S(2)}) %collective-permute-start.37) | collective-permute-done | bytes 1056 | tf_op jit(solution)/shard_map/ppermute | solution.py:16
  160.5 3.5 %collective-permute-done.38 = f32[128,1]{0,1:T(1,128)S(1)} collective-permute-done((f32[128,1]{0,1:T(1,128)S(1)}, f32[128,1]{0,1:T(1,128)S(1)}, u32[]{:S(2)}, u32[]{:S(2)}) %collective-permute-start.38) | collective-permute-done | bytes 544 | tf_op jit(solution)/shard_map/ppermute | solution.py:16
  164.1 3.2 %collective-permute-start.39 = (f32[64,1]{0,1:T(1,128)S(1)}, f32[64,1]{0,1:T(1,128)S(1)}, u32[]{:S(2)}, u32[]{:S(2)}) collective-permute-start(f32[64,1]{0,1:T(1,128)S(1)} %slice.433), channel_id=1, source_target_pairs={{0,3},{1,2},{2,1},{3,0},{4,7},{5,6},{6,5},{7,4},{8,11},{9,10},{10,... | collective-permute-start | bytes 776 | tf_op jit(solution)/shard_map/ppermute | solution.py:16
  170.1 7.4 %collective-permute-done.34 = f32[128,1024]{1,0:T(8,128)S(1)} collective-permute-done((f32[128,1024]{1,0:T(8,128)S(1)}, f32[128,1024]{1,0:T(8,128)S(1)}, u32[]{:S(2)}, u32[]{:S(2)}) %collective-permute-start.34) | collective-permute-done | bytes 524320 | tf_op jit(solution)/shard_map/ppermute | solution.py:16
  178.6 8.0 %collective-permute-done.35 = f32[64,1024]{1,0:T(8,128)S(1)} collective-permute-done((f32[64,1024]{1,0:T(8,128)S(1)}, f32[64,1024]{1,0:T(8,128)S(1)}, u32[]{:S(2)}, u32[]{:S(2)}) %collective-permute-start.35) | collective-permute-done | bytes 262176 | tf_op jit(solution)/shard_map/ppermute | solution.py:16
  188.6 3.1 %collective-permute-done.36 = f32[32,1024]{1,0:T(8,128)S(1)} collective-permute-done((f32[32,1024]{1,0:T(8,128)S(1)}, f32[32,1024]{1,0:T(8,128)S(1)}, u32[]{:S(2)}, u32[]{:S(2)}) %collective-permute-start.36) | collective-permute-done | bytes 131104 | tf_op jit(solution)/shard_map/ppermute | solution.py:16
  (243 shorter events, 70.5 us)
Async XLA Ops:
  1.7 5.0 %collective-permute-start.4 = (f32[32,1024]{1,0:T(8,128)S(1)}, f32[32,1024]{1,0:T(8,128)S(1)}, u32[]{:S(2)}, u32[]{:S(2)}) collective-permute-start(f32[32,1024]{1,0:T(8,128)S(1)} %get-tuple-element.59), channel_id=1, source_target_pairs={{0,4},{1,5},{2,6},{3,7},{4,0},{5,1},{6,2},{7,3},{8,12},{9,13},{10,... | collective-permute-start | bytes 393224 | tf_op jit(solution)/shard_map/ppermute | solution.py:16
  3.5 6.5 %collective-permute-start = (f32[32,1024]{1,0:T(8,128)S(1)}, f32[32,1024]{1,0:T(8,128)S(1)}, u32[]{:S(2)}, u32[]{:S(2)}) collective-permute-start(f32[32,1024]{1,0:T(8,128)S(1)} %get-tuple-element.56), channel_id=1, source_target_pairs={{0,1},{1,0},{2,3},{3,2},{4,5},{5,4},{6,7},{7,6},{8,9},{9,8},{10,11... | collective-permute-start | bytes 393224 | tf_op jit(solution)/shard_map/ppermute | solution.py:16
  6.8 10.5 %collective-permute-start.5 = (f32[64,1024]{1,0:T(8,128)S(1)}, f32[64,1024]{1,0:T(8,128)S(1)}, u32[]{:S(2)}, u32[]{:S(2)}) collective-permute-start(f32[64,1024]{1,0:T(8,128)S(1)} %pad_maximum_fusion.10), channel_id=1, source_target_pairs={{0,12},{1,13},{2,14},{3,15},{4,8},{5,9},{6,10},{7,11},{8,4},{9,5},... | collective-permute-start | bytes 786440 | tf_op jit(solution)/shard_map/ppermute | solution.py:16
  10.0 7.7 %collective-permute-start.1 = (f32[64,1024]{1,0:T(8,128)S(1)}, f32[64,1024]{1,0:T(8,128)S(1)}, u32[]{:S(2)}, u32[]{:S(2)}) collective-permute-start(f32[64,1024]{1,0:T(8,128)S(1)} %pad_maximum_fusion.9), channel_id=1, source_target_pairs={{0,3},{1,2},{2,1},{3,0},{4,7},{5,6},{6,5},{7,4},{8,11},{9,10},{10,... | collective-permute-start | bytes 786440 | tf_op jit(solution)/shard_map/ppermute | solution.py:16
  12.9 26.2 %collective-permute-start.9 = (f32[128,2048]{1,0:T(8,128)}, f32[128,2048]{1,0:T(8,128)S(1)}, u32[]{:S(2)}, u32[]{:S(2)}) collective-permute-start(f32[128,2048]{1,0:T(8,128)} %param.4), channel_id=1, source_target_pairs={{0,32},{1,33},{2,34},{3,35},{4,36},{5,37},{6,38},{7,39},{8,40},{9,... | collective-permute-start | bytes 3145736 | tf_op jit(solution)/shard_map/ppermute | solution.py:25
  14.8 25.1 %collective-permute-start.11 = (f32[128,2048]{1,0:T(8,128)}, f32[128,2048]{1,0:T(8,128)S(1)}, u32[]{:S(2)}, u32[]{:S(2)}) collective-permute-start(f32[128,2048]{1,0:T(8,128)} %param.4), channel_id=1, source_target_pairs={{0,96},{1,97},{2,98},{3,99},{4,100},{5,101},{6,102},{7,103},{8,104... | collective-permute-start | bytes 3145736 | tf_op jit(solution)/shard_map/ppermute | solution.py:25
  17.3 38.0 %collective-permute-start.8 = (f32[128,2048]{1,0:T(8,128)}, f32[128,2048]{1,0:T(8,128)S(1)}, u32[]{:S(2)}, u32[]{:S(2)}) collective-permute-start(f32[128,2048]{1,0:T(8,128)} %param.4), channel_id=1, source_target_pairs={{0,16},{16,0},{32,48},{48,32},{64,80},{80,64},{96,112},{112,96},{1... | collective-permute-start | bytes 3145736 | tf_op jit(solution)/shard_map/ppermute | solution.py:29
  17.4 9.3 %collective-permute-start.6 = (f32[128,1024]{1,0:T(8,128)S(1)}, f32[128,1024]{1,0:T(8,128)S(1)}, u32[]{:S(2)}, u32[]{:S(2)}) collective-permute-start(f32[128,1024]{1,0:T(8,128)S(1)} %pad_maximum_fusion.8), channel_id=1, source_target_pairs={{0,1},{1,0},{2,3},{3,2},{4,5},{5,4},{6,7},{7,6},{8,9},{9,8},{10,11... | collective-permute-start | bytes 1572872 | tf_op jit(solution)/shard_map/ppermute | solution.py:16
  17.7 9.6 %collective-permute-start.2 = (f32[128,1024]{1,0:T(8,128)S(1)}, f32[128,1024]{1,0:T(8,128)S(1)}, u32[]{:S(2)}, u32[]{:S(2)}) collective-permute-start(f32[128,1024]{1,0:T(8,128)S(1)} %pad_maximum_fusion.7), channel_id=1, source_target_pairs={{0,4},{1,5},{2,6},{3,7},{4,0},{5,1},{6,2},{7,3},{8,12},{9,13},{10,... | collective-permute-start | bytes 1572872 | tf_op jit(solution)/shard_map/ppermute | solution.py:16
  26.7 16.1 %collective-permute-start.7 = (f32[256,1024]{1,0:T(8,128)S(1)}, f32[256,1024]{1,0:T(8,128)S(1)}, u32[]{:S(2)}, u32[]{:S(2)}) collective-permute-start(f32[256,1024]{1,0:T(8,128)S(1)} %pad_maximum_fusion.6), channel_id=1, source_target_pairs={{0,3},{1,2},{2,1},{3,0},{4,7},{5,6},{6,5},{7,4},{8,11},{9,10},{10,... | collective-permute-start | bytes 3145736 | tf_op jit(solution)/shard_map/ppermute | solution.py:16
  27.4 16.1 %collective-permute-start.3 = (f32[256,1024]{1,0:T(8,128)S(1)}, f32[256,1024]{1,0:T(8,128)S(1)}, u32[]{:S(2)}, u32[]{:S(2)}) collective-permute-start(f32[256,1024]{1,0:T(8,128)S(1)} %pad_maximum_fusion.5), channel_id=1, source_target_pairs={{0,12},{1,13},{2,14},{3,15},{4,8},{5,9},{6,10},{7,11},{8,4},{9,5},... | collective-permute-start | bytes 3145736 | tf_op jit(solution)/shard_map/ppermute | solution.py:16
  39.1 16.0 %collective-permute-start.13 = (f32[128,2048]{1,0:T(8,128)S(1)}, f32[128,2048]{1,0:T(8,128)S(1)}, u32[]{:S(2)}, u32[]{:S(2)}) collective-permute-start(f32[128,2048]{1,0:T(8,128)S(1)} %collective-permute-done.9), channel_id=1, source_target_pairs={{0,96},{1,97},{2,98},{3,99},{4,100},{5,101},{6,102},{7,103},{8,104... | collective-permute-start | bytes 3145736 | tf_op jit(solution)/shard_map/ppermute | solution.py:25
  39.9 15.7 %collective-permute-start.10 = (f32[128,2048]{1,0:T(8,128)S(1)}, f32[128,2048]{1,0:T(8,128)S(1)}, u32[]{:S(2)}, u32[]{:S(2)}) collective-permute-start(f32[128,2048]{1,0:T(8,128)S(1)} %collective-permute-done.9), channel_id=1, source_target_pairs={{0,16},{16,0},{32,48},{48,32},{64,80},{80,64},{96,112},{112,96},{1... | collective-permute-start | bytes 3145736 | tf_op jit(solution)/shard_map/ppermute | solution.py:29
  42.8 13.0 %collective-permute-start.12 = (f32[128,2048]{1,0:T(8,128)S(1)}, f32[128,2048]{1,0:T(8,128)S(1)}, u32[]{:S(2)}, u32[]{:S(2)}) collective-permute-start(f32[128,2048]{1,0:T(8,128)S(1)} %collective-permute-done.11), channel_id=1, source_target_pairs={{0,16},{16,0},{32,48},{48,32},{64,80},{80,64},{96,112},{112,96},{1... | collective-permute-start | bytes 3145736 | tf_op jit(solution)/shard_map/ppermute | solution.py:29
  138.4 28.9 %collective-permute-start.33 = (f32[256,1024]{1,0:T(8,128)S(1)}, f32[256,1024]{1,0:T(8,128)S(1)}, u32[]{:S(2)}, u32[]{:S(2)}) collective-permute-start(f32[256,1024]{1,0:T(8,128)S(1)} %slice.483), channel_id=1, source_target_pairs={{0,3},{1,2},{2,1},{3,0},{4,7},{5,6},{6,5},{7,4},{8,11},{9,10},{10,... | collective-permute-start | bytes 3145736 | tf_op jit(solution)/shard_map/ppermute | solution.py:16
  144.3 23.3 %collective-permute-start.29 = (f32[256,1024]{1,0:T(8,128)S(1)}, f32[256,1024]{1,0:T(8,128)S(1)}, u32[]{:S(2)}, u32[]{:S(2)}) collective-permute-start(f32[256,1024]{1,0:T(8,128)S(1)} %slice.474), channel_id=1, source_target_pairs={{0,12},{1,13},{2,14},{3,15},{4,8},{5,9},{6,10},{7,11},{8,4},{9,5},... | collective-permute-start | bytes 3145736 | tf_op jit(solution)/shard_map/ppermute | solution.py:16
  145.4 15.1 %collective-permute-start.37 = (f32[256,1]{0,1:T(1,128)S(1)}, f32[256,1]{0,1:T(1,128)S(1)}, u32[]{:S(2)}, u32[]{:S(2)}) collective-permute-start(f32[256,1]{0,1:T(1,128)S(1)} %bitcast.185), channel_id=1, source_target_pairs={{0,12},{1,13},{2,14},{3,15},{4,8},{5,9},{6,10},{7,11},{8,4},{9,5},... | collective-permute-start | bytes 3080 | tf_op jit(solution)/shard_map/ppermute | solution.py:16
  167.5 9.9 %collective-permute-start.34 = (f32[128,1024]{1,0:T(8,128)S(1)}, f32[128,1024]{1,0:T(8,128)S(1)}, u32[]{:S(2)}, u32[]{:S(2)}) collective-permute-start(f32[128,1024]{1,0:T(8,128)S(1)} %slice.485), channel_id=1, source_target_pairs={{0,1},{1,0},{2,3},{3,2},{4,5},{5,4},{6,7},{7,6},{8,9},{9,8},{10,11... | collective-permute-start | bytes 1572872 | tf_op jit(solution)/shard_map/ppermute | solution.py:16
  167.8 10.6 %collective-permute-start.30 = (f32[128,1024]{1,0:T(8,128)S(1)}, f32[128,1024]{1,0:T(8,128)S(1)}, u32[]{:S(2)}, u32[]{:S(2)}) collective-permute-start(f32[128,1024]{1,0:T(8,128)S(1)} %slice.476), channel_id=1, source_target_pairs={{0,4},{1,5},{2,6},{3,7},{4,0},{5,1},{6,2},{7,3},{8,12},{9,13},{10,... | collective-permute-start | bytes 1572872 | tf_op jit(solution)/shard_map/ppermute | solution.py:16
  169.0 9.6 %collective-permute-start.40 = (f32[32,1]{0,1:T(1,128)S(1)}, f32[32,1]{0,1:T(1,128)S(1)}, u32[]{:S(2)}, u32[]{:S(2)}) collective-permute-start(f32[32,1]{0,1:T(1,128)S(1)} %slice.435), channel_id=1, source_target_pairs={{0,1},{1,0},{2,3},{3,2},{4,5},{5,4},{6,7},{7,6},{8,9},{9,8},{10,11... | collective-permute-start | bytes 392 | tf_op jit(solution)/shard_map/ppermute | solution.py:16
  177.6 9.1 %collective-permute-start.35 = (f32[64,1024]{1,0:T(8,128)S(1)}, f32[64,1024]{1,0:T(8,128)S(1)}, u32[]{:S(2)}, u32[]{:S(2)}) collective-permute-start(f32[64,1024]{1,0:T(8,128)S(1)} %slice.487), channel_id=1, source_target_pairs={{0,12},{1,13},{2,14},{3,15},{4,8},{5,9},{6,10},{7,11},{8,4},{9,5},... | collective-permute-start | bytes 786440 | tf_op jit(solution)/shard_map/ppermute | solution.py:16
  178.5 9.1 %collective-permute-start.31 = (f32[64,1024]{1,0:T(8,128)S(1)}, f32[64,1024]{1,0:T(8,128)S(1)}, u32[]{:S(2)}, u32[]{:S(2)}) collective-permute-start(f32[64,1024]{1,0:T(8,128)S(1)} %slice.478), channel_id=1, source_target_pairs={{0,3},{1,2},{2,1},{3,0},{4,7},{5,6},{6,5},{7,4},{8,11},{9,10},{10,... | collective-permute-start | bytes 786440 | tf_op jit(solution)/shard_map/ppermute | solution.py:16
  186.7 5.0 %collective-permute-start.36 = (f32[32,1024]{1,0:T(8,128)S(1)}, f32[32,1024]{1,0:T(8,128)S(1)}, u32[]{:S(2)}, u32[]{:S(2)}) collective-permute-start(f32[32,1024]{1,0:T(8,128)S(1)} %slice.489), channel_id=1, source_target_pairs={{0,4},{1,5},{2,6},{3,7},{4,0},{5,1},{6,2},{7,3},{8,12},{9,13},{10,... | collective-permute-start | bytes 393224 | tf_op jit(solution)/shard_map/ppermute | solution.py:16
  187.6 5.0 %collective-permute-start.32 = (f32[32,1024]{1,0:T(8,128)S(1)}, f32[32,1024]{1,0:T(8,128)S(1)}, u32[]{:S(2)}, u32[]{:S(2)}) collective-permute-start(f32[32,1024]{1,0:T(8,128)S(1)} %slice.480), channel_id=1, source_target_pairs={{0,1},{1,0},{2,3},{3,2},{4,5},{5,4},{6,7},{7,6},{8,9},{9,8},{10,11... | collective-permute-start | bytes 393224 | tf_op jit(solution)/shard_map/ppermute | solution.py:16
  (22 other events, 105.1 us)

commit v2 on v1

v2 whole, which is shorter than its diff:
```python
import math

import jax
import jax.numpy as jnp
from jax import lax
from jax.experimental import pallas as pl
from jax.experimental.pallas import tpu as pltpu
from jax.sharding import PartitionSpec as P

EPS = 0.05
LIMIT = 14
BOTH = ("row", "col")
NOISE, DATA = 4096, 16384
ROWS, COLS = 512, 1024
BF, F32 = jnp.bfloat16, jnp.float32

XA, XB, YA, YB = (1, 3), (3, 1), (4, 12), (12, 4)
ZA, ZB = (1, 3), (3, 1)


def swap_col(value, masks):
    pairs = [
        (row * 16 + col, row * 16 + (col ^ masks[row % 2])) for row in range(8) for col in range(16)
    ]
    return lax.ppermute(value, BOTH, pairs)


def swap_z(value, masks):
    pairs = [
        (row * 16 + col, (row ^ (2 * masks[row % 2])) * 16 + col)
        for row in range(8)
        for col in range(16)
    ]
    return lax.ppermute(value, BOTH, pairs)


def swap_core(value):
    return lax.ppermute(value, "row", [(row, row ^ 1) for row in range(8)])


def row_places():
    tables = []
    for core in range(2):
        masks = [m[core] for m in (XA, XB, YA, YB)]
        table = []
        for p in range(16):
            rel = 0
            for bit in range(4):
                rel ^= masks[bit] if p >> bit & 1 else 0
            table.append(rel)
        tables.append(table)
    core = lax.axis_index("row") % 2
    table = jnp.where(core == 0, jnp.array(tables[0], jnp.int32), jnp.array(tables[1], jnp.int32))
    return table ^ lax.axis_index("col").astype(jnp.int32)


def col_places():
    tables = []
    for core in range(2):
        table = []
        for k in range(4):
            for sibling in range(2):
                of = core ^ sibling
                z = (ZA[of] if k & 1 else 0) ^ (ZB[of] if k & 2 else 0)
                table.append(z * 2 + sibling)
        tables.append(table + [0])
    row = lax.axis_index("row").astype(jnp.int32)
    table = jnp.where(row % 2 == 0, jnp.array(tables[0], jnp.int32), jnp.array(tables[1], jnp.int32))
    return table ^ row


def vmem(count):
    return [pl.BlockSpec(memory_space=pltpu.VMEM)] * count


def smem(count):
    return [pl.BlockSpec(memory_space=pltpu.SMEM)] * count


def call(body, outs, places=0, arrays=0, scratch=(), flops=0, moved=0, limit=LIMIT, far=0, far_out=0):
    out_specs = jax.tree.map(lambda _: pl.BlockSpec(memory_space=pltpu.VMEM), outs)
    if far_out:
        out_specs = out_specs[:-far_out] + (pl.BlockSpec(memory_space=pltpu.HBM),) * far_out
    return pl.pallas_call(
        body,
        out_shape=outs,
        in_specs=smem(places) + [pl.BlockSpec(memory_space=pltpu.HBM)] * far + vmem(arrays),
        out_specs=out_specs,
        scratch_shapes=list(scratch),
        compiler_params=pltpu.CompilerParams(vmem_limit_bytes=limit * 2**20),
        cost_estimate=pl.CostEstimate(flops=flops, bytes_accessed=moved, transcendentals=0),
    )


def shape(dims, dtype=F32):
    return jax.ShapeDtypeStruct(dims, dtype)


def split(value):
    high = value.astype(BF)
    return high, (value - high.astype(F32)).astype(BF)


def diagonal():
    one = lax.broadcasted_iota(jnp.int32, (128, 128), 0)
    return one == lax.broadcasted_iota(jnp.int32, (128, 128), 1)


def compact(ref):
    eye = diagonal()
    return jnp.concatenate(
        [
            jnp.sum(jnp.where(eye, ref[128 * q : 128 * q + 128, :], 0.0), axis=0, keepdims=True)
            for q in range(4)
        ],
        axis=0,
    )


def spread(value, ref):
    eye = diagonal()
    for q in range(4):
        wide = jnp.broadcast_to(value[q : q + 1, :], (128, 128))
        column = jnp.sum(jnp.where(eye, wide, 0.0), axis=1, keepdims=True)
        ref[128 * q : 128 * q + 128, :] = jnp.broadcast_to(column, (128, 128))


def block(p):
    return pl.ds(32 * p, 32)


def place(places, p):
    return pl.ds(pl.multiple_of(places[p] * 32, 32), 32)


def dot_t(one, two):
    return lax.dot_general(one, two, (((1,), (1,)), ((), ())), preferred_element_type=F32)


def group(k, pieces, high, low, norm):
    for at, ref in ((0, pieces[2 * k]), (128, pieces[2 * k + 1])):
        for p in range(4):
            rows = slice(256 * k + at + 32 * p, 256 * k + at + 32 * p + 32)
            value = ref[32 * p : 32 * p + 32, :]
            high[rows, :], low[rows, :] = split(value)
            total = jnp.sum(value * value, axis=1, keepdims=True)
            norm[at + 32 * p : at + 32 * p + 32, :] = jnp.broadcast_to(total, (32, 128))


def score(k, scale, terms, nn, high, low, norm, out, lanes):
    eye = diagonal()
    norms = jnp.concatenate(
        [
            jnp.sum(jnp.where(eye, norm[128 * q : 128 * q + 128, :], 0.0), axis=0, keepdims=True)
            for q in range(2)
        ],
        axis=1,
    )
    cols = slice(256 * k, 256 * k + 256)
    both = dot_t(terms[...], high[cols, :])
    cross = both[:ROWS] + both[ROWS:] + dot_t(terms[:ROWS, :], low[cols, :])
    out[:, lanes] = (2.0 * cross - nn[:, :1] - norms) * scale


def data_body(*refs):
    pieces, norms, (dh, dl), (high, low, outs) = refs[:6], refs[6], refs[7:9], refs[9:]
    sent = []
    for k in range(3):
        group(k, pieces, high, low, norms.at[256 * k : 256 * k + 256, :])
        rows = slice(256 * k, 256 * k + 256)
        for i, (source, target) in enumerate(((high, dh), (low, dl))):
            sent.append(
                pltpu.make_async_copy(source.at[rows, :], target.at[rows, :], outs.at[2 * k + i])
            )
            sent[-1].start()
    for copy in sent:
        copy.wait()


def row_sums(value):
    peak = jnp.max(value, axis=1, keepdims=True)
    total = jnp.sum(jnp.exp(value - peak), axis=1, keepdims=True)
    return jnp.broadcast_to(peak, (32, 128)), jnp.broadcast_to(total, (32, 128))


def early_body(scale, *refs):
    data, norms, noise = refs[0:2], refs[2], refs[3:7]
    terms, nn, scores, peaks, totals = refs[7:12]
    high, low, sems = refs[12:]
    copies = []
    for k in range(3):
        rows = slice(256 * k, 256 * k + 256)
        for i, (source, target) in enumerate(zip(data, (high, low))):
            copies.append(
                pltpu.make_async_copy(source.at[rows, :], target.at[rows, :], sems.at[2 * k + i])
            )
            copies[-1].start()
    middle = noise[0].shape[1]
    for p in range(16):
        xs, ys = p % 4, p // 4
        q = xs * 4 + ys
        one = noise[p // 8][32 * (p % 8) : 32 * (p % 8) + 32, :]
        two = noise[2 + q // 8][32 * (q % 8) : 32 * (q % 8) + 32, :]
        top, under = slice(32 * p, 32 * p + 32), slice(ROWS + 32 * p, ROWS + 32 * p + 32)
        terms[top, :middle], terms[under, :middle] = split(one)
        terms[top, middle:], terms[under, middle:] = split(two)
        total = jnp.sum(one * one + two * two, axis=1, keepdims=True)
        nn[32 * p : 32 * p + 32, :] = jnp.broadcast_to(total, (32, 128))
    for copy in copies:
        copy.wait()
    for k in range(3):
        rows = slice(256 * k, 256 * k + 256)
        score(k, scale, terms, nn, high, low, norms.at[rows, :], scores, rows)
    for p in range(16):
        peaks[block(p), :], totals[block(p), :] = row_sums(scores[block(p), :])


def late_body(scale, places, own, sibling, terms, nn, peaks, totals, scores, out, dh, dl, *scratch):
    high, low, norm, ends, sums, sems = scratch
    group(0, (own, sibling), high, low, norm)
    sent = [
        pltpu.make_async_copy(source, target, sems.at[i])
        for i, (source, target) in enumerate(((high, dh), (low, dl)))
    ]
    for copy in sent:
        copy.start()
    score(0, scale, terms, nn, high, low, norm, scores, slice(0, 256))
    for p in range(16):
        peak, total = row_sums(scores[block(p), :])
        before = peaks[block(p), :]
        top = jnp.maximum(peak, before)
        ends[place(places, p), :] = top
        sums[place(places, p), :] = total * jnp.exp(peak - top) + totals[block(p), :] * jnp.exp(
            before - top
        )
    value = jnp.concatenate([compact(ends), compact(sums)], axis=0)
    for to in range(16):
        out[to] = value
    for copy in sent:
        copy.wait()


def col_first_body(rplaces, cplaces, got, early, late, plan, out, pots, ends):
    peak = got[0, 0:4, :]
    for one in range(1, 16):
        peak = jnp.maximum(peak, got[one, 0:4, :])
    total = got[0, 4:8, :] * jnp.exp(got[0, 0:4, :] - peak)
    for one in range(1, 16):
        total = total + got[one, 4:8, :] * jnp.exp(got[one, 0:4, :] - peak)
    spread(math.log(DATA) - (peak + jnp.log(total)), pots)
    for k in range(4):
        lanes = slice(256 * k, 256 * k + 256)
        high = None
        for p in range(16):
            value = late[block(p), :] if k == 3 else early[block(p), lanes]
            value = value + pots[place(rplaces, p), :][:, :1]
            plan[block(p), lanes] = value
            value = jnp.max(value.reshape(4, 8, 256), axis=0)
            high = value if high is None else jnp.maximum(high, value)
        high = jnp.max(high, axis=0, keepdims=True)
        sums = None
        for p in range(16):
            value = jnp.exp(plan[block(p), lanes] - high)
            plan[block(p), lanes] = value
            value = jnp.sum(value.reshape(4, 8, 256), axis=0)
            sums = value if sums is None else sums + value
        sums = jnp.sum(sums, axis=0, keepdims=True)
        for half in range(2):
            at = cplaces[2 * k + half]
            ends[pl.ds(at, 1), :] = high[:, 128 * half : 128 * half + 128]
            ends[pl.ds(8 + at, 1), :] = sums[:, 128 * half : 128 * half + 128]
    for to in range(8):
        out[to] = ends[...]


def to_lanes(cplaces, ref):
    return jnp.concatenate([ref[pl.ds(cplaces[b], 1), :] for b in range(8)], axis=1)


def row_second_body(rplaces, cplaces, got, plan, out, gains, totals):
    high = got[0, 0:8, :]
    for one in range(1, 8):
        high = jnp.maximum(high, got[one, 0:8, :])
    total = got[0, 8:16, :] * jnp.exp(got[0, 0:8, :] - high)
    for one in range(1, 8):
        total = total + got[one, 8:16, :] * jnp.exp(got[one, 0:8, :] - high)
    own = got[pl.ds(cplaces[8], 1)][0, 0:8, :]
    gains[...] = NOISE * jnp.exp(own - high) / total
    lanes = to_lanes(cplaces, gains)
    for p in range(16):
        value = jnp.sum(plan[block(p), :] * lanes, axis=1, keepdims=True)
        totals[place(rplaces, p), :] = jnp.broadcast_to(value, (32, 128))
    value = compact(totals)
    value = jnp.concatenate([value, value], axis=0)
    for to in range(16):
        out[to] = value


def col_second_body(rplaces, cplaces, got, gains, plan, out, scales, ends):
    total = got[0, 0:4, :]
    for one in range(1, 16):
        total = total + got[one, 0:4, :]
    spread(DATA / total, scales)
    sums = None
    for p in range(16):
        value = plan[block(p), :] * scales[place(rplaces, p), :][:, :1]
        value = jnp.sum(value.reshape(4, 8, COLS), axis=0)
        sums = value if sums is None else sums + value
    sums = jnp.sum(sums, axis=0, keepdims=True)
    for b in range(8):
        ends[pl.ds(cplaces[b], 1), :] = sums[:, 128 * b : 128 * b + 128]
    value = ends[...] * gains[...]
    for to in range(8):
        out[to] = value


def weight_body(cplaces, got, gains, plan, high, low, denom, ends, totals):
    total = got[0]
    for one in range(1, 8):
        total = total + got[one]
    ends[...] = gains[...] * (NOISE / total)
    lanes = to_lanes(cplaces, ends)
    for p in range(16):
        value = plan[block(p), :] * lanes
        high[block(p), :], low[block(p), :] = split(value)
        totals[block(p), :] = jnp.broadcast_to(jnp.sum(value, axis=1, keepdims=True), (32, 128))
    denom[...] = totals[...]


def dot(one, two):
    return jnp.dot(one, two, preferred_element_type=F32)


def product_body(blocks, lanes, wh, wl, denom, h0, l0, h1, l1, out):
    terms = [
        jnp.concatenate([ref[block(p), at] for ref in (wh, wl) for p in blocks], axis=0)
        for at in (slice(0, 768), slice(768, 1024))
    ]
    for n in range(4):
        at = slice(lanes + 256 * n, lanes + 256 * n + 256)
        both = dot(terms[0], h0[:, at]) + dot(terms[1], h1[:, at])
        more = dot(terms[0][:256], l0[:, at]) + dot(terms[1][:256], l1[:, at])
        total = both[:256] + both[256:] + more
        for i in range(8):
            for t in range(2):
                tile = total[32 * i : 32 * i + 32, 128 * t : 128 * t + 128]
                out[i, 32 * (2 * n + t) : 32 * (2 * n + t) + 32, :] = tile
    if lanes == 0:
        eye = diagonal()[:32, :]
        for i, p in enumerate(blocks):
            row = jnp.sum(jnp.where(eye, denom[block(p), :], 0.0), axis=0, keepdims=True)
            out[i, 256:264, :] = jnp.broadcast_to(row, (8, 128))


def end_body(left, right, noise, times, path, velocity):
    eye = diagonal()[:32, :]
    wide = jnp.broadcast_to(left[0, 256:257, :], (32, 128))
    inverse = 1.0 / jnp.sum(jnp.where(eye, wide, 0.0), axis=1, keepdims=True)
    for side, ref in enumerate((left, right)):
        for t in range(8):
            lanes = slice(1024 * side + 128 * t, 1024 * side + 128 * t + 128)
            target = ref[0, 32 * t : 32 * t + 32, :] * inverse
            own = noise[:, lanes]
            at = times[:, :1]
            path[:, lanes] = (1.0 - at) * own + at * target
            velocity[:, lanes] = target - own


def after(*values):
    return lax.optimization_barrier(values)


def product(blocks, lanes, *arrays):
    def body(*refs):
        product_body(blocks, lanes, *refs)

    return call(
        body,
        shape((8, 264 if lanes == 0 else 256, 128)),
        0,
        7,
        flops=3 * 2 * 256 * 1024 * 1024,
        moved=6 * 2**20,
    )(*arrays)


X_FIRST = list(range(16))
Y_FIRST = [ys * 4 + xs for xs in range(4) for ys in range(4)]


def per_device(noise, data, times):
    features = noise.shape[1]
    middle = features // 2
    scale = 1.0 / (features * EPS)
    rplaces, cplaces = row_places(), col_places()

    near, far = swap_z(data, ZA), swap_z(data, ZB)
    parts = [noise[:, :middle], noise[:, middle:]]
    orders = ((XA, XB, YA, YB), (YA, YB, XA, XB))
    stages = []
    for step in range(3):
        parts = [
            jnp.concatenate([part, swap_col(part, order[step])], axis=0)
            for part, order in zip(parts, orders)
        ]
        stages.append(parts)
    last = [swap_col(part, order[3]) for part, order in zip(parts, orders)]
    first = data
    near = after(near, *stages[1])[0]
    own = [data, near, far, swap_z(near, ZB)]
    cross = [swap_core(first), swap_core(near), swap_core(far), swap_core(own[3])]
    pieces = [[part, one] for part, one in zip(parts, last)]

    wide = pltpu.VMEM((ROWS, 128), F32)
    norms, h0, l0 = call(
        data_body,
        (shape((768, 128)),) + (shape((768, features), BF),) * 2,
        arrays=6,
        scratch=(
            pltpu.VMEM((768, features), BF),
            pltpu.VMEM((768, features), BF),
            pltpu.SemaphoreType.DMA((6,)),
        ),
        moved=12 * 2**20,
        far_out=2,
    )(own[0], cross[0], own[1], cross[1], own[2], cross[2])
    rows, row_norms, early, peaks, totals = call(
        lambda *refs: early_body(scale, *refs),
        (shape((2 * ROWS, features), BF), shape((ROWS, 128)), shape((ROWS, 768)))
        + (shape((ROWS, 128)),) * 2,
        arrays=5,
        scratch=(
            pltpu.VMEM((768, features), BF),
            pltpu.VMEM((768, features), BF),
            pltpu.SemaphoreType.DMA((6,)),
        ),
        flops=3 * 2 * ROWS * 768 * features,
        moved=16 * 2**20,
        limit=20,
        far=2,
    )(h0, l0, norms, *pieces[0], *pieces[1])
    late, send, h1, l1 = call(
        lambda *refs: late_body(scale, *refs),
        (shape((ROWS, 256)), shape((16, 8, 128))) + (shape((256, features), BF),) * 2,
        1,
        6,
        scratch=(
            pltpu.VMEM((256, features), BF),
            pltpu.VMEM((256, features), BF),
            pltpu.VMEM((256, 128), F32),
            wide,
            wide,
            pltpu.SemaphoreType.DMA((2,)),
        ),
        flops=3 * 2 * ROWS * 256 * features,
        moved=8 * 2**20,
        far_out=2,
    )(rplaces, own[3], cross[3], rows, row_norms, peaks, totals)
    send, rplaces, cplaces = after(send, rplaces, cplaces)
    got = lax.all_to_all(send, "col", 0, 0)
    plan, send = call(
        col_first_body,
        (shape((ROWS, COLS)), shape((8, 16, 128))),
        2,
        3,
        (wide, pltpu.VMEM((16, 128), F32)),
    )(rplaces, cplaces, got, early, late)
    got = lax.all_to_all(send, "row", 0, 0)
    send, gains = call(
        row_second_body,
        (shape((16, 8, 128)), shape((8, 128))),
        2,
        2,
        (wide,),
    )(rplaces, cplaces, got, plan)
    got = lax.all_to_all(send, "col", 0, 0)
    send = call(
        col_second_body,
        shape((8, 8, 128)),
        2,
        3,
        (wide, pltpu.VMEM((8, 128), F32)),
    )(rplaces, cplaces, got, gains, plan)
    got = lax.all_to_all(send, "row", 0, 0)
    wh, wl, denom = call(
        weight_body,
        (shape((ROWS, COLS), BF), shape((ROWS, COLS), BF), shape((ROWS, 128))),
        1,
        3,
        (pltpu.VMEM((8, 128), F32), wide),
    )(cplaces, got, gains, plan)

    rest = (wh, wl, denom, h0, l0, h1, l1)
    left_out = product(X_FIRST[8:], 0, *rest)
    rest = after(left_out, *rest)
    left_out, rest = rest[0], rest[1:]
    right_out = product(Y_FIRST[8:], middle, *rest)
    rest = after(right_out, *rest)
    right_out, rest = rest[0], rest[1:]
    left_in, right_in = swap_col(left_out, YB), swap_col(right_out, XB)
    left = product(X_FIRST[:8], 0, *rest)
    rest = after(left, *rest)
    left, rest = rest[0], rest[1:]
    right = product(Y_FIRST[:8], middle, *rest)
    left, right = left + left_in, right + right_in
    for first, second in zip((YA, XB, XA), (XA, YB, YA)):
        rows = left.shape[0] // 2
        left_in, right_in = swap_col(left[rows:], first), swap_col(right[rows:], second)
        left, right = left[:rows] + left_in, right[:rows] + right_in
    wide_times = jnp.broadcast_to(times[:, None], (times.shape[0], 128))
    outs = (shape(noise.shape), shape(noise.shape))
    return call(end_body, outs, 0, 4)(left, right, noise, wide_times)


def solution(mesh):
    in_specs = (P(("row", "col"), None), P(("col", "row"), None), P(("row", "col")))
    out_specs = (P(("row", "col"), None), P(("row", "col"), None))
    return jax.shard_map(
        per_device, mesh=mesh, in_specs=in_specs, out_specs=out_specs, check_vma=False
    )
```

time: 194 us -> 155 us (0.80)
  waiting for transfers between devices: 112 us -> 50.6 us
  blocking collectives: 0 us -> 40 us
  Pallas kernels: 0 us -> 28.5 us
  matrix products: 18.9 us -> 0 us
  local copies, waits for them, and re-layouts: 16.9 us -> 4.76 us
  other arithmetic: 12.8 us -> 1.76 us
  starting transfers between devices: 31.2 us -> 27.8 us
    all_to_all x0 -> x4, blocking collectives: none -> 40 us  [the longest x2 23.4 us: per_device(): got = lax.all_to_all(send, 'col', 0, 0)]
    ppermute x28 -> x16, waiting for transfers between devices: 79.9 us -> 46 us  [swap_col(): return lax.ppermute(value, BOTH, pairs)]
    pallas_call x0 -> x12, Pallas kernels: none -> 28.5 us  [the longest x1 8.59 us: per_device(): call(lambda *refs: early_body(scale, *refs), (shape((2 * ROWS, features),...]
    ppermute x7 -> x3, waiting for transfers between devices: 31.4 us -> 4.66 us  [swap_z(): return lax.ppermute(value, BOTH, pairs)]
    dot_general x6 -> x0, matrix products: 18.9 us -> none  [the longest x4 7.44 us: per_device(): lax.dot_general(rows, piece, (((1,), (1,)), ((), ())), precision=HIGH)]
    unnamed x37 -> x20, local copies, waits for them, and re-layouts: 10.4 us -> 3.57 us
    reduce_sum x10 -> x0, other arithmetic: 3.84 us -> none  [the longest x4 0.88 us: per_device(): col_sq = jnp.sum(piece * piece, axis=1)]
    ppermute x28 -> x16, starting transfers between devices: 23.5 us -> 20.1 us  [swap_col(): return lax.ppermute(value, BOTH, pairs)]
  transfers between devices with their start and end apart: 41 -> 23, of which waited for: 28 -> 13; matrix products, arithmetic and copies ran while one was open for 12% -> 2% of each run, Pallas kernels for 0% -> 11%
where the time goes in v2:
time: 155 us
  waiting for transfers between devices  50.6 us (33%)
  blocking collectives  40 us (26%)
  Pallas kernels  28.5 us (18%)
  starting transfers between devices  27.8 us (18%)
  local copies, waits for them, and re-layouts  4.76 us (3%)
  other arithmetic  1.76 us (1%)
    ppermute x16, waiting for transfers between devices, swap_col(): return lax.ppermute(value, BOTH, pairs)  46 us
    all_to_all x2, blocking collectives, per_device(): got = lax.all_to_all(send, 'col', 0, 0)  23.4 us
    ppermute x16, starting transfers between devices, swap_col(): return lax.ppermute(value, BOTH, pairs)  20.1 us
    all_to_all x2, blocking collectives, per_device(): got = lax.all_to_all(send, 'row', 0, 0)  16.7 us
    pallas_call x1, Pallas kernels, per_device(): call(lambda *refs: early_body(scale, *refs), (shape((2 * ROWS, features),...  8.59 us
    ppermute x3, starting transfers between devices, swap_z(): return lax.ppermute(value, BOTH, pairs)  7.21 us
    pallas_call x4, Pallas kernels, product(): call(body, shape((8, 264 if lanes == 0 else 256, 128)), 0, 7, flops=3 * 2...  7.19 us
    ppermute x3, waiting for transfers between devices, swap_z(): return lax.ppermute(value, BOTH, pairs)  4.66 us
  transfers between devices with their start and end apart: 23, of which 13 were waited for; matrix products, arithmetic and copies ran while one was open for 2% of the time, Pallas kernels for 11%

profile of v2, /device:TPU:0, one launch (start us, length us, event | category | flops | bytes accessed | tf_op | source)
XLA Modules:
  0.0 154.5 jit_solution(1293605025162885721)
XLA Ops:
  0.6 2.1 %collective-permute-start = (f32[128,2048]{1,0:T(8,128)}, f32[128,2048]{1,0:T(8,128)}, u32[]{:S(2)}, u32[]{:S(2)}) collective-permute-start(f32[128,2048]{1,0:T(8,128)} %refs_0_.1), channel_id=1, source_target_pairs={{0,32},{1,33},{2,34},{3,35},{4,36},{5,37},{6,38},{7,39},{8,40},{9,... | collective-permute-start | bytes 3145736 | tf_op jit(solution)/shard_map/ppermute | solution.py:34
  6.9 1.9 %collective-permute-done.1 = f32[32,1024]{1,0:T(8,128)S(1)} collective-permute-done((f32[32,1024]{1,0:T(8,128)S(1)}, f32[32,1024]{1,0:T(8,128)S(1)}, u32[]{:S(2)}, u32[]{:S(2)}) %collective-permute-start.1) | collective-permute-done | bytes 131104 | tf_op jit(solution)/shard_map/ppermute | solution.py:25
  8.8 2.8 %collective-permute-start.2 = (f32[64,1024]{1,0:T(8,128)S(1)}, f32[64,1024]{1,0:T(8,128)S(1)}, u32[]{:S(2)}, u32[]{:S(2)}) collective-permute-start(f32[64,1024]{1,0:T(8,128)S(1)} %pad_maximum_fusion.4), channel_id=1, source_target_pairs={{0,3},{1,2},{2,1},{3,0},{4,7},{5,6},{6,5},{7,4},{8,11},{9,10},{10,... | collective-permute-start | bytes 786440 | tf_op jit(solution)/shard_map/ppermute | solution.py:25
  11.6 2.5 %collective-permute-start.9 = (f32[128,2048]{1,0:T(8,128)}, f32[128,2048]{1,0:T(8,128)}, u32[]{:S(2)}, u32[]{:S(2)}) collective-permute-start(f32[128,2048]{1,0:T(8,128)} %refs_0_.1), channel_id=1, source_target_pairs={{0,96},{1,97},{2,98},{3,99},{4,100},{5,101},{6,102},{7,103},{8,104... | collective-permute-start | bytes 3145736 | tf_op jit(solution)/shard_map/ppermute | solution.py:34
  14.2 3.1 %collective-permute-start.4 = (f32[64,1024]{1,0:T(8,128)S(1)}, f32[64,1024]{1,0:T(8,128)S(1)}, u32[]{:S(2)}, u32[]{:S(2)}) collective-permute-start(f32[64,1024]{1,0:T(8,128)S(1)} %pad_maximum_fusion.5), channel_id=1, source_target_pairs={{0,12},{1,13},{2,14},{3,15},{4,8},{5,9},{6,10},{7,11},{8,4},{9,5},... | collective-permute-start | bytes 786440 | tf_op jit(solution)/shard_map/ppermute | solution.py:25
  18.1 4.7 %collective-permute-done.4 = f32[64,1024]{1,0:T(8,128)S(1)} collective-permute-done((f32[64,1024]{1,0:T(8,128)S(1)}, f32[64,1024]{1,0:T(8,128)S(1)}, u32[]{:S(2)}, u32[]{:S(2)}) %collective-permute-start.4) | collective-permute-done | bytes 262176 | tf_op jit(solution)/shard_map/ppermute | solution.py:25
  23.0 2.6 %collective-permute-start.5 = (f32[128,2048]{1,0:T(8,128)}, f32[128,2048]{1,0:T(8,128)S(1)}, u32[]{:S(2)}, u32[]{:S(2)}) collective-permute-start(f32[128,2048]{1,0:T(8,128)} %collective-permute-done.refs_2_), channel_id=1, source_target_pairs={{0,96},{1,97},{2,98},{3,99},{4,100},{5,101},{6,102},{7,103},{8,104... | collective-permute-start | bytes 3145736 | tf_op jit(solution)/shard_map/ppermute | solution.py:34
  26.7 2.3 %collective-permute-start.12 = (f32[256,1024]{1,0:T(8,128)S(1)}, f32[256,1024]{1,0:T(8,128)}, u32[]{:S(2)}, u32[]{:S(2)}) collective-permute-start(f32[256,1024]{1,0:T(8,128)S(1)} %pad_maximum_fusion.refs_3_), channel_id=1, source_target_pairs={{0,12},{1,13},{2,14},{3,15},{4,8},{5,9},{6,10},{7,11},{8,4},{9,5},... | collective-permute-start | bytes 3145736 | tf_op jit(solution)/shard_map/ppermute | solution.py:25
  29.0 3.1 %collective-permute-done.13 = f32[128,1024]{1,0:T(8,128)S(1)} collective-permute-done((f32[128,1024]{1,0:T(8,128)S(1)}, f32[128,1024]{1,0:T(8,128)S(1)}, u32[]{:S(2)}, u32[]{:S(2)}) %collective-permute-start.13) | collective-permute-done | bytes 524320 | tf_op jit(solution)/shard_map/ppermute | solution.py:25
  34.8 4.7 %collective-permute-done.5.refs_1_ = f32[128,2048]{1,0:T(8,128)S(1)} collective-permute-done((f32[128,2048]{1,0:T(8,128)}, f32[128,2048]{1,0:T(8,128)S(1)}, u32[]{:S(2)}, u32[]{:S(2)}) %collective-permute-start.5) | collective-permute-done | bytes 1048608 | tf_op jit(solution)/shard_map/ppermute | solution.py:34
  42.0 4.3 %shard_map.86 = (f32[768,128]{1,0:T(8,128)S(1)}, bf16[768,2048]{1,0:T(8,128)(2,1)S(1)}, bf16[768,2048]{1,0:T(8,128)(2,1)S(1)}) custom-call(f32[128,2048]{1,0:T(8,128)S(1)} %copy-done.2, f32[128,2048]{1,0:T(8,128)S(1)} %copy-done.4, f32[128,2048]{1,0:T(8,128)} %collective-permute-done.refs_2_, f32[128,2048]{1,0:T(8,128)} %collective-permute-done.8.refs_3_, ...), custom_call_target="tpu_custom_call" | custom-call | bytes 12582912 | tf_op jit(solution)/shard_map/pallas_call | solution.py:415
  46.3 4.8 %collective-permute-done.14.refs_6_ = f32[256,1024]{1,0:T(8,128)} collective-permute-done((f32[256,1024]{1,0:T(8,128)}, f32[256,1024]{1,0:T(8,128)}, u32[]{:S(2)}, u32[]{:S(2)}) %collective-permute-start.14) | collective-permute-done | bytes 1048608 | tf_op jit(solution)/shard_map/ppermute | solution.py:25
  51.1 8.6 %shard_map.87 = (bf16[1024,2048]{1,0:T(8,128)(2,1)S(1)}, f32[512,128]{1,0:T(8,128)S(1)}, f32[512,768]{1,0:T(8,128)S(1)}, f32[512,128]{1,0:T(8,128)S(1)}, f32[512,128]{1,0:T(8,128)S(1)}) custom-call(bf16[768,2048]{1,0:T(8,128)(2,1)S(1)} %get-tuple-element.91.refs_0_.refs_3_, bf16[768,2048]{1,0:T(8,128)(2,1)S(1)} %get-tuple-element.92.refs_1_.refs_4_, ...), custom_call_target="tpu_custom_call" | custom-call | flops 4831838208 | bytes 16777216 | tf_op jit(solution)/shard_map/pallas_call | solution.py:427
  59.7 3.3 %shard_map.88 = (f32[512,256]{1,0:T(8,128)S(1)}, f32[16,8,128]{2,1,0:T(8,128)S(1)}, bf16[256,2048]{1,0:T(8,128)(2,1)S(1)}, bf16[256,2048]{1,0:T(8,128)(2,1)S(1)}) custom-call(s32[16]{0:T(128)S(1)} %fusion.refs_0_.rplaces, f32[128,2048]{1,0:T(8,128)S(1)} %collective-permute-done.5.refs_1_, f32[128,2048]{1,0:T(8,128)S(1)} %collective-permute-done.6.refs_2_, ...), custom_call_target="tpu_custom_call" | custom-call | flops 1610612736 | bytes 8388608 | tf_op jit(solution)/shard_map/pallas_call | solution.py:442
  63.0 12.6 %all_to_all.20.got = f32[16,8,128]{2,1,0:T(8,128)S(1)} all-to-all(f32[16,8,128]{2,1,0:T(8,128)S(1)} %get-tuple-element.60), channel_id=1, replica_groups=mesh['row'=8,'col'=16] {'col'}, dimensions={0} | all-to-all | bytes 131072 | tf_op jit(solution)/shard_map/all_to_all | solution.py:460
  76.9 8.9 %all_to_all.21.got = f32[8,16,128]{2,1,0:T(8,128)S(1)} all-to-all(f32[8,16,128]{2,1,0:T(8,128)S(1)} %get-tuple-element.63), channel_id=1, replica_groups=mesh['row'=8,'col'=16] {'row'}, dimensions={0} | all-to-all | bytes 131072 | tf_op jit(solution)/shard_map/all_to_all | solution.py:468
  86.6 10.8 %all_to_all.22.got = f32[16,8,128]{2,1,0:T(8,128)S(1)} all-to-all(f32[16,8,128]{2,1,0:T(8,128)S(1)} %get-tuple-element.65), channel_id=1, replica_groups=mesh['row'=8,'col'=16] {'col'}, dimensions={0} | all-to-all | bytes 131072 | tf_op jit(solution)/shard_map/all_to_all | solution.py:476
  98.4 7.8 %all_to_all.23.got = f32[8,8,128]{2,1,0:T(8,128)S(1)} all-to-all(f32[8,8,128]{2,1,0:T(8,128)S(1)} %shard_map.91), channel_id=1, replica_groups=mesh['row'=8,'col'=16] {'row'}, dimensions={0} | all-to-all | bytes 65536 | tf_op jit(solution)/shard_map/all_to_all | solution.py:484
  116.9 10.1 %collective-permute-done.19 = f32[8,256,128]{2,1,0:T(8,128)S(1)} collective-permute-done((f32[8,256,128]{2,1,0:T(8,128)S(1)}, f32[8,256,128]{2,1,0:T(8,128)S(1)}, u32[]{:S(2)}, u32[]{:S(2)}) %collective-permute-start.19) | collective-permute-done | bytes 1048608 | tf_op jit(solution)/shard_map/ppermute | solution.py:25
  128.7 7.7 %collective-permute-done.20 = f32[4,256,128]{2,1,0:T(8,128)S(1)} collective-permute-done((f32[4,256,128]{2,1,0:T(8,128)S(1)}, f32[4,256,128]{2,1,0:T(8,128)S(1)}, u32[]{:S(2)}, u32[]{:S(2)}) %collective-permute-start.20) | collective-permute-done | bytes 524320 | tf_op jit(solution)/shard_map/ppermute | solution.py:25
  139.3 3.0 %collective-permute-start.17 = (f32[2,264,128]{2,1,0:T(8,128)S(1)}, f32[2,264,128]{2,1,0:T(8,128)S(1)}, u32[]{:S(2)}, u32[]{:S(2)}) collective-permute-start(f32[2,264,128]{2,1,0:T(8,128)S(1)} %slice.59), channel_id=1, source_target_pairs={{0,3},{1,2},{2,1},{3,0},{4,7},{5,6},{6,5},{7,4},{8,11},{9,10},{10,... | collective-permute-start | bytes 811016 | tf_op jit(solution)/shard_map/ppermute | solution.py:25
  142.3 1.8 %collective-permute-done.21 = f32[2,256,128]{2,1,0:T(8,128)S(1)} collective-permute-done((f32[2,256,128]{2,1,0:T(8,128)S(1)}, f32[2,256,128]{2,1,0:T(8,128)S(1)}, u32[]{:S(2)}, u32[]{:S(2)}) %collective-permute-start.21) | collective-permute-done | bytes 262176 | tf_op jit(solution)/shard_map/ppermute | solution.py:25
  144.3 4.0 %collective-permute-done.17 = f32[2,264,128]{2,1,0:T(8,128)S(1)} collective-permute-done((f32[2,264,128]{2,1,0:T(8,128)S(1)}, f32[2,264,128]{2,1,0:T(8,128)S(1)}, u32[]{:S(2)}, u32[]{:S(2)}) %collective-permute-start.17) | collective-permute-done | bytes 270368 | tf_op jit(solution)/shard_map/ppermute | solution.py:25
  149.3 4.1 %collective-permute-done.18 = f32[1,264,128]{2,1,0:T(8,128)S(1)} collective-permute-done((f32[1,264,128]{2,1,0:T(8,128)S(1)}, f32[1,264,128]{2,1,0:T(8,128)S(1)}, u32[]{:S(2)}, u32[]{:S(2)}) %collective-permute-start.18) | collective-permute-done | bytes 135200 | tf_op jit(solution)/shard_map/ppermute | solution.py:25
  (82 shorter events, 32.0 us)
Async XLA Ops:
  0.6 16.6 %copy-start.1 = (f32[128,2048]{1,0:T(8,128)S(1)}, f32[128,2048]{1,0:T(8,128)}, u32[]{:S(2)}) copy-start(f32[128,2048]{1,0:T(8,128)} %refs_0_.1) | copy-start | bytes 3145732
  0.6 22.3 %collective-permute-start = (f32[128,2048]{1,0:T(8,128)}, f32[128,2048]{1,0:T(8,128)}, u32[]{:S(2)}, u32[]{:S(2)}) collective-permute-start(f32[128,2048]{1,0:T(8,128)} %refs_0_.1), channel_id=1, source_target_pairs={{0,32},{1,33},{2,34},{3,35},{4,36},{5,37},{6,38},{7,39},{8,40},{9,... | collective-permute-start | bytes 3145736 | tf_op jit(solution)/shard_map/ppermute | solution.py:34
  3.7 5.0 %collective-permute-start.1 = (f32[32,1024]{1,0:T(8,128)S(1)}, f32[32,1024]{1,0:T(8,128)S(1)}, u32[]{:S(2)}, u32[]{:S(2)}) collective-permute-start(f32[32,1024]{1,0:T(8,128)S(1)} %get-tuple-element.97), channel_id=1, source_target_pairs={{0,1},{1,0},{2,3},{3,2},{4,5},{5,4},{6,7},{7,6},{8,9},{9,8},{10,11... | collective-permute-start | bytes 393224 | tf_op jit(solution)/shard_map/ppermute | solution.py:25
  5.3 8.9 %collective-permute-start.3 = (f32[32,1024]{1,0:T(8,128)S(1)}, f32[32,1024]{1,0:T(8,128)S(1)}, u32[]{:S(2)}, u32[]{:S(2)}) collective-permute-start(f32[32,1024]{1,0:T(8,128)S(1)} %get-tuple-element.96), channel_id=1, source_target_pairs={{0,4},{1,5},{2,6},{3,7},{4,0},{5,1},{6,2},{7,3},{8,12},{9,13},{10,... | collective-permute-start | bytes 393224 | tf_op jit(solution)/shard_map/ppermute | solution.py:25
  8.8 8.5 %collective-permute-start.2 = (f32[64,1024]{1,0:T(8,128)S(1)}, f32[64,1024]{1,0:T(8,128)S(1)}, u32[]{:S(2)}, u32[]{:S(2)}) collective-permute-start(f32[64,1024]{1,0:T(8,128)S(1)} %pad_maximum_fusion.4), channel_id=1, source_target_pairs={{0,3},{1,2},{2,1},{3,0},{4,7},{5,6},{6,5},{7,4},{8,11},{9,10},{10,... | collective-permute-start | bytes 786440 | tf_op jit(solution)/shard_map/ppermute | solution.py:25
  11.6 20.5 %collective-permute-start.9 = (f32[128,2048]{1,0:T(8,128)}, f32[128,2048]{1,0:T(8,128)}, u32[]{:S(2)}, u32[]{:S(2)}) collective-permute-start(f32[128,2048]{1,0:T(8,128)} %refs_0_.1), channel_id=1, source_target_pairs={{0,96},{1,97},{2,98},{3,99},{4,100},{5,101},{6,102},{7,103},{8,104... | collective-permute-start | bytes 3145736 | tf_op jit(solution)/shard_map/ppermute | solution.py:34
  14.2 8.6 %collective-permute-start.4 = (f32[64,1024]{1,0:T(8,128)S(1)}, f32[64,1024]{1,0:T(8,128)S(1)}, u32[]{:S(2)}, u32[]{:S(2)}) collective-permute-start(f32[64,1024]{1,0:T(8,128)S(1)} %pad_maximum_fusion.5), channel_id=1, source_target_pairs={{0,12},{1,13},{2,14},{3,15},{4,8},{5,9},{6,10},{7,11},{8,4},{9,5},... | collective-permute-start | bytes 786440 | tf_op jit(solution)/shard_map/ppermute | solution.py:25
  17.3 16.4 %collective-permute-start.7 = (f32[128,2048]{1,0:T(8,128)S(1)}, f32[128,2048]{1,0:T(8,128)S(1)}, u32[]{:S(2)}, u32[]{:S(2)}) collective-permute-start(f32[128,2048]{1,0:T(8,128)S(1)} %copy-done.1), channel_id=1, source_target_pairs={{0,16},{16,0},{32,48},{48,32},{64,80},{80,64},{96,112},{112,96},{1... | collective-permute-start | bytes 3145736 | tf_op jit(solution)/shard_map/ppermute | solution.py:38
  17.3 9.3 %collective-permute-start.11 = (f32[128,1024]{1,0:T(8,128)S(1)}, f32[128,1024]{1,0:T(8,128)S(1)}, u32[]{:S(2)}, u32[]{:S(2)}) collective-permute-start(f32[128,1024]{1,0:T(8,128)S(1)} %pad_maximum_fusion.2), channel_id=1, source_target_pairs={{0,4},{1,5},{2,6},{3,7},{4,0},{5,1},{6,2},{7,3},{8,12},{9,13},{10,... | collective-permute-start | bytes 1572872 | tf_op jit(solution)/shard_map/ppermute | solution.py:25
  22.9 9.3 %collective-permute-start.13 = (f32[128,1024]{1,0:T(8,128)S(1)}, f32[128,1024]{1,0:T(8,128)S(1)}, u32[]{:S(2)}, u32[]{:S(2)}) collective-permute-start(f32[128,1024]{1,0:T(8,128)S(1)} %pad_maximum_fusion.3), channel_id=1, source_target_pairs={{0,1},{1,0},{2,3},{3,2},{4,5},{5,4},{6,7},{7,6},{8,9},{9,8},{10,11... | collective-permute-start | bytes 1572872 | tf_op jit(solution)/shard_map/ppermute | solution.py:25
  23.0 16.5 %collective-permute-start.5 = (f32[128,2048]{1,0:T(8,128)}, f32[128,2048]{1,0:T(8,128)S(1)}, u32[]{:S(2)}, u32[]{:S(2)}) collective-permute-start(f32[128,2048]{1,0:T(8,128)} %collective-permute-done.refs_2_), channel_id=1, source_target_pairs={{0,96},{1,97},{2,98},{3,99},{4,100},{5,101},{6,102},{7,103},{8,104... | collective-permute-start | bytes 3145736 | tf_op jit(solution)/shard_map/ppermute | solution.py:34
  26.7 19.5 %collective-permute-start.12 = (f32[256,1024]{1,0:T(8,128)S(1)}, f32[256,1024]{1,0:T(8,128)}, u32[]{:S(2)}, u32[]{:S(2)}) collective-permute-start(f32[256,1024]{1,0:T(8,128)S(1)} %pad_maximum_fusion.refs_3_), channel_id=1, source_target_pairs={{0,12},{1,13},{2,14},{3,15},{4,8},{5,9},{6,10},{7,11},{8,4},{9,5},... | collective-permute-start | bytes 3145736 | tf_op jit(solution)/shard_map/ppermute | solution.py:25
  32.1 7.4 %collective-permute-start.8 = (f32[128,2048]{1,0:T(8,128)}, f32[128,2048]{1,0:T(8,128)}, u32[]{:S(2)}, u32[]{:S(2)}) collective-permute-start(f32[128,2048]{1,0:T(8,128)} %collective-permute-done.refs_2_), channel_id=1, source_target_pairs={{0,16},{16,0},{32,48},{48,32},{64,80},{80,64},{96,112},{112,96},{1... | collective-permute-start | bytes 3145736 | tf_op jit(solution)/shard_map/ppermute | solution.py:38
  32.1 7.4 %collective-permute-start.10 = (f32[128,2048]{1,0:T(8,128)}, f32[128,2048]{1,0:T(8,128)}, u32[]{:S(2)}, u32[]{:S(2)}) collective-permute-start(f32[128,2048]{1,0:T(8,128)} %collective-permute-done.9.refs_4_), channel_id=1, source_target_pairs={{0,16},{16,0},{32,48},{48,32},{64,80},{80,64},{96,112},{112,96},{1... | collective-permute-start | bytes 3145736 | tf_op jit(solution)/shard_map/ppermute | solution.py:38
  34.8 16.3 %collective-permute-start.14 = (f32[256,1024]{1,0:T(8,128)}, f32[256,1024]{1,0:T(8,128)}, u32[]{:S(2)}, u32[]{:S(2)}) collective-permute-start(f32[256,1024]{1,0:T(8,128)} %pad_maximum_fusion.1.refs_5_), channel_id=1, source_target_pairs={{0,3},{1,2},{2,1},{3,0},{4,7},{5,6},{6,5},{7,4},{8,11},{9,10},{10,... | collective-permute-start | bytes 3145736 | tf_op jit(solution)/shard_map/ppermute | solution.py:25
  39.4 20.3 %collective-permute-start.6 = (f32[128,2048]{1,0:T(8,128)S(1)}, f32[128,2048]{1,0:T(8,128)S(1)}, u32[]{:S(2)}, u32[]{:S(2)}) collective-permute-start(f32[128,2048]{1,0:T(8,128)S(1)} %collective-permute-done.5.refs_1_), channel_id=1, source_target_pairs={{0,16},{16,0},{32,48},{48,32},{64,80},{80,64},{96,112},{112,96},{1... | collective-permute-start | bytes 3145736 | tf_op jit(solution)/shard_map/ppermute | solution.py:38
  110.9 16.1 %collective-permute-start.19 = (f32[8,256,128]{2,1,0:T(8,128)S(1)}, f32[8,256,128]{2,1,0:T(8,128)S(1)}, u32[]{:S(2)}, u32[]{:S(2)}) collective-permute-start(f32[8,256,128]{2,1,0:T(8,128)S(1)} %shard_map.94), channel_id=1, source_target_pairs={{0,3},{1,2},{2,1},{3,0},{4,7},{5,6},{6,5},{7,4},{8,11},{9,10},{10,... | collective-permute-start | bytes 3145736 | tf_op jit(solution)/shard_map/ppermute | solution.py:25
  112.1 16.4 %collective-permute-start.15 = (f32[8,264,128]{2,1,0:T(8,128)S(1)}, f32[8,264,128]{2,1,0:T(8,128)S(1)}, u32[]{:S(2)}, u32[]{:S(2)}) collective-permute-start(f32[8,264,128]{2,1,0:T(8,128)S(1)} %shard_map.93), channel_id=1, source_target_pairs={{0,12},{1,13},{2,14},{3,15},{4,8},{5,9},{6,10},{7,11},{8,4},{9,5},... | collective-permute-start | bytes 3244040 | tf_op jit(solution)/shard_map/ppermute | solution.py:25
  127.1 9.3 %collective-permute-start.20 = (f32[4,256,128]{2,1,0:T(8,128)S(1)}, f32[4,256,128]{2,1,0:T(8,128)S(1)}, u32[]{:S(2)}, u32[]{:S(2)}) collective-permute-start(f32[4,256,128]{2,1,0:T(8,128)S(1)} %slice.63), channel_id=1, source_target_pairs={{0,1},{1,0},{2,3},{3,2},{4,5},{5,4},{6,7},{7,6},{8,9},{9,8},{10,11... | collective-permute-start | bytes 1572872 | tf_op jit(solution)/shard_map/ppermute | solution.py:25
  128.6 10.5 %collective-permute-start.16 = (f32[4,264,128]{2,1,0:T(8,128)S(1)}, f32[4,264,128]{2,1,0:T(8,128)S(1)}, u32[]{:S(2)}, u32[]{:S(2)}) collective-permute-start(f32[4,264,128]{2,1,0:T(8,128)S(1)} %slice.57), channel_id=1, source_target_pairs={{0,4},{1,5},{2,6},{3,7},{4,0},{5,1},{6,2},{7,3},{8,12},{9,13},{10,... | collective-permute-start | bytes 1622024 | tf_op jit(solution)/shard_map/ppermute | solution.py:25
  136.5 7.7 %collective-permute-start.21 = (f32[2,256,128]{2,1,0:T(8,128)S(1)}, f32[2,256,128]{2,1,0:T(8,128)S(1)}, u32[]{:S(2)}, u32[]{:S(2)}) collective-permute-start(f32[2,256,128]{2,1,0:T(8,128)S(1)} %slice.65), channel_id=1, source_target_pairs={{0,12},{1,13},{2,14},{3,15},{4,8},{5,9},{6,10},{7,11},{8,4},{9,5},... | collective-permute-start | bytes 786440 | tf_op jit(solution)/shard_map/ppermute | solution.py:25
  139.3 9.0 %collective-permute-start.17 = (f32[2,264,128]{2,1,0:T(8,128)S(1)}, f32[2,264,128]{2,1,0:T(8,128)S(1)}, u32[]{:S(2)}, u32[]{:S(2)}) collective-permute-start(f32[2,264,128]{2,1,0:T(8,128)S(1)} %slice.59), channel_id=1, source_target_pairs={{0,3},{1,2},{2,1},{3,0},{4,7},{5,6},{6,5},{7,4},{8,11},{9,10},{10,... | collective-permute-start | bytes 811016 | tf_op jit(solution)/shard_map/ppermute | solution.py:25
  144.2 5.1 %collective-permute-start.22 = (f32[1,256,128]{2,1,0:T(8,128)S(1)}, f32[1,256,128]{2,1,0:T(8,128)S(1)}, u32[]{:S(2)}, u32[]{:S(2)}) collective-permute-start(f32[1,256,128]{2,1,0:T(8,128)S(1)} %slice.67), channel_id=1, source_target_pairs={{0,4},{1,5},{2,6},{3,7},{4,0},{5,1},{6,2},{7,3},{8,12},{9,13},{10,... | collective-permute-start | bytes 393224 | tf_op jit(solution)/shard_map/ppermute | solution.py:25
  148.3 5.1 %collective-permute-start.18 = (f32[1,264,128]{2,1,0:T(8,128)S(1)}, f32[1,264,128]{2,1,0:T(8,128)S(1)}, u32[]{:S(2)}, u32[]{:S(2)}) collective-permute-start(f32[1,264,128]{2,1,0:T(8,128)S(1)} %slice.61), channel_id=1, source_target_pairs={{0,1},{1,0},{2,3},{3,2},{4,5},{5,4},{6,7},{7,6},{8,9},{9,8},{10,11... | collective-permute-start | bytes 405512 | tf_op jit(solution)/shard_map/ppermute | solution.py:25
  (9 other events, 83.1 us)

commit v3 on v2

--- a/solution.py
+++ b/solution.py
@@ -14,7 +14,8 @@
 ROWS, COLS = 512, 1024
 BF, F32 = jnp.bfloat16, jnp.float32
 
-XA, XB, YA, YB = (1, 3), (3, 1), (4, 12), (12, 4)
+UA, UB, VA, VB = (1, 4), (3, 12), (4, 1), (12, 3)
+FIRST, SECOND = (VA, VB, UA, UB), (VB, VA, UB, UA)
 ZA, ZB = (1, 3), (3, 1)
 
 
@@ -41,7 +42,7 @@
 def row_places():
     tables = []
     for core in range(2):
-        masks = [m[core] for m in (XA, XB, YA, YB)]
+        masks = [m[core] for m in FIRST]
         table = []
         for p in range(16):
             rel = 0
@@ -67,6 +68,10 @@
     row = lax.axis_index("row").astype(jnp.int32)
     table = jnp.where(row % 2 == 0, jnp.array(tables[0], jnp.int32), jnp.array(tables[1], jnp.int32))
     return table ^ row
+
+
+def second(p):
+    return (p & 5) << 1 | (p & 10) >> 1
 
 
 def vmem(count):
@@ -197,8 +202,7 @@
             copies[-1].start()
     middle = noise[0].shape[1]
     for p in range(16):
-        xs, ys = p % 4, p // 4
-        q = xs * 4 + ys
+        q = second(p)
         one = noise[p // 8][32 * (p % 8) : 32 * (p % 8) + 32, :]
         two = noise[2 + q // 8][32 * (q % 8) : 32 * (q % 8) + 32, :]
         top, under = slice(32 * p, 32 * p + 32), slice(ROWS + 32 * p, ROWS + 32 * p + 32)
@@ -331,35 +335,37 @@
     return jnp.dot(one, two, preferred_element_type=F32)
 
 
-def product_body(blocks, lanes, wh, wl, denom, h0, l0, h1, l1, out):
+def product_body(blocks, chunks, wh, wl, denom, h0, l0, h1, l1, *outs):
     terms = [
         jnp.concatenate([ref[block(p), at] for ref in (wh, wl) for p in blocks], axis=0)
         for at in (slice(0, 768), slice(768, 1024))
     ]
-    for n in range(4):
-        at = slice(lanes + 256 * n, lanes + 256 * n + 256)
-        both = dot(terms[0], h0[:, at]) + dot(terms[1], h1[:, at])
-        more = dot(terms[0][:256], l0[:, at]) + dot(terms[1][:256], l1[:, at])
-        total = both[:256] + both[256:] + more
-        for i in range(8):
-            for t in range(2):
-                tile = total[32 * i : 32 * i + 32, 128 * t : 128 * t + 128]
-                out[i, 32 * (2 * n + t) : 32 * (2 * n + t) + 32, :] = tile
-    if lanes == 0:
-        eye = diagonal()[:32, :]
-        for i, p in enumerate(blocks):
-            row = jnp.sum(jnp.where(eye, denom[block(p), :], 0.0), axis=0, keepdims=True)
-            out[i, 256:264, :] = jnp.broadcast_to(row, (8, 128))
+    for chunk, out in zip(chunks, outs):
+        for n in range(2):
+            at = slice(512 * chunk + 256 * n, 512 * chunk + 256 * n + 256)
+            both = dot(terms[0], h0[:, at]) + dot(terms[1], h1[:, at])
+            more = dot(terms[0][:256], l0[:, at]) + dot(terms[1][:256], l1[:, at])
+            total = both[:256] + both[256:] + more
+            for i in range(8):
+                for t in range(2):
+                    tile = total[32 * i : 32 * i + 32, 128 * t : 128 * t + 128]
+                    out[i, 32 * (2 * n + t) : 32 * (2 * n + t) + 32, :] = tile
+        if chunk == 0:
+            eye = diagonal()[:32, :]
+            for i, p in enumerate(blocks):
+                row = jnp.sum(jnp.where(eye, denom[block(p), :], 0.0), axis=0, keepdims=True)
+                out[i, 128:136, :] = jnp.broadcast_to(row, (8, 128))
 
 
 def end_body(left, right, noise, times, path, velocity):
     eye = diagonal()[:32, :]
-    wide = jnp.broadcast_to(left[0, 256:257, :], (32, 128))
+    wide = jnp.broadcast_to(left[0, 128:129, :], (32, 128))
     inverse = 1.0 / jnp.sum(jnp.where(eye, wide, 0.0), axis=1, keepdims=True)
-    for side, ref in enumerate((left, right)):
+    for side, (ref, starts) in enumerate(((left, (0, 136)), (right, (0, 128)))):
         for t in range(8):
             lanes = slice(1024 * side + 128 * t, 1024 * side + 128 * t + 128)
-            target = ref[0, 32 * t : 32 * t + 32, :] * inverse
+            first = starts[t // 4] + 32 * (t % 4)
+            target = ref[0, first : first + 32, :] * inverse
             own = noise[:, lanes]
             at = times[:, :1]
             path[:, lanes] = (1.0 - at) * own + at * target
@@ -370,22 +376,17 @@
     return lax.optimization_barrier(values)
 
 
-def product(blocks, lanes, *arrays):
-    def body(*refs):
-        product_body(blocks, lanes, *refs)
-
+def product(blocks, chunks, *arrays):
     return call(
-        body,
-        shape((8, 264 if lanes == 0 else 256, 128)),
+        lambda *refs: product_body(blocks, chunks, *refs),
+        tuple(shape((8, 136 if chunk == 0 else 128, 128)) for chunk in chunks),
         0,
         7,
-        flops=3 * 2 * 256 * 1024 * 1024,
-        moved=6 * 2**20,
     )(*arrays)
 
 
-X_FIRST = list(range(16))
-Y_FIRST = [ys * 4 + xs for xs in range(4) for ys in range(4)]
+ORDER_1 = list(range(16))
+ORDER_2 = [second(p) for p in ORDER_1]
 
 
 def per_device(noise, data, times):
@@ -396,7 +397,7 @@
 
     near, far = swap_z(data, ZA), swap_z(data, ZB)
     parts = [noise[:, :middle], noise[:, middle:]]
-    orders = ((XA, XB, YA, YB), (YA, YB, XA, XB))
+    orders = (FIRST, SECOND)
     stages = []
     for step in range(3):
         parts = [
@@ -491,22 +492,34 @@
     )(cplaces, got, gains, plan)
 
     rest = (wh, wl, denom, h0, l0, h1, l1)
-    left_out = product(X_FIRST[8:], 0, *rest)
-    rest = after(left_out, *rest)
-    left_out, rest = rest[0], rest[1:]
-    right_out = product(Y_FIRST[8:], middle, *rest)
-    rest = after(right_out, *rest)
-    right_out, rest = rest[0], rest[1:]
-    left_in, right_in = swap_col(left_out, YB), swap_col(right_out, XB)
-    left = product(X_FIRST[:8], 0, *rest)
-    rest = after(left, *rest)
-    left, rest = rest[0], rest[1:]
-    right = product(Y_FIRST[:8], middle, *rest)
-    left, right = left + left_in, right + right_in
-    for first, second in zip((YA, XB, XA), (XA, YB, YA)):
-        rows = left.shape[0] // 2
-        left_in, right_in = swap_col(left[rows:], first), swap_col(right[rows:], second)
-        left, right = left[:rows] + left_in, right[:rows] + right_in
+    halves = ((ORDER_1, (0, 1), FIRST[::-1]), (ORDER_2, (2, 3), SECOND[::-1]))
+    leaving = {}
+    for i in range(2):
+        for blocks, chunks, steps in halves:
+            (out,) = product(blocks[8:], (chunks[i],), *rest)
+            out, *rest = after(out, *rest)
+            leaving[chunks[i]] = swap_col(out, steps[0])
+    sums = {}
+    for blocks, chunks, steps in halves:
+        out = product(blocks[:8], chunks, *rest)
+        *out, denom = after(*out, rest[2])
+        rest = (rest[0], rest[1], denom) + tuple(rest[3:])
+        sums.update(zip(chunks, out))
+    order = [(chunks[i], steps) for i in range(2) for _, chunks, steps in halves]
+    last = rest[2]
+    for chunk, steps in order:
+        sums[chunk] = last = sums[chunk] + after(leaving[chunk], last)[0]
+        leaving[chunk] = swap_col(last[4:], steps[1])
+    for chunk, steps in order:
+        sums[chunk] = last = sums[chunk][:4] + after(leaving[chunk], last)[0]
+    ends = [
+        jnp.concatenate([sums[chunk] for chunk in chunks], axis=1) for _, chunks, _ in halves
+    ]
+    for step, rows in ((2, 2), (3, 1)):
+        coming = [swap_col(end[rows:], half[2][step]) for end, half in zip(ends, halves)]
+        for i in range(2):
+            ends[i] = last = ends[i][:rows] + after(coming[i], last)[0]
+    left, right = ends
     wide_times = jnp.broadcast_to(times[:, None], (times.shape[0], 128))
     outs = (shape(noise.shape), shape(noise.shape))
     return call(end_body, outs, 0, 4)(left, right, noise, wide_times)

time: 155 us -> 148 us (0.955)
  waiting for transfers between devices: 50.6 us -> 37.9 us
  starting transfers between devices: 27.8 us -> 34.1 us
    ppermute x16 -> x20, waiting for transfers between devices: 46 us -> 33.3 us  [swap_col(): return lax.ppermute(value, BOTH, pairs)]
    ppermute x16 -> x20, starting transfers between devices: 20.1 us -> 27.8 us  [swap_col(): return lax.ppermute(value, BOTH, pairs)]
    pallas_call x4 -> x6, Pallas kernels: 7.19 us -> 7.52 us  [product(): call(lambda *refs: product_body(blocks, chunks, *refs), tuple((shape((8,...]
    unnamed x20 -> x18, local copies, waits for them, and re-layouts: 3.57 us -> 3.54 us
  transfers between devices with their start and end apart: 23 -> 27, of which waited for: 13 -> 16; matrix products, arithmetic and copies ran while one was open for 2% -> 2% of each run, Pallas kernels for 11% -> 13%
where the time goes in v3:
time: 148 us
  blocking collectives  39.3 us (27%)
  waiting for transfers between devices  37.9 us (26%)
  starting transfers between devices  34.1 us (23%)
  Pallas kernels  28.8 us (19%)
  local copies, waits for them, and re-layouts  4.69 us (3%)
  other arithmetic  1.82 us (1%)
    ppermute x20, waiting for transfers between devices, swap_col(): return lax.ppermute(value, BOTH, pairs)  33.3 us
    ppermute x20, starting transfers between devices, swap_col(): return lax.ppermute(value, BOTH, pairs)  27.8 us
    all_to_all x2, blocking collectives, per_device(): got = lax.all_to_all(send, 'col', 0, 0)  22.6 us
    all_to_all x2, blocking collectives, per_device(): got = lax.all_to_all(send, 'row', 0, 0)  16.7 us
    pallas_call x1, Pallas kernels, per_device(): call(lambda *refs: early_body(scale, *refs), (shape((2 * ROWS, features),...  8.59 us
    pallas_call x6, Pallas kernels, product(): call(lambda *refs: product_body(blocks, chunks, *refs), tuple((shape((8,...  7.52 us
    ppermute x3, starting transfers between devices, swap_z(): return lax.ppermute(value, BOTH, pairs)  5.79 us
    ppermute x3, waiting for transfers between devices, swap_z(): return lax.ppermute(value, BOTH, pairs)  4.57 us
  transfers between devices with their start and end apart: 27, of which 16 were waited for; matrix products, arithmetic and copies ran while one was open for 2% of the time, Pallas kernels for 13%

profile of v3, /device:TPU:0, one launch (start us, length us, event | category | flops | bytes accessed | tf_op | source)
XLA Modules:
  0.0 147.7 jit_solution(12430024252855958386)
XLA Ops:
  0.6 2.1 %collective-permute-start = (f32[128,2048]{1,0:T(8,128)}, f32[128,2048]{1,0:T(8,128)}, u32[]{:S(2)}, u32[]{:S(2)}) collective-permute-start(f32[128,2048]{1,0:T(8,128)} %refs_0_.1), channel_id=1, source_target_pairs={{0,32},{1,33},{2,34},{3,35},{4,36},{5,37},{6,38},{7,39},{8,40},{9,... | collective-permute-start | bytes 3145736 | tf_op jit(solution)/shard_map/ppermute | solution.py:35
  5.4 2.2 %collective-permute-start.3 = (f32[32,1024]{1,0:T(8,128)S(1)}, f32[32,1024]{1,0:T(8,128)S(1)}, u32[]{:S(2)}, u32[]{:S(2)}) collective-permute-start(f32[32,1024]{1,0:T(8,128)S(1)} %get-tuple-element.152), channel_id=1, source_target_pairs={{0,12},{1,13},{2,14},{3,15},{4,8},{5,9},{6,10},{7,11},{8,4},{9,5},... | collective-permute-start | bytes 393224 | tf_op jit(solution)/shard_map/ppermute | solution.py:26
  8.8 3.1 %collective-permute-start.2 = (f32[64,1024]{1,0:T(8,128)S(1)}, f32[64,1024]{1,0:T(8,128)S(1)}, u32[]{:S(2)}, u32[]{:S(2)}) collective-permute-start(f32[64,1024]{1,0:T(8,128)S(1)} %pad_maximum_fusion.6), channel_id=1, source_target_pairs={{0,12},{1,13},{2,14},{3,15},{4,8},{5,9},{6,10},{7,11},{8,4},{9,5},... | collective-permute-start | bytes 786440 | tf_op jit(solution)/shard_map/ppermute | solution.py:26
  11.9 2.5 %collective-permute-start.9 = (f32[128,2048]{1,0:T(8,128)}, f32[128,2048]{1,0:T(8,128)}, u32[]{:S(2)}, u32[]{:S(2)}) collective-permute-start(f32[128,2048]{1,0:T(8,128)} %refs_0_.1), channel_id=1, source_target_pairs={{0,96},{1,97},{2,98},{3,99},{4,100},{5,101},{6,102},{7,103},{8,104... | collective-permute-start | bytes 3145736 | tf_op jit(solution)/shard_map/ppermute | solution.py:35
  18.0 4.5 %collective-permute-done.4 = f32[64,1024]{1,0:T(8,128)S(1)} collective-permute-done((f32[64,1024]{1,0:T(8,128)S(1)}, f32[64,1024]{1,0:T(8,128)S(1)}, u32[]{:S(2)}, u32[]{:S(2)}) %collective-permute-start.4) | collective-permute-done | bytes 262176 | tf_op jit(solution)/shard_map/ppermute | solution.py:26
  22.6 2.8 %collective-permute-start.13 = (f32[128,1024]{1,0:T(8,128)S(1)}, f32[128,1024]{1,0:T(8,128)S(1)}, u32[]{:S(2)}, u32[]{:S(2)}) collective-permute-start(f32[128,1024]{1,0:T(8,128)S(1)} %pad_maximum_fusion.3), channel_id=1, source_target_pairs={{0,3},{1,2},{2,1},{3,0},{4,7},{5,6},{6,5},{7,4},{8,11},{9,10},{10,... | collective-permute-start | bytes 1572872 | tf_op jit(solution)/shard_map/ppermute | solution.py:26
  26.8 2.8 %collective-permute-start.12 = (f32[256,1024]{1,0:T(8,128)S(1)}, f32[256,1024]{1,0:T(8,128)}, u32[]{:S(2)}, u32[]{:S(2)}) collective-permute-start(f32[256,1024]{1,0:T(8,128)S(1)} %pad_maximum_fusion.refs_3_), channel_id=1, source_target_pairs={{0,3},{1,2},{2,1},{3,0},{4,7},{5,6},{6,5},{7,4},{8,11},{9,10},{10,... | collective-permute-start | bytes 3145736 | tf_op jit(solution)/shard_map/ppermute | solution.py:26
  29.6 3.5 %collective-permute-done.13 = f32[128,1024]{1,0:T(8,128)S(1)} collective-permute-done((f32[128,1024]{1,0:T(8,128)S(1)}, f32[128,1024]{1,0:T(8,128)S(1)}, u32[]{:S(2)}, u32[]{:S(2)}) %collective-permute-start.13) | collective-permute-done | bytes 524320 | tf_op jit(solution)/shard_map/ppermute | solution.py:26
  37.1 4.6 %collective-permute-done.5.refs_1_ = f32[128,2048]{1,0:T(8,128)S(1)} collective-permute-done((f32[128,2048]{1,0:T(8,128)}, f32[128,2048]{1,0:T(8,128)S(1)}, u32[]{:S(2)}, u32[]{:S(2)}) %collective-permute-start.5) | collective-permute-done | bytes 1048608 | tf_op jit(solution)/shard_map/ppermute | solution.py:35
  44.2 4.3 %shard_map.86 = (f32[768,128]{1,0:T(8,128)S(1)}, bf16[768,2048]{1,0:T(8,128)(2,1)S(1)}, bf16[768,2048]{1,0:T(8,128)(2,1)S(1)}) custom-call(f32[128,2048]{1,0:T(8,128)S(1)} %copy-done.1, f32[128,2048]{1,0:T(8,128)S(1)} %copy-done.3, f32[128,2048]{1,0:T(8,128)} %collective-permute-done.refs_2_, f32[128,2048]{1,0:T(8,128)} %collective-permute-done.8.refs_3_, ...), custom_call_target="tpu_custom_call" | custom-call | bytes 12582912 | tf_op jit(solution)/shard_map/pallas_call | solution.py:416
  48.5 2.3 %collective-permute-done.14.refs_6_ = f32[256,1024]{1,0:T(8,128)} collective-permute-done((f32[256,1024]{1,0:T(8,128)}, f32[256,1024]{1,0:T(8,128)}, u32[]{:S(2)}, u32[]{:S(2)}) %collective-permute-start.14) | collective-permute-done | bytes 1048608 | tf_op jit(solution)/shard_map/ppermute | solution.py:26
  50.8 8.6 %shard_map.87 = (bf16[1024,2048]{1,0:T(8,128)(2,1)S(1)}, f32[512,128]{1,0:T(8,128)S(1)}, f32[512,768]{1,0:T(8,128)S(1)}, f32[512,128]{1,0:T(8,128)S(1)}, f32[512,128]{1,0:T(8,128)S(1)}) custom-call(bf16[768,2048]{1,0:T(8,128)(2,1)S(1)} %get-tuple-element.124.refs_0_.refs_3_, bf16[768,2048]{1,0:T(8,128)(2,1)S(1)} %get-tuple-element.125.refs_1_.refs_4_, ...), custom_call_target="tpu_custom_call" | custom-call | flops 4831838208 | bytes 16777216 | tf_op jit(solution)/shard_map/pallas_call | solution.py:428
  59.5 3.3 %shard_map.88 = (f32[512,256]{1,0:T(8,128)S(1)}, f32[16,8,128]{2,1,0:T(8,128)S(1)}, bf16[256,2048]{1,0:T(8,128)(2,1)S(1)}, bf16[256,2048]{1,0:T(8,128)(2,1)S(1)}) custom-call(s32[16]{0:T(128)S(1)} %fusion.4.refs_0_.rplaces, f32[128,2048]{1,0:T(8,128)S(1)} %collective-permute-done.5.refs_1_, f32[128,2048]{1,0:T(8,128)S(1)} %collective-permute-done.6.refs_2_, ...), custom_call_target="tpu_custom_call" | custom-call | flops 1610612736 | bytes 8388608 | tf_op jit(solution)/shard_map/pallas_call | solution.py:443
  62.8 11.8 %all_to_all.20.got = f32[16,8,128]{2,1,0:T(8,128)S(1)} all-to-all(f32[16,8,128]{2,1,0:T(8,128)S(1)} %get-tuple-element.88), channel_id=1, replica_groups=mesh['row'=8,'col'=16] {'col'}, dimensions={0} | all-to-all | bytes 131072 | tf_op jit(solution)/shard_map/all_to_all | solution.py:461
  75.9 8.9 %all_to_all.21.got = f32[8,16,128]{2,1,0:T(8,128)S(1)} all-to-all(f32[8,16,128]{2,1,0:T(8,128)S(1)} %get-tuple-element.91), channel_id=1, replica_groups=mesh['row'=8,'col'=16] {'row'}, dimensions={0} | all-to-all | bytes 131072 | tf_op jit(solution)/shard_map/all_to_all | solution.py:469
  85.7 10.8 %all_to_all.22.got = f32[16,8,128]{2,1,0:T(8,128)S(1)} all-to-all(f32[16,8,128]{2,1,0:T(8,128)S(1)} %get-tuple-element.93), channel_id=1, replica_groups=mesh['row'=8,'col'=16] {'col'}, dimensions={0} | all-to-all | bytes 131072 | tf_op jit(solution)/shard_map/all_to_all | solution.py:477
  97.4 7.8 %all_to_all.23.got = f32[8,8,128]{2,1,0:T(8,128)S(1)} all-to-all(f32[8,8,128]{2,1,0:T(8,128)S(1)} %shard_map.91), channel_id=1, replica_groups=mesh['row'=8,'col'=16] {'row'}, dimensions={0} | all-to-all | bytes 65536 | tf_op jit(solution)/shard_map/all_to_all | solution.py:485
  110.9 2.1 %collective-permute-start.18 = (f32[8,128,128]{2,1,0:T(8,128)S(1)}, f32[8,128,128]{2,1,0:T(8,128)S(1)}, u32[]{:S(2)}, u32[]{:S(2)}) collective-permute-start(f32[8,128,128]{2,1,0:T(8,128)S(1)} %shard_map.95), channel_id=1, source_target_pairs={{0,3},{1,2},{2,1},{3,0},{4,7},{5,6},{6,5},{7,4},{8,11},{9,10},{10,... | collective-permute-start | bytes 1572872 | tf_op jit(solution)/shard_map/ppermute | solution.py:26
  121.5 2.3 %collective-permute-done.18 = f32[8,128,128]{2,1,0:T(8,128)S(1)} collective-permute-done((f32[8,128,128]{2,1,0:T(8,128)S(1)}, f32[8,128,128]{2,1,0:T(8,128)S(1)}, u32[]{:S(2)}, u32[]{:S(2)}) %collective-permute-start.18) | collective-permute-done | bytes 524320 | tf_op jit(solution)/shard_map/ppermute | solution.py:26
  124.8 2.1 %collective-permute-start.23 = (f32[4,128,128]{2,1,0:T(8,128)S(1)}, f32[4,128,128]{2,1,0:T(8,128)S(1)}, u32[]{:S(2)}, u32[]{:S(2)}) collective-permute-start(f32[4,128,128]{2,1,0:T(8,128)S(1)} %slice.81), channel_id=1, source_target_pairs={{0,3},{1,2},{2,1},{3,0},{4,7},{5,6},{6,5},{7,4},{8,11},{9,10},{10,... | collective-permute-start | bytes 786440 | tf_op jit(solution)/shard_map/ppermute | solution.py:26
  127.9 3.1 %collective-permute-done.20 = f32[4,128,128]{2,1,0:T(8,128)S(1)} collective-permute-done((f32[4,128,128]{2,1,0:T(8,128)S(1)}, f32[4,128,128]{2,1,0:T(8,128)S(1)}, u32[]{:S(2)}, u32[]{:S(2)}) %collective-permute-start.20) | collective-permute-done | bytes 262176 | tf_op jit(solution)/shard_map/ppermute | solution.py:26
  133.8 6.4 %collective-permute-done.22 = f32[2,264,128]{2,1,0:T(8,128)S(1)} collective-permute-done((f32[2,264,128]{2,1,0:T(8,128)S(1)}, f32[2,264,128]{2,1,0:T(8,128)S(1)}, u32[]{:S(2)}, u32[]{:S(2)}) %collective-permute-start.22) | collective-permute-done | bytes 270368 | tf_op jit(solution)/shard_map/ppermute | solution.py:26
  140.3 2.0 %collective-permute-start.26 = (f32[1,256,128]{2,1,0:T(8,128)S(1)}, f32[1,256,128]{2,1,0:T(8,128)S(1)}, u32[]{:S(2)}, u32[]{:S(2)}) collective-permute-start(f32[1,256,128]{2,1,0:T(8,128)S(1)} %slice.87), channel_id=1, source_target_pairs={{0,12},{1,13},{2,14},{3,15},{4,8},{5,9},{6,10},{7,11},{8,4},{9,5},... | collective-permute-start | bytes 393224 | tf_op jit(solution)/shard_map/ppermute | solution.py:26
  142.3 2.9 %collective-permute-done.24 = f32[1,264,128]{2,1,0:T(8,128)S(1)} collective-permute-done((f32[1,264,128]{2,1,0:T(8,128)S(1)}, f32[1,264,128]{2,1,0:T(8,128)S(1)}, u32[]{:S(2)}, u32[]{:S(2)}) %collective-permute-start.24) | collective-permute-done | bytes 135200 | tf_op jit(solution)/shard_map/ppermute | solution.py:26
  (96 shorter events, 39.9 us)
Async XLA Ops:
  0.6 24.8 %collective-permute-start = (f32[128,2048]{1,0:T(8,128)}, f32[128,2048]{1,0:T(8,128)}, u32[]{:S(2)}, u32[]{:S(2)}) collective-permute-start(f32[128,2048]{1,0:T(8,128)} %refs_0_.1), channel_id=1, source_target_pairs={{0,32},{1,33},{2,34},{3,35},{4,36},{5,37},{6,38},{7,39},{8,40},{9,... | collective-permute-start | bytes 3145736 | tf_op jit(solution)/shard_map/ppermute | solution.py:35
  5.4 9.0 %collective-permute-start.3 = (f32[32,1024]{1,0:T(8,128)S(1)}, f32[32,1024]{1,0:T(8,128)S(1)}, u32[]{:S(2)}, u32[]{:S(2)}) collective-permute-start(f32[32,1024]{1,0:T(8,128)S(1)} %get-tuple-element.152), channel_id=1, source_target_pairs={{0,12},{1,13},{2,14},{3,15},{4,8},{5,9},{6,10},{7,11},{8,4},{9,5},... | collective-permute-start | bytes 393224 | tf_op jit(solution)/shard_map/ppermute | solution.py:26
  8.8 7.7 %collective-permute-start.2 = (f32[64,1024]{1,0:T(8,128)S(1)}, f32[64,1024]{1,0:T(8,128)S(1)}, u32[]{:S(2)}, u32[]{:S(2)}) collective-permute-start(f32[64,1024]{1,0:T(8,128)S(1)} %pad_maximum_fusion.6), channel_id=1, source_target_pairs={{0,12},{1,13},{2,14},{3,15},{4,8},{5,9},{6,10},{7,11},{8,4},{9,5},... | collective-permute-start | bytes 786440 | tf_op jit(solution)/shard_map/ppermute | solution.py:26
  11.9 21.2 %collective-permute-start.9 = (f32[128,2048]{1,0:T(8,128)}, f32[128,2048]{1,0:T(8,128)}, u32[]{:S(2)}, u32[]{:S(2)}) collective-permute-start(f32[128,2048]{1,0:T(8,128)} %refs_0_.1), channel_id=1, source_target_pairs={{0,96},{1,97},{2,98},{3,99},{4,100},{5,101},{6,102},{7,103},{8,104... | collective-permute-start | bytes 3145736 | tf_op jit(solution)/shard_map/ppermute | solution.py:35
  14.5 8.1 %collective-permute-start.4 = (f32[64,1024]{1,0:T(8,128)S(1)}, f32[64,1024]{1,0:T(8,128)S(1)}, u32[]{:S(2)}, u32[]{:S(2)}) collective-permute-start(f32[64,1024]{1,0:T(8,128)S(1)} %pad_maximum_fusion.7), channel_id=1, source_target_pairs={{0,4},{1,5},{2,6},{3,7},{4,0},{5,1},{6,2},{7,3},{8,12},{9,13},{10,... | collective-permute-start | bytes 786440 | tf_op jit(solution)/shard_map/ppermute | solution.py:26
  14.7 20.0 %collective-permute-start.7 = (f32[128,2048]{1,0:T(8,128)}, f32[128,2048]{1,0:T(8,128)S(1)}, u32[]{:S(2)}, u32[]{:S(2)}) collective-permute-start(f32[128,2048]{1,0:T(8,128)} %refs_0_.1), channel_id=1, source_target_pairs={{0,16},{16,0},{32,48},{48,32},{64,80},{80,64},{96,112},{112,96},{1... | collective-permute-start | bytes 3145736 | tf_op jit(solution)/shard_map/ppermute | solution.py:39
  16.5 10.2 %collective-permute-start.11 = (f32[128,1024]{1,0:T(8,128)S(1)}, f32[128,1024]{1,0:T(8,128)S(1)}, u32[]{:S(2)}, u32[]{:S(2)}) collective-permute-start(f32[128,1024]{1,0:T(8,128)S(1)} %pad_maximum_fusion.2), channel_id=1, source_target_pairs={{0,1},{1,0},{2,3},{3,2},{4,5},{5,4},{6,7},{7,6},{8,9},{9,8},{10,11... | collective-permute-start | bytes 1572872 | tf_op jit(solution)/shard_map/ppermute | solution.py:26
  22.6 10.5 %collective-permute-start.13 = (f32[128,1024]{1,0:T(8,128)S(1)}, f32[128,1024]{1,0:T(8,128)S(1)}, u32[]{:S(2)}, u32[]{:S(2)}) collective-permute-start(f32[128,1024]{1,0:T(8,128)S(1)} %pad_maximum_fusion.3), channel_id=1, source_target_pairs={{0,3},{1,2},{2,1},{3,0},{4,7},{5,6},{6,5},{7,4},{8,11},{9,10},{10,... | collective-permute-start | bytes 1572872 | tf_op jit(solution)/shard_map/ppermute | solution.py:26
  25.5 16.2 %collective-permute-start.5 = (f32[128,2048]{1,0:T(8,128)}, f32[128,2048]{1,0:T(8,128)S(1)}, u32[]{:S(2)}, u32[]{:S(2)}) collective-permute-start(f32[128,2048]{1,0:T(8,128)} %collective-permute-done.refs_2_), channel_id=1, source_target_pairs={{0,96},{1,97},{2,98},{3,99},{4,100},{5,101},{6,102},{7,103},{8,104... | collective-permute-start | bytes 3145736 | tf_op jit(solution)/shard_map/ppermute | solution.py:35
  26.8 21.8 %collective-permute-start.12 = (f32[256,1024]{1,0:T(8,128)S(1)}, f32[256,1024]{1,0:T(8,128)}, u32[]{:S(2)}, u32[]{:S(2)}) collective-permute-start(f32[256,1024]{1,0:T(8,128)S(1)} %pad_maximum_fusion.refs_3_), channel_id=1, source_target_pairs={{0,3},{1,2},{2,1},{3,0},{4,7},{5,6},{6,5},{7,4},{8,11},{9,10},{10,... | collective-permute-start | bytes 3145736 | tf_op jit(solution)/shard_map/ppermute | solution.py:26
  33.1 8.7 %collective-permute-start.8 = (f32[128,2048]{1,0:T(8,128)}, f32[128,2048]{1,0:T(8,128)}, u32[]{:S(2)}, u32[]{:S(2)}) collective-permute-start(f32[128,2048]{1,0:T(8,128)} %collective-permute-done.refs_2_), channel_id=1, source_target_pairs={{0,16},{16,0},{32,48},{48,32},{64,80},{80,64},{96,112},{112,96},{1... | collective-permute-start | bytes 3145736 | tf_op jit(solution)/shard_map/ppermute | solution.py:39
  33.1 8.7 %collective-permute-start.10 = (f32[128,2048]{1,0:T(8,128)}, f32[128,2048]{1,0:T(8,128)}, u32[]{:S(2)}, u32[]{:S(2)}) collective-permute-start(f32[128,2048]{1,0:T(8,128)} %collective-permute-done.9.refs_4_), channel_id=1, source_target_pairs={{0,16},{16,0},{32,48},{48,32},{64,80},{80,64},{96,112},{112,96},{1... | collective-permute-start | bytes 3145736 | tf_op jit(solution)/shard_map/ppermute | solution.py:39
  35.7 15.1 %collective-permute-start.14 = (f32[256,1024]{1,0:T(8,128)}, f32[256,1024]{1,0:T(8,128)}, u32[]{:S(2)}, u32[]{:S(2)}) collective-permute-start(f32[256,1024]{1,0:T(8,128)} %pad_maximum_fusion.1.refs_5_), channel_id=1, source_target_pairs={{0,1},{1,0},{2,3},{3,2},{4,5},{5,4},{6,7},{7,6},{8,9},{9,8},{10,11... | collective-permute-start | bytes 3145736 | tf_op jit(solution)/shard_map/ppermute | solution.py:26
  41.7 17.8 %collective-permute-start.6 = (f32[128,2048]{1,0:T(8,128)S(1)}, f32[128,2048]{1,0:T(8,128)S(1)}, u32[]{:S(2)}, u32[]{:S(2)}) collective-permute-start(f32[128,2048]{1,0:T(8,128)S(1)} %collective-permute-done.5.refs_1_), channel_id=1, source_target_pairs={{0,16},{16,0},{32,48},{48,32},{64,80},{80,64},{96,112},{112,96},{1... | collective-permute-start | bytes 3145736 | tf_op jit(solution)/shard_map/ppermute | solution.py:39
  107.3 10.8 %collective-permute-start.15 = (f32[8,136,128]{2,1,0:T(8,128)S(1)}, f32[8,136,128]{2,1,0:T(8,128)S(1)}, u32[]{:S(2)}, u32[]{:S(2)}) collective-permute-start(f32[8,136,128]{2,1,0:T(8,128)S(1)} %shard_map.93), channel_id=1, source_target_pairs={{0,3},{1,2},{2,1},{3,0},{4,7},{5,6},{6,5},{7,4},{8,11},{9,10},{10,... | collective-permute-start | bytes 1671176 | tf_op jit(solution)/shard_map/ppermute | solution.py:26
  109.5 10.6 %collective-permute-start.19 = (f32[8,128,128]{2,1,0:T(8,128)S(1)}, f32[8,128,128]{2,1,0:T(8,128)S(1)}, u32[]{:S(2)}, u32[]{:S(2)}) collective-permute-start(f32[8,128,128]{2,1,0:T(8,128)S(1)} %shard_map.94), channel_id=1, source_target_pairs={{0,1},{1,0},{2,3},{3,2},{4,5},{5,4},{6,7},{7,6},{8,9},{9,8},{10,11... | collective-permute-start | bytes 1572872 | tf_op jit(solution)/shard_map/ppermute | solution.py:26
  110.9 12.8 %collective-permute-start.18 = (f32[8,128,128]{2,1,0:T(8,128)S(1)}, f32[8,128,128]{2,1,0:T(8,128)S(1)}, u32[]{:S(2)}, u32[]{:S(2)}) collective-permute-start(f32[8,128,128]{2,1,0:T(8,128)S(1)} %shard_map.95), channel_id=1, source_target_pairs={{0,3},{1,2},{2,1},{3,0},{4,7},{5,6},{6,5},{7,4},{8,11},{9,10},{10,... | collective-permute-start | bytes 1572872 | tf_op jit(solution)/shard_map/ppermute | solution.py:26
  113.9 10.7 %collective-permute-start.17 = (f32[8,128,128]{2,1,0:T(8,128)S(1)}, f32[8,128,128]{2,1,0:T(8,128)S(1)}, u32[]{:S(2)}, u32[]{:S(2)}) collective-permute-start(f32[8,128,128]{2,1,0:T(8,128)S(1)} %shard_map.96), channel_id=1, source_target_pairs={{0,1},{1,0},{2,3},{3,2},{4,5},{5,4},{6,7},{7,6},{8,9},{9,8},{10,11... | collective-permute-start | bytes 1572872 | tf_op jit(solution)/shard_map/ppermute | solution.py:26
  118.2 9.4 %collective-permute-start.16 = (f32[4,136,128]{2,1,0:T(8,128)S(1)}, f32[4,136,128]{2,1,0:T(8,128)S(1)}, u32[]{:S(2)}, u32[]{:S(2)}) collective-permute-start(f32[4,136,128]{2,1,0:T(8,128)S(1)} %slice.73), channel_id=1, source_target_pairs={{0,1},{1,0},{2,3},{3,2},{4,5},{5,4},{6,7},{7,6},{8,9},{9,8},{10,11... | collective-permute-start | bytes 835592 | tf_op jit(solution)/shard_map/ppermute | solution.py:26
  120.2 7.7 %collective-permute-start.21 = (f32[4,128,128]{2,1,0:T(8,128)S(1)}, f32[4,128,128]{2,1,0:T(8,128)S(1)}, u32[]{:S(2)}, u32[]{:S(2)}) collective-permute-start(f32[4,128,128]{2,1,0:T(8,128)S(1)} %slice.77), channel_id=1, source_target_pairs={{0,3},{1,2},{2,1},{3,0},{4,7},{5,6},{6,5},{7,4},{8,11},{9,10},{10,... | collective-permute-start | bytes 786440 | tf_op jit(solution)/shard_map/ppermute | solution.py:26
  124.6 6.4 %collective-permute-start.20 = (f32[4,128,128]{2,1,0:T(8,128)S(1)}, f32[4,128,128]{2,1,0:T(8,128)S(1)}, u32[]{:S(2)}, u32[]{:S(2)}) collective-permute-start(f32[4,128,128]{2,1,0:T(8,128)S(1)} %slice.75), channel_id=1, source_target_pairs={{0,1},{1,0},{2,3},{3,2},{4,5},{5,4},{6,7},{7,6},{8,9},{9,8},{10,11... | collective-permute-start | bytes 786440 | tf_op jit(solution)/shard_map/ppermute | solution.py:26
  124.8 7.7 %collective-permute-start.23 = (f32[4,128,128]{2,1,0:T(8,128)S(1)}, f32[4,128,128]{2,1,0:T(8,128)S(1)}, u32[]{:S(2)}, u32[]{:S(2)}) collective-permute-start(f32[4,128,128]{2,1,0:T(8,128)S(1)} %slice.81), channel_id=1, source_target_pairs={{0,3},{1,2},{2,1},{3,0},{4,7},{5,6},{6,5},{7,4},{8,11},{9,10},{10,... | collective-permute-start | bytes 786440 | tf_op jit(solution)/shard_map/ppermute | solution.py:26
  132.5 7.7 %collective-permute-start.22 = (f32[2,264,128]{2,1,0:T(8,128)S(1)}, f32[2,264,128]{2,1,0:T(8,128)S(1)}, u32[]{:S(2)}, u32[]{:S(2)}) collective-permute-start(f32[2,264,128]{2,1,0:T(8,128)S(1)} %pad_maximum_fusion.4), channel_id=1, source_target_pairs={{0,12},{1,13},{2,14},{3,15},{4,8},{5,9},{6,10},{7,11},{8,4},{9,5},... | collective-permute-start | bytes 811016 | tf_op jit(solution)/shard_map/ppermute | solution.py:26
  133.7 6.5 %collective-permute-start.25 = (f32[2,256,128]{2,1,0:T(8,128)S(1)}, f32[2,256,128]{2,1,0:T(8,128)S(1)}, u32[]{:S(2)}, u32[]{:S(2)}) collective-permute-start(f32[2,256,128]{2,1,0:T(8,128)S(1)} %pad_maximum_fusion.5), channel_id=1, source_target_pairs={{0,4},{1,5},{2,6},{3,7},{4,0},{5,1},{6,2},{7,3},{8,12},{9,13},{10,... | collective-permute-start | bytes 786440 | tf_op jit(solution)/shard_map/ppermute | solution.py:26
  (12 other events, 166.6 us)

commit v4 on v3

--- a/solution.py
+++ b/solution.py
@@ -14,7 +14,7 @@
 ROWS, COLS = 512, 1024
 BF, F32 = jnp.bfloat16, jnp.float32
 
-UA, UB, VA, VB = (1, 4), (3, 12), (4, 1), (12, 3)
+UA, UB, VA, VB, VC = (1, 4), (3, 12), (4, 1), (12, 3), (8, 2)
 FIRST, SECOND = (VA, VB, UA, UB), (VB, VA, UB, UA)
 ZA, ZB = (1, 3), (3, 1)
 
@@ -142,8 +142,8 @@
     return lax.dot_general(one, two, (((1,), (1,)), ((), ())), preferred_element_type=F32)
 
 
-def group(k, pieces, high, low, norm):
-    for at, ref in ((0, pieces[2 * k]), (128, pieces[2 * k + 1])):
+def group(k, pair, high, low, norm):
+    for at, ref in ((0, pair[0]), (128, pair[1])):
         for p in range(4):
             rows = slice(256 * k + at + 32 * p, 256 * k + at + 32 * p + 32)
             value = ref[32 * p : 32 * p + 32, :]
@@ -168,10 +168,16 @@
 
 
 def data_body(*refs):
-    pieces, norms, (dh, dl), (high, low, outs) = refs[:6], refs[6], refs[7:9], refs[9:]
+    data, norms, (dh, dl), (pieces, high, low, sems, outs) = refs[:6], refs[6], refs[7:9], refs[9:]
+    copies = [pltpu.make_async_copy(ref, pieces.at[i], sems.at[i]) for i, ref in enumerate(data)]
+    for copy in copies:
+        copy.start()
     sent = []
     for k in range(3):
-        group(k, pieces, high, low, norms.at[256 * k : 256 * k + 256, :])
+        copies[2 * k].wait()
+        copies[2 * k + 1].wait()
+        both = [pieces.at[2 * k + i] for i in range(2)]
+        group(k, both, high, low, norms.at[256 * k : 256 * k + 256, :])
         rows = slice(256 * k, 256 * k + 256)
         for i, (source, target) in enumerate(((high, dh), (low, dl))):
             sent.append(
@@ -357,19 +363,22 @@
                 out[i, 128:136, :] = jnp.broadcast_to(row, (8, 128))
 
 
-def end_body(left, right, noise, times, path, velocity):
+def end_body(one, two, three, four, noise, times, path, velocity):
     eye = diagonal()[:32, :]
-    wide = jnp.broadcast_to(left[0, 128:129, :], (32, 128))
+
+    def total(rows):
+        return (one[rows, :] + two[rows, :]) + (three[rows, :] + four[rows, :])
+
+    wide = jnp.broadcast_to(total(slice(128, 136))[:1, :], (32, 128))
     inverse = 1.0 / jnp.sum(jnp.where(eye, wide, 0.0), axis=1, keepdims=True)
-    for side, (ref, starts) in enumerate(((left, (0, 136)), (right, (0, 128)))):
-        for t in range(8):
-            lanes = slice(1024 * side + 128 * t, 1024 * side + 128 * t + 128)
-            first = starts[t // 4] + 32 * (t % 4)
-            target = ref[0, first : first + 32, :] * inverse
-            own = noise[:, lanes]
-            at = times[:, :1]
-            path[:, lanes] = (1.0 - at) * own + at * target
-            velocity[:, lanes] = target - own
+    for t in range(16):
+        lanes = slice(128 * t, 128 * t + 128)
+        first = 32 * t + (0 if t < 4 else 8)
+        target = total(slice(first, first + 32)) * inverse
+        own = noise[:, lanes]
+        at = times[:, :1]
+        path[:, lanes] = (1.0 - at) * own + at * target
+        velocity[:, lanes] = target - own
 
 
 def after(*values):
@@ -416,13 +425,15 @@
     norms, h0, l0 = call(
         data_body,
         (shape((768, 128)),) + (shape((768, features), BF),) * 2,
-        arrays=6,
         scratch=(
+            pltpu.VMEM((6, 128, features), F32),
             pltpu.VMEM((768, features), BF),
             pltpu.VMEM((768, features), BF),
             pltpu.SemaphoreType.DMA((6,)),
+            pltpu.SemaphoreType.DMA((6,)),
         ),
         moved=12 * 2**20,
+        far=6,
         far_out=2,
     )(own[0], cross[0], own[1], cross[1], own[2], cross[2])
     rows, row_norms, early, peaks, totals = call(
@@ -512,17 +523,16 @@
         leaving[chunk] = swap_col(last[4:], steps[1])
     for chunk, steps in order:
         sums[chunk] = last = sums[chunk][:4] + after(leaving[chunk], last)[0]
-    ends = [
-        jnp.concatenate([sums[chunk] for chunk in chunks], axis=1) for _, chunks, _ in halves
-    ]
-    for step, rows in ((2, 2), (3, 1)):
-        coming = [swap_col(end[rows:], half[2][step]) for end, half in zip(ends, halves)]
-        for i in range(2):
-            ends[i] = last = ends[i][:rows] + after(coming[i], last)[0]
-    left, right = ends
+    places = {(0, 0): (0, 0), VA: (1, 2), VB: (2, 1), VC: (3, 3)}
+
+    def piece(masks):
+        at = places[masks]
+        return jnp.concatenate([sums[chunk][at[chunk // 2]] for chunk in range(4)], axis=0)
+
+    parts = [piece((0, 0))] + [swap_col(piece(masks), masks) for masks in (VC, VA, VB)]
     wide_times = jnp.broadcast_to(times[:, None], (times.shape[0], 128))
     outs = (shape(noise.shape), shape(noise.shape))
-    return call(end_body, outs, 0, 4)(left, right, noise, wide_times)
+    return call(end_body, outs, 0, 6)(*parts, noise, wide_times)
 
 
 def solution(mesh):

time: 148 us -> 146 us (0.986)
  waiting for transfers between devices: 37.9 us -> 35.6 us
  starting transfers between devices: 34.1 us -> 35.7 us
    ppermute x20 -> x19, waiting for transfers between devices: 33.3 us -> 31 us  [swap_col(): return lax.ppermute(value, BOTH, pairs)]
    ppermute x20 -> x19, starting transfers between devices: 27.8 us -> 29.4 us  [swap_col(): return lax.ppermute(value, BOTH, pairs)]
  transfers between devices with their start and end apart: 27 -> 26, of which waited for: 16 -> 16; matrix products, arithmetic and copies ran while one was open for 2% -> 2% of each run, Pallas kernels for 13% -> 12%
where the time goes in v4:
time: 146 us
  blocking collectives  39.3 us (27%)
  starting transfers between devices  35.7 us (24%)
  waiting for transfers between devices  35.6 us (24%)
  Pallas kernels  27.7 us (19%)
  local copies, waits for them, and re-layouts  4.73 us (3%)
  other arithmetic  1.76 us (1%)
    ppermute x19, waiting for transfers between devices, swap_col(): return lax.ppermute(value, BOTH, pairs)  31 us
    ppermute x19, starting transfers between devices, swap_col(): return lax.ppermute(value, BOTH, pairs)  29.4 us
    all_to_all x2, blocking collectives, per_device(): got = lax.all_to_all(send, 'col', 0, 0)  22.6 us
    all_to_all x2, blocking collectives, per_device(): got = lax.all_to_all(send, 'row', 0, 0)  16.7 us
    pallas_call x1, Pallas kernels, per_device(): call(lambda *refs: early_body(scale, *refs), (shape((2 * ROWS, features),...  8.6 us
    pallas_call x6, Pallas kernels, product(): call(lambda *refs: product_body(blocks, chunks, *refs), tuple((shape((8,...  7.52 us
    ppermute x3, starting transfers between devices, swap_z(): return lax.ppermute(value, BOTH, pairs)  5.79 us
    ppermute x3, waiting for transfers between devices, swap_z(): return lax.ppermute(value, BOTH, pairs)  4.59 us
  transfers between devices with their start and end apart: 26, of which 16 were waited for; matrix products, arithmetic and copies ran while one was open for 2% of the time, Pallas kernels for 12%

profile of v4, /device:TPU:0, one launch (start us, length us, event | category | flops | bytes accessed | tf_op | source)
XLA Modules:
  0.0 145.7 jit_solution(5566799834176732103)
XLA Ops:
  0.6 2.1 %collective-permute-start = (f32[128,2048]{1,0:T(8,128)}, f32[128,2048]{1,0:T(8,128)}, u32[]{:S(2)}, u32[]{:S(2)}) collective-permute-start(f32[128,2048]{1,0:T(8,128)} %refs_0_.1), channel_id=1, source_target_pairs={{0,32},{1,33},{2,34},{3,35},{4,36},{5,37},{6,38},{7,39},{8,40},{9,... | collective-permute-start | bytes 3145736 | tf_op jit(solution)/shard_map/ppermute | solution.py:35
  5.4 2.2 %collective-permute-start.3 = (f32[32,1024]{1,0:T(8,128)S(1)}, f32[32,1024]{1,0:T(8,128)S(1)}, u32[]{:S(2)}, u32[]{:S(2)}) collective-permute-start(f32[32,1024]{1,0:T(8,128)S(1)} %get-tuple-element.160), channel_id=1, source_target_pairs={{0,12},{1,13},{2,14},{3,15},{4,8},{5,9},{6,10},{7,11},{8,4},{9,5},... | collective-permute-start | bytes 393224 | tf_op jit(solution)/shard_map/ppermute | solution.py:26
  8.8 3.1 %collective-permute-start.2 = (f32[64,1024]{1,0:T(8,128)S(1)}, f32[64,1024]{1,0:T(8,128)S(1)}, u32[]{:S(2)}, u32[]{:S(2)}) collective-permute-start(f32[64,1024]{1,0:T(8,128)S(1)} %pad_maximum_fusion.8), channel_id=1, source_target_pairs={{0,12},{1,13},{2,14},{3,15},{4,8},{5,9},{6,10},{7,11},{8,4},{9,5},... | collective-permute-start | bytes 786440 | tf_op jit(solution)/shard_map/ppermute | solution.py:26
  11.9 2.5 %collective-permute-start.9 = (f32[128,2048]{1,0:T(8,128)}, f32[128,2048]{1,0:T(8,128)}, u32[]{:S(2)}, u32[]{:S(2)}) collective-permute-start(f32[128,2048]{1,0:T(8,128)} %refs_0_.1), channel_id=1, source_target_pairs={{0,96},{1,97},{2,98},{3,99},{4,100},{5,101},{6,102},{7,103},{8,104... | collective-permute-start | bytes 3145736 | tf_op jit(solution)/shard_map/ppermute | solution.py:35
  18.0 4.5 %collective-permute-done.4 = f32[64,1024]{1,0:T(8,128)S(1)} collective-permute-done((f32[64,1024]{1,0:T(8,128)S(1)}, f32[64,1024]{1,0:T(8,128)S(1)}, u32[]{:S(2)}, u32[]{:S(2)}) %collective-permute-start.4) | collective-permute-done | bytes 262176 | tf_op jit(solution)/shard_map/ppermute | solution.py:26
  22.6 2.8 %collective-permute-start.13 = (f32[128,1024]{1,0:T(8,128)S(1)}, f32[128,1024]{1,0:T(8,128)S(1)}, u32[]{:S(2)}, u32[]{:S(2)}) collective-permute-start(f32[128,1024]{1,0:T(8,128)S(1)} %pad_maximum_fusion.3), channel_id=1, source_target_pairs={{0,3},{1,2},{2,1},{3,0},{4,7},{5,6},{6,5},{7,4},{8,11},{9,10},{10,... | collective-permute-start | bytes 1572872 | tf_op jit(solution)/shard_map/ppermute | solution.py:26
  26.8 2.8 %collective-permute-start.12 = (f32[256,1024]{1,0:T(8,128)S(1)}, f32[256,1024]{1,0:T(8,128)}, u32[]{:S(2)}, u32[]{:S(2)}) collective-permute-start(f32[256,1024]{1,0:T(8,128)S(1)} %pad_maximum_fusion.refs_3_), channel_id=1, source_target_pairs={{0,3},{1,2},{2,1},{3,0},{4,7},{5,6},{6,5},{7,4},{8,11},{9,10},{10,... | collective-permute-start | bytes 3145736 | tf_op jit(solution)/shard_map/ppermute | solution.py:26
  29.6 3.5 %collective-permute-done.13 = f32[128,1024]{1,0:T(8,128)S(1)} collective-permute-done((f32[128,1024]{1,0:T(8,128)S(1)}, f32[128,1024]{1,0:T(8,128)S(1)}, u32[]{:S(2)}, u32[]{:S(2)}) %collective-permute-start.13) | collective-permute-done | bytes 524320 | tf_op jit(solution)/shard_map/ppermute | solution.py:26
  37.1 4.6 %collective-permute-done.5.refs_1_ = f32[128,2048]{1,0:T(8,128)S(1)} collective-permute-done((f32[128,2048]{1,0:T(8,128)}, f32[128,2048]{1,0:T(8,128)S(1)}, u32[]{:S(2)}, u32[]{:S(2)}) %collective-permute-start.5) | collective-permute-done | bytes 1048608 | tf_op jit(solution)/shard_map/ppermute | solution.py:35
  44.2 3.1 %shard_map.86 = (f32[768,128]{1,0:T(8,128)S(1)}, bf16[768,2048]{1,0:T(8,128)(2,1)S(1)}, bf16[768,2048]{1,0:T(8,128)(2,1)S(1)}) custom-call(f32[128,2048]{1,0:T(8,128)S(1)} %copy-done.1, f32[128,2048]{1,0:T(8,128)S(1)} %copy-done.3, f32[128,2048]{1,0:T(8,128)} %collective-permute-done.refs_2_, f32[128,2048]{1,0:T(8,128)} %collective-permute-done.8.refs_3_, ...), custom_call_target="tpu_custom_call" | custom-call | bytes 12582912 | tf_op jit(solution)/shard_map/pallas_call | solution.py:425
  47.3 3.5 %collective-permute-done.14.refs_6_ = f32[256,1024]{1,0:T(8,128)} collective-permute-done((f32[256,1024]{1,0:T(8,128)}, f32[256,1024]{1,0:T(8,128)}, u32[]{:S(2)}, u32[]{:S(2)}) %collective-permute-start.14) | collective-permute-done | bytes 1048608 | tf_op jit(solution)/shard_map/ppermute | solution.py:26
  50.8 8.6 %shard_map.87 = (bf16[1024,2048]{1,0:T(8,128)(2,1)S(1)}, f32[512,128]{1,0:T(8,128)S(1)}, f32[512,768]{1,0:T(8,128)S(1)}, f32[512,128]{1,0:T(8,128)S(1)}, f32[512,128]{1,0:T(8,128)S(1)}) custom-call(bf16[768,2048]{1,0:T(8,128)(2,1)S(1)} %get-tuple-element.120.refs_0_.refs_3_, bf16[768,2048]{1,0:T(8,128)(2,1)S(1)} %get-tuple-element.121.refs_1_.refs_4_, ...), custom_call_target="tpu_custom_call" | custom-call | flops 4831838208 | bytes 16777216 | tf_op jit(solution)/shard_map/pallas_call | solution.py:439
  59.4 3.3 %shard_map.88 = (f32[512,256]{1,0:T(8,128)S(1)}, f32[16,8,128]{2,1,0:T(8,128)S(1)}, bf16[256,2048]{1,0:T(8,128)(2,1)S(1)}, bf16[256,2048]{1,0:T(8,128)(2,1)S(1)}) custom-call(s32[16]{0:T(128)S(1)} %fusion.refs_0_.rplaces, f32[128,2048]{1,0:T(8,128)S(1)} %collective-permute-done.5.refs_1_, f32[128,2048]{1,0:T(8,128)S(1)} %collective-permute-done.6.refs_2_, ...), custom_call_target="tpu_custom_call" | custom-call | flops 1610612736 | bytes 8388608 | tf_op jit(solution)/shard_map/pallas_call | solution.py:454
  62.8 11.8 %all_to_all.20.got = f32[16,8,128]{2,1,0:T(8,128)S(1)} all-to-all(f32[16,8,128]{2,1,0:T(8,128)S(1)} %get-tuple-element.84), channel_id=1, replica_groups=mesh['row'=8,'col'=16] {'col'}, dimensions={0} | all-to-all | bytes 131072 | tf_op jit(solution)/shard_map/all_to_all | solution.py:472
  75.9 8.9 %all_to_all.21.got = f32[8,16,128]{2,1,0:T(8,128)S(1)} all-to-all(f32[8,16,128]{2,1,0:T(8,128)S(1)} %get-tuple-element.87), channel_id=1, replica_groups=mesh['row'=8,'col'=16] {'row'}, dimensions={0} | all-to-all | bytes 131072 | tf_op jit(solution)/shard_map/all_to_all | solution.py:480
  85.6 10.8 %all_to_all.22.got = f32[16,8,128]{2,1,0:T(8,128)S(1)} all-to-all(f32[16,8,128]{2,1,0:T(8,128)S(1)} %get-tuple-element.89), channel_id=1, replica_groups=mesh['row'=8,'col'=16] {'col'}, dimensions={0} | all-to-all | bytes 131072 | tf_op jit(solution)/shard_map/all_to_all | solution.py:488
  97.4 7.8 %all_to_all.23.got = f32[8,8,128]{2,1,0:T(8,128)S(1)} all-to-all(f32[8,8,128]{2,1,0:T(8,128)S(1)} %shard_map.91), channel_id=1, replica_groups=mesh['row'=8,'col'=16] {'row'}, dimensions={0} | all-to-all | bytes 65536 | tf_op jit(solution)/shard_map/all_to_all | solution.py:496
  110.9 2.1 %collective-permute-start.18 = (f32[8,128,128]{2,1,0:T(8,128)S(1)}, f32[8,128,128]{2,1,0:T(8,128)S(1)}, u32[]{:S(2)}, u32[]{:S(2)}) collective-permute-start(f32[8,128,128]{2,1,0:T(8,128)S(1)} %shard_map.95), channel_id=1, source_target_pairs={{0,3},{1,2},{2,1},{3,0},{4,7},{5,6},{6,5},{7,4},{8,11},{9,10},{10,... | collective-permute-start | bytes 1572872 | tf_op jit(solution)/shard_map/ppermute | solution.py:26
  121.4 2.3 %collective-permute-done.18 = f32[8,128,128]{2,1,0:T(8,128)S(1)} collective-permute-done((f32[8,128,128]{2,1,0:T(8,128)S(1)}, f32[8,128,128]{2,1,0:T(8,128)S(1)}, u32[]{:S(2)}, u32[]{:S(2)}) %collective-permute-start.18) | collective-permute-done | bytes 524320 | tf_op jit(solution)/shard_map/ppermute | solution.py:26
  124.8 2.1 %collective-permute-start.22 = (f32[4,128,128]{2,1,0:T(8,128)S(1)}, f32[4,128,128]{2,1,0:T(8,128)S(1)}, u32[]{:S(2)}, u32[]{:S(2)}) collective-permute-start(f32[4,128,128]{2,1,0:T(8,128)S(1)} %slice.114), channel_id=1, source_target_pairs={{0,3},{1,2},{2,1},{3,0},{4,7},{5,6},{6,5},{7,4},{8,11},{9,10},{10,... | collective-permute-start | bytes 786440 | tf_op jit(solution)/shard_map/ppermute | solution.py:26
  127.9 3.1 %collective-permute-done.20 = f32[4,128,128]{2,1,0:T(8,128)S(1)} collective-permute-done((f32[4,128,128]{2,1,0:T(8,128)S(1)}, f32[4,128,128]{2,1,0:T(8,128)S(1)}, u32[]{:S(2)}, u32[]{:S(2)}) %collective-permute-start.20) | collective-permute-done | bytes 262176 | tf_op jit(solution)/shard_map/ppermute | solution.py:26
  133.9 3.6 %collective-permute-start.23 = (f32[520,128]{1,0:T(8,128)S(1)}, f32[520,128]{1,0:T(8,128)S(1)}, u32[]{:S(2)}, u32[]{:S(2)}) collective-permute-start(f32[520,128]{1,0:T(8,128)S(1)} %pad_maximum_fusion.5), channel_id=1, source_target_pairs={{0,8},{1,9},{2,10},{3,11},{4,12},{5,13},{6,14},{7,15},{8,0},{9,1},... | collective-permute-start | bytes 798728 | tf_op jit(solution)/shard_map/ppermute | solution.py:26
  137.6 2.7 %collective-permute-done.25.four = f32[520,128]{1,0:T(8,128)S(1)} collective-permute-done((f32[520,128]{1,0:T(8,128)S(1)}, f32[520,128]{1,0:T(8,128)S(1)}, u32[]{:S(2)}, u32[]{:S(2)}) %collective-permute-start.25) | collective-permute-done | bytes 266272 | tf_op jit(solution)/shard_map/ppermute | solution.py:26
  140.3 4.4 %collective-permute-done.23.two = f32[520,128]{1,0:T(8,128)S(1)} collective-permute-done((f32[520,128]{1,0:T(8,128)S(1)}, f32[520,128]{1,0:T(8,128)S(1)}, u32[]{:S(2)}, u32[]{:S(2)}) %collective-permute-start.23) | collective-permute-done | bytes 266272 | tf_op jit(solution)/shard_map/ppermute | solution.py:26
  (93 shorter events, 38.6 us)
Async XLA Ops:
  0.6 24.8 %collective-permute-start = (f32[128,2048]{1,0:T(8,128)}, f32[128,2048]{1,0:T(8,128)}, u32[]{:S(2)}, u32[]{:S(2)}) collective-permute-start(f32[128,2048]{1,0:T(8,128)} %refs_0_.1), channel_id=1, source_target_pairs={{0,32},{1,33},{2,34},{3,35},{4,36},{5,37},{6,38},{7,39},{8,40},{9,... | collective-permute-start | bytes 3145736 | tf_op jit(solution)/shard_map/ppermute | solution.py:35
  5.4 9.0 %collective-permute-start.3 = (f32[32,1024]{1,0:T(8,128)S(1)}, f32[32,1024]{1,0:T(8,128)S(1)}, u32[]{:S(2)}, u32[]{:S(2)}) collective-permute-start(f32[32,1024]{1,0:T(8,128)S(1)} %get-tuple-element.160), channel_id=1, source_target_pairs={{0,12},{1,13},{2,14},{3,15},{4,8},{5,9},{6,10},{7,11},{8,4},{9,5},... | collective-permute-start | bytes 393224 | tf_op jit(solution)/shard_map/ppermute | solution.py:26
  8.8 7.7 %collective-permute-start.2 = (f32[64,1024]{1,0:T(8,128)S(1)}, f32[64,1024]{1,0:T(8,128)S(1)}, u32[]{:S(2)}, u32[]{:S(2)}) collective-permute-start(f32[64,1024]{1,0:T(8,128)S(1)} %pad_maximum_fusion.8), channel_id=1, source_target_pairs={{0,12},{1,13},{2,14},{3,15},{4,8},{5,9},{6,10},{7,11},{8,4},{9,5},... | collective-permute-start | bytes 786440 | tf_op jit(solution)/shard_map/ppermute | solution.py:26
  11.9 21.2 %collective-permute-start.9 = (f32[128,2048]{1,0:T(8,128)}, f32[128,2048]{1,0:T(8,128)}, u32[]{:S(2)}, u32[]{:S(2)}) collective-permute-start(f32[128,2048]{1,0:T(8,128)} %refs_0_.1), channel_id=1, source_target_pairs={{0,96},{1,97},{2,98},{3,99},{4,100},{5,101},{6,102},{7,103},{8,104... | collective-permute-start | bytes 3145736 | tf_op jit(solution)/shard_map/ppermute | solution.py:35
  14.5 8.1 %collective-permute-start.4 = (f32[64,1024]{1,0:T(8,128)S(1)}, f32[64,1024]{1,0:T(8,128)S(1)}, u32[]{:S(2)}, u32[]{:S(2)}) collective-permute-start(f32[64,1024]{1,0:T(8,128)S(1)} %pad_maximum_fusion.9), channel_id=1, source_target_pairs={{0,4},{1,5},{2,6},{3,7},{4,0},{5,1},{6,2},{7,3},{8,12},{9,13},{10,... | collective-permute-start | bytes 786440 | tf_op jit(solution)/shard_map/ppermute | solution.py:26
  14.7 20.0 %collective-permute-start.7 = (f32[128,2048]{1,0:T(8,128)}, f32[128,2048]{1,0:T(8,128)S(1)}, u32[]{:S(2)}, u32[]{:S(2)}) collective-permute-start(f32[128,2048]{1,0:T(8,128)} %refs_0_.1), channel_id=1, source_target_pairs={{0,16},{16,0},{32,48},{48,32},{64,80},{80,64},{96,112},{112,96},{1... | collective-permute-start | bytes 3145736 | tf_op jit(solution)/shard_map/ppermute | solution.py:39
  16.5 10.2 %collective-permute-start.11 = (f32[128,1024]{1,0:T(8,128)S(1)}, f32[128,1024]{1,0:T(8,128)S(1)}, u32[]{:S(2)}, u32[]{:S(2)}) collective-permute-start(f32[128,1024]{1,0:T(8,128)S(1)} %pad_maximum_fusion.2), channel_id=1, source_target_pairs={{0,1},{1,0},{2,3},{3,2},{4,5},{5,4},{6,7},{7,6},{8,9},{9,8},{10,11... | collective-permute-start | bytes 1572872 | tf_op jit(solution)/shard_map/ppermute | solution.py:26
  22.6 10.5 %collective-permute-start.13 = (f32[128,1024]{1,0:T(8,128)S(1)}, f32[128,1024]{1,0:T(8,128)S(1)}, u32[]{:S(2)}, u32[]{:S(2)}) collective-permute-start(f32[128,1024]{1,0:T(8,128)S(1)} %pad_maximum_fusion.3), channel_id=1, source_target_pairs={{0,3},{1,2},{2,1},{3,0},{4,7},{5,6},{6,5},{7,4},{8,11},{9,10},{10,... | collective-permute-start | bytes 1572872 | tf_op jit(solution)/shard_map/ppermute | solution.py:26
  25.5 16.2 %collective-permute-start.5 = (f32[128,2048]{1,0:T(8,128)}, f32[128,2048]{1,0:T(8,128)S(1)}, u32[]{:S(2)}, u32[]{:S(2)}) collective-permute-start(f32[128,2048]{1,0:T(8,128)} %collective-permute-done.refs_2_), channel_id=1, source_target_pairs={{0,96},{1,97},{2,98},{3,99},{4,100},{5,101},{6,102},{7,103},{8,104... | collective-permute-start | bytes 3145736 | tf_op jit(solution)/shard_map/ppermute | solution.py:35
  26.8 20.5 %collective-permute-start.12 = (f32[256,1024]{1,0:T(8,128)S(1)}, f32[256,1024]{1,0:T(8,128)}, u32[]{:S(2)}, u32[]{:S(2)}) collective-permute-start(f32[256,1024]{1,0:T(8,128)S(1)} %pad_maximum_fusion.refs_3_), channel_id=1, source_target_pairs={{0,3},{1,2},{2,1},{3,0},{4,7},{5,6},{6,5},{7,4},{8,11},{9,10},{10,... | collective-permute-start | bytes 3145736 | tf_op jit(solution)/shard_map/ppermute | solution.py:26
  33.1 8.7 %collective-permute-start.8 = (f32[128,2048]{1,0:T(8,128)}, f32[128,2048]{1,0:T(8,128)}, u32[]{:S(2)}, u32[]{:S(2)}) collective-permute-start(f32[128,2048]{1,0:T(8,128)} %collective-permute-done.refs_2_), channel_id=1, source_target_pairs={{0,16},{16,0},{32,48},{48,32},{64,80},{80,64},{96,112},{112,96},{1... | collective-permute-start | bytes 3145736 | tf_op jit(solution)/shard_map/ppermute | solution.py:39
  33.1 8.7 %collective-permute-start.10 = (f32[128,2048]{1,0:T(8,128)}, f32[128,2048]{1,0:T(8,128)}, u32[]{:S(2)}, u32[]{:S(2)}) collective-permute-start(f32[128,2048]{1,0:T(8,128)} %collective-permute-done.9.refs_4_), channel_id=1, source_target_pairs={{0,16},{16,0},{32,48},{48,32},{64,80},{80,64},{96,112},{112,96},{1... | collective-permute-start | bytes 3145736 | tf_op jit(solution)/shard_map/ppermute | solution.py:39
  35.7 15.1 %collective-permute-start.14 = (f32[256,1024]{1,0:T(8,128)}, f32[256,1024]{1,0:T(8,128)}, u32[]{:S(2)}, u32[]{:S(2)}) collective-permute-start(f32[256,1024]{1,0:T(8,128)} %pad_maximum_fusion.1.refs_5_), channel_id=1, source_target_pairs={{0,1},{1,0},{2,3},{3,2},{4,5},{5,4},{6,7},{7,6},{8,9},{9,8},{10,11... | collective-permute-start | bytes 3145736 | tf_op jit(solution)/shard_map/ppermute | solution.py:26
  41.7 17.7 %collective-permute-start.6 = (f32[128,2048]{1,0:T(8,128)S(1)}, f32[128,2048]{1,0:T(8,128)S(1)}, u32[]{:S(2)}, u32[]{:S(2)}) collective-permute-start(f32[128,2048]{1,0:T(8,128)S(1)} %collective-permute-done.5.refs_1_), channel_id=1, source_target_pairs={{0,16},{16,0},{32,48},{48,32},{64,80},{80,64},{96,112},{112,96},{1... | collective-permute-start | bytes 3145736 | tf_op jit(solution)/shard_map/ppermute | solution.py:39
  107.3 10.8 %collective-permute-start.15 = (f32[8,136,128]{2,1,0:T(8,128)S(1)}, f32[8,136,128]{2,1,0:T(8,128)S(1)}, u32[]{:S(2)}, u32[]{:S(2)}) collective-permute-start(f32[8,136,128]{2,1,0:T(8,128)S(1)} %shard_map.93), channel_id=1, source_target_pairs={{0,3},{1,2},{2,1},{3,0},{4,7},{5,6},{6,5},{7,4},{8,11},{9,10},{10,... | collective-permute-start | bytes 1671176 | tf_op jit(solution)/shard_map/ppermute | solution.py:26
  109.5 10.6 %collective-permute-start.19 = (f32[8,128,128]{2,1,0:T(8,128)S(1)}, f32[8,128,128]{2,1,0:T(8,128)S(1)}, u32[]{:S(2)}, u32[]{:S(2)}) collective-permute-start(f32[8,128,128]{2,1,0:T(8,128)S(1)} %shard_map.94), channel_id=1, source_target_pairs={{0,1},{1,0},{2,3},{3,2},{4,5},{5,4},{6,7},{7,6},{8,9},{9,8},{10,11... | collective-permute-start | bytes 1572872 | tf_op jit(solution)/shard_map/ppermute | solution.py:26
  110.9 12.8 %collective-permute-start.18 = (f32[8,128,128]{2,1,0:T(8,128)S(1)}, f32[8,128,128]{2,1,0:T(8,128)S(1)}, u32[]{:S(2)}, u32[]{:S(2)}) collective-permute-start(f32[8,128,128]{2,1,0:T(8,128)S(1)} %shard_map.95), channel_id=1, source_target_pairs={{0,3},{1,2},{2,1},{3,0},{4,7},{5,6},{6,5},{7,4},{8,11},{9,10},{10,... | collective-permute-start | bytes 1572872 | tf_op jit(solution)/shard_map/ppermute | solution.py:26
  113.9 10.7 %collective-permute-start.17 = (f32[8,128,128]{2,1,0:T(8,128)S(1)}, f32[8,128,128]{2,1,0:T(8,128)S(1)}, u32[]{:S(2)}, u32[]{:S(2)}) collective-permute-start(f32[8,128,128]{2,1,0:T(8,128)S(1)} %shard_map.96), channel_id=1, source_target_pairs={{0,1},{1,0},{2,3},{3,2},{4,5},{5,4},{6,7},{7,6},{8,9},{9,8},{10,11... | collective-permute-start | bytes 1572872 | tf_op jit(solution)/shard_map/ppermute | solution.py:26
  118.2 9.4 %collective-permute-start.16 = (f32[4,136,128]{2,1,0:T(8,128)S(1)}, f32[4,136,128]{2,1,0:T(8,128)S(1)}, u32[]{:S(2)}, u32[]{:S(2)}) collective-permute-start(f32[4,136,128]{2,1,0:T(8,128)S(1)} %slice.105), channel_id=1, source_target_pairs={{0,1},{1,0},{2,3},{3,2},{4,5},{5,4},{6,7},{7,6},{8,9},{9,8},{10,11... | collective-permute-start | bytes 835592 | tf_op jit(solution)/shard_map/ppermute | solution.py:26
  120.2 7.7 %collective-permute-start.21 = (f32[4,128,128]{2,1,0:T(8,128)S(1)}, f32[4,128,128]{2,1,0:T(8,128)S(1)}, u32[]{:S(2)}, u32[]{:S(2)}) collective-permute-start(f32[4,128,128]{2,1,0:T(8,128)S(1)} %slice.110), channel_id=1, source_target_pairs={{0,3},{1,2},{2,1},{3,0},{4,7},{5,6},{6,5},{7,4},{8,11},{9,10},{10,... | collective-permute-start | bytes 786440 | tf_op jit(solution)/shard_map/ppermute | solution.py:26
  124.8 7.7 %collective-permute-start.22 = (f32[4,128,128]{2,1,0:T(8,128)S(1)}, f32[4,128,128]{2,1,0:T(8,128)S(1)}, u32[]{:S(2)}, u32[]{:S(2)}) collective-permute-start(f32[4,128,128]{2,1,0:T(8,128)S(1)} %slice.114), channel_id=1, source_target_pairs={{0,3},{1,2},{2,1},{3,0},{4,7},{5,6},{6,5},{7,4},{8,11},{9,10},{10,... | collective-permute-start | bytes 786440 | tf_op jit(solution)/shard_map/ppermute | solution.py:26
  132.6 7.7 %collective-permute-start.25 = (f32[520,128]{1,0:T(8,128)S(1)}, f32[520,128]{1,0:T(8,128)S(1)}, u32[]{:S(2)}, u32[]{:S(2)}) collective-permute-start(f32[520,128]{1,0:T(8,128)S(1)} %pad_maximum_fusion.7), channel_id=1, source_target_pairs={{0,12},{1,13},{2,14},{3,15},{4,8},{5,9},{6,10},{7,11},{8,4},{9,5},... | collective-permute-start | bytes 798728 | tf_op jit(solution)/shard_map/ppermute | solution.py:26
  133.8 6.5 %collective-permute-start.24 = (f32[520,128]{1,0:T(8,128)S(1)}, f32[520,128]{1,0:T(8,128)S(1)}, u32[]{:S(2)}, u32[]{:S(2)}) collective-permute-start(f32[520,128]{1,0:T(8,128)S(1)} %pad_maximum_fusion.6), channel_id=1, source_target_pairs={{0,4},{1,5},{2,6},{3,7},{4,0},{5,1},{6,2},{7,3},{8,12},{9,13},{10,... | collective-permute-start | bytes 798728 | tf_op jit(solution)/shard_map/ppermute | solution.py:26
  133.9 10.7 %collective-permute-start.23 = (f32[520,128]{1,0:T(8,128)S(1)}, f32[520,128]{1,0:T(8,128)S(1)}, u32[]{:S(2)}, u32[]{:S(2)}) collective-permute-start(f32[520,128]{1,0:T(8,128)S(1)} %pad_maximum_fusion.5), channel_id=1, source_target_pairs={{0,8},{1,9},{2,10},{3,11},{4,12},{5,13},{6,14},{7,15},{8,0},{9,1},... | collective-permute-start | bytes 798728 | tf_op jit(solution)/shard_map/ppermute | solution.py:26
  (11 other events, 158.3 us)

commit v5 on v4

--- a/solution.py
+++ b/solution.py
@@ -152,7 +152,7 @@
             norm[at + 32 * p : at + 32 * p + 32, :] = jnp.broadcast_to(total, (32, 128))
 
 
-def score(k, scale, terms, nn, high, low, norm, out, lanes):
+def score(k, scale, terms, nn, high, low, norm, out, lanes, half):
     eye = diagonal()
     norms = jnp.concatenate(
         [
@@ -162,9 +162,10 @@
         axis=1,
     )
     cols = slice(256 * k, 256 * k + 256)
-    both = dot_t(terms[...], high[cols, :])
-    cross = both[:ROWS] + both[ROWS:] + dot_t(terms[:ROWS, :], low[cols, :])
-    out[:, lanes] = (2.0 * cross - nn[:, :1] - norms) * scale
+    rows = slice(256 * half, 256 * half + 256)
+    top, under = terms[rows, :], terms[ROWS + 256 * half : ROWS + 256 * half + 256, :]
+    cross = dot_t(top, high[cols, :]) + dot_t(under, high[cols, :]) + dot_t(top, low[cols, :])
+    out[rows, lanes] = (2.0 * cross - nn[rows, :1] - norms) * scale
 
 
 def data_body(*refs):
@@ -218,11 +219,12 @@
         nn[32 * p : 32 * p + 32, :] = jnp.broadcast_to(total, (32, 128))
     for copy in copies:
         copy.wait()
-    for k in range(3):
-        rows = slice(256 * k, 256 * k + 256)
-        score(k, scale, terms, nn, high, low, norms.at[rows, :], scores, rows)
-    for p in range(16):
-        peaks[block(p), :], totals[block(p), :] = row_sums(scores[block(p), :])
+    for half in range(2):
+        for k in range(3):
+            rows = slice(256 * k, 256 * k + 256)
+            score(k, scale, terms, nn, high, low, norms.at[rows, :], scores, rows, half)
+        for p in range(8 * half, 8 * half + 8):
+            peaks[block(p), :], totals[block(p), :] = row_sums(scores[block(p), :])
 
 
 def late_body(scale, places, own, sibling, terms, nn, peaks, totals, scores, out, dh, dl, *scratch):
@@ -234,15 +236,16 @@
     ]
     for copy in sent:
         copy.start()
-    score(0, scale, terms, nn, high, low, norm, scores, slice(0, 256))
-    for p in range(16):
-        peak, total = row_sums(scores[block(p), :])
-        before = peaks[block(p), :]
-        top = jnp.maximum(peak, before)
-        ends[place(places, p), :] = top
-        sums[place(places, p), :] = total * jnp.exp(peak - top) + totals[block(p), :] * jnp.exp(
-            before - top
-        )
+    for half in range(2):
+        score(0, scale, terms, nn, high, low, norm, scores, slice(0, 256), half)
+        for p in range(8 * half, 8 * half + 8):
+            peak, total = row_sums(scores[block(p), :])
+            before = peaks[block(p), :]
+            top = jnp.maximum(peak, before)
+            ends[place(places, p), :] = top
+            sums[place(places, p), :] = total * jnp.exp(peak - top) + totals[block(p), :] * jnp.exp(
+                before - top
+            )
     value = jnp.concatenate([compact(ends), compact(sums)], axis=0)
     for to in range(16):
         out[to] = value

time: 146 us -> 146 us (level)
  transfers between devices with their start and end apart: 26 -> 26, of which waited for: 16 -> 16; matrix products, arithmetic and copies ran while one was open for 2% -> 2% of each run, Pallas kernels for 12% -> 13%
where the time goes in v5:
time: 146 us
  blocking collectives  39.3 us (27%)
  waiting for transfers between devices  35.6 us (24%)
  starting transfers between devices  35.5 us (24%)
  Pallas kernels  27.7 us (19%)
  local copies, waits for them, and re-layouts  4.73 us (3%)
  other arithmetic  1.76 us (1%)
    ppermute x19, waiting for transfers between devices, swap_col(): return lax.ppermute(value, BOTH, pairs)  31 us
    ppermute x19, starting transfers between devices, swap_col(): return lax.ppermute(value, BOTH, pairs)  29.2 us
    all_to_all x2, blocking collectives, per_device(): got = lax.all_to_all(send, 'col', 0, 0)  22.6 us
    all_to_all x2, blocking collectives, per_device(): got = lax.all_to_all(send, 'row', 0, 0)  16.7 us
    pallas_call x1, Pallas kernels, per_device(): call(lambda *refs: early_body(scale, *refs), (shape((2 * ROWS, features),...  8.61 us
    pallas_call x6, Pallas kernels, product(): call(lambda *refs: product_body(blocks, chunks, *refs), tuple((shape((8,...  7.52 us
    ppermute x3, starting transfers between devices, swap_z(): return lax.ppermute(value, BOTH, pairs)  5.79 us
    ppermute x3, waiting for transfers between devices, swap_z(): return lax.ppermute(value, BOTH, pairs)  4.59 us
  transfers between devices with their start and end apart: 26, of which 16 were waited for; matrix products, arithmetic and copies ran while one was open for 2% of the time, Pallas kernels for 13%

profile of v5, /device:TPU:0, one launch (start us, length us, event | category | flops | bytes accessed | tf_op | source)
XLA Modules:
  0.0 145.6 jit_solution(17189478876638232891)
XLA Ops:
  0.6 2.1 %collective-permute-start = (f32[128,2048]{1,0:T(8,128)}, f32[128,2048]{1,0:T(8,128)}, u32[]{:S(2)}, u32[]{:S(2)}) collective-permute-start(f32[128,2048]{1,0:T(8,128)} %refs_0_.1), channel_id=1, source_target_pairs={{0,32},{1,33},{2,34},{3,35},{4,36},{5,37},{6,38},{7,39},{8,40},{9,... | collective-permute-start | bytes 3145736 | tf_op jit(solution)/shard_map/ppermute | solution.py:35
  5.4 2.2 %collective-permute-start.3 = (f32[32,1024]{1,0:T(8,128)S(1)}, f32[32,1024]{1,0:T(8,128)S(1)}, u32[]{:S(2)}, u32[]{:S(2)}) collective-permute-start(f32[32,1024]{1,0:T(8,128)S(1)} %get-tuple-element.160), channel_id=1, source_target_pairs={{0,12},{1,13},{2,14},{3,15},{4,8},{5,9},{6,10},{7,11},{8,4},{9,5},... | collective-permute-start | bytes 393224 | tf_op jit(solution)/shard_map/ppermute | solution.py:26
  8.8 3.1 %collective-permute-start.2 = (f32[64,1024]{1,0:T(8,128)S(1)}, f32[64,1024]{1,0:T(8,128)S(1)}, u32[]{:S(2)}, u32[]{:S(2)}) collective-permute-start(f32[64,1024]{1,0:T(8,128)S(1)} %pad_maximum_fusion.8), channel_id=1, source_target_pairs={{0,12},{1,13},{2,14},{3,15},{4,8},{5,9},{6,10},{7,11},{8,4},{9,5},... | collective-permute-start | bytes 786440 | tf_op jit(solution)/shard_map/ppermute | solution.py:26
  11.9 2.5 %collective-permute-start.9 = (f32[128,2048]{1,0:T(8,128)}, f32[128,2048]{1,0:T(8,128)}, u32[]{:S(2)}, u32[]{:S(2)}) collective-permute-start(f32[128,2048]{1,0:T(8,128)} %refs_0_.1), channel_id=1, source_target_pairs={{0,96},{1,97},{2,98},{3,99},{4,100},{5,101},{6,102},{7,103},{8,104... | collective-permute-start | bytes 3145736 | tf_op jit(solution)/shard_map/ppermute | solution.py:35
  18.0 4.5 %collective-permute-done.4 = f32[64,1024]{1,0:T(8,128)S(1)} collective-permute-done((f32[64,1024]{1,0:T(8,128)S(1)}, f32[64,1024]{1,0:T(8,128)S(1)}, u32[]{:S(2)}, u32[]{:S(2)}) %collective-permute-start.4) | collective-permute-done | bytes 262176 | tf_op jit(solution)/shard_map/ppermute | solution.py:26
  22.6 2.8 %collective-permute-start.13 = (f32[128,1024]{1,0:T(8,128)S(1)}, f32[128,1024]{1,0:T(8,128)S(1)}, u32[]{:S(2)}, u32[]{:S(2)}) collective-permute-start(f32[128,1024]{1,0:T(8,128)S(1)} %pad_maximum_fusion.3), channel_id=1, source_target_pairs={{0,3},{1,2},{2,1},{3,0},{4,7},{5,6},{6,5},{7,4},{8,11},{9,10},{10,... | collective-permute-start | bytes 1572872 | tf_op jit(solution)/shard_map/ppermute | solution.py:26
  26.8 2.8 %collective-permute-start.12 = (f32[256,1024]{1,0:T(8,128)S(1)}, f32[256,1024]{1,0:T(8,128)}, u32[]{:S(2)}, u32[]{:S(2)}) collective-permute-start(f32[256,1024]{1,0:T(8,128)S(1)} %pad_maximum_fusion.refs_3_), channel_id=1, source_target_pairs={{0,3},{1,2},{2,1},{3,0},{4,7},{5,6},{6,5},{7,4},{8,11},{9,10},{10,... | collective-permute-start | bytes 3145736 | tf_op jit(solution)/shard_map/ppermute | solution.py:26
  29.6 3.5 %collective-permute-done.13 = f32[128,1024]{1,0:T(8,128)S(1)} collective-permute-done((f32[128,1024]{1,0:T(8,128)S(1)}, f32[128,1024]{1,0:T(8,128)S(1)}, u32[]{:S(2)}, u32[]{:S(2)}) %collective-permute-start.13) | collective-permute-done | bytes 524320 | tf_op jit(solution)/shard_map/ppermute | solution.py:26
  37.1 4.6 %collective-permute-done.5.refs_1_ = f32[128,2048]{1,0:T(8,128)S(1)} collective-permute-done((f32[128,2048]{1,0:T(8,128)}, f32[128,2048]{1,0:T(8,128)S(1)}, u32[]{:S(2)}, u32[]{:S(2)}) %collective-permute-start.5) | collective-permute-done | bytes 1048608 | tf_op jit(solution)/shard_map/ppermute | solution.py:35
  44.2 3.1 %shard_map.86 = (f32[768,128]{1,0:T(8,128)S(1)}, bf16[768,2048]{1,0:T(8,128)(2,1)S(1)}, bf16[768,2048]{1,0:T(8,128)(2,1)S(1)}) custom-call(f32[128,2048]{1,0:T(8,128)S(1)} %copy-done.1, f32[128,2048]{1,0:T(8,128)S(1)} %copy-done.3, f32[128,2048]{1,0:T(8,128)} %collective-permute-done.refs_2_, f32[128,2048]{1,0:T(8,128)} %collective-permute-done.8.refs_3_, ...), custom_call_target="tpu_custom_call" | custom-call | bytes 12582912 | tf_op jit(solution)/shard_map/pallas_call | solution.py:428
  47.3 3.5 %collective-permute-done.14.refs_6_ = f32[256,1024]{1,0:T(8,128)} collective-permute-done((f32[256,1024]{1,0:T(8,128)}, f32[256,1024]{1,0:T(8,128)}, u32[]{:S(2)}, u32[]{:S(2)}) %collective-permute-start.14) | collective-permute-done | bytes 1048608 | tf_op jit(solution)/shard_map/ppermute | solution.py:26
  50.8 8.6 %shard_map.87 = (bf16[1024,2048]{1,0:T(8,128)(2,1)S(1)}, f32[512,128]{1,0:T(8,128)S(1)}, f32[512,768]{1,0:T(8,128)S(1)}, f32[512,128]{1,0:T(8,128)S(1)}, f32[512,128]{1,0:T(8,128)S(1)}) custom-call(bf16[768,2048]{1,0:T(8,128)(2,1)S(1)} %get-tuple-element.120.refs_0_.refs_3_, bf16[768,2048]{1,0:T(8,128)(2,1)S(1)} %get-tuple-element.121.refs_1_.refs_4_, ...), custom_call_target="tpu_custom_call" | custom-call | flops 4831838208 | bytes 16777216 | tf_op jit(solution)/shard_map/pallas_call | solution.py:442
  59.5 3.4 %shard_map.88 = (f32[512,256]{1,0:T(8,128)S(1)}, f32[16,8,128]{2,1,0:T(8,128)S(1)}, bf16[256,2048]{1,0:T(8,128)(2,1)S(1)}, bf16[256,2048]{1,0:T(8,128)(2,1)S(1)}) custom-call(s32[16]{0:T(128)S(1)} %fusion.refs_0_.rplaces, f32[128,2048]{1,0:T(8,128)S(1)} %collective-permute-done.5.refs_1_, f32[128,2048]{1,0:T(8,128)S(1)} %collective-permute-done.6.refs_2_, ...), custom_call_target="tpu_custom_call" | custom-call | flops 1610612736 | bytes 8388608 | tf_op jit(solution)/shard_map/pallas_call | solution.py:457
  62.8 11.8 %all_to_all.20.got = f32[16,8,128]{2,1,0:T(8,128)S(1)} all-to-all(f32[16,8,128]{2,1,0:T(8,128)S(1)} %get-tuple-element.84), channel_id=1, replica_groups=mesh['row'=8,'col'=16] {'col'}, dimensions={0} | all-to-all | bytes 131072 | tf_op jit(solution)/shard_map/all_to_all | solution.py:475
  76.0 8.9 %all_to_all.21.got = f32[8,16,128]{2,1,0:T(8,128)S(1)} all-to-all(f32[8,16,128]{2,1,0:T(8,128)S(1)} %get-tuple-element.87), channel_id=1, replica_groups=mesh['row'=8,'col'=16] {'row'}, dimensions={0} | all-to-all | bytes 131072 | tf_op jit(solution)/shard_map/all_to_all | solution.py:483
  85.7 10.8 %all_to_all.22.got = f32[16,8,128]{2,1,0:T(8,128)S(1)} all-to-all(f32[16,8,128]{2,1,0:T(8,128)S(1)} %get-tuple-element.89), channel_id=1, replica_groups=mesh['row'=8,'col'=16] {'col'}, dimensions={0} | all-to-all | bytes 131072 | tf_op jit(solution)/shard_map/all_to_all | solution.py:491
  97.5 7.8 %all_to_all.23.got = f32[8,8,128]{2,1,0:T(8,128)S(1)} all-to-all(f32[8,8,128]{2,1,0:T(8,128)S(1)} %shard_map.91), channel_id=1, replica_groups=mesh['row'=8,'col'=16] {'row'}, dimensions={0} | all-to-all | bytes 65536 | tf_op jit(solution)/shard_map/all_to_all | solution.py:499
  110.7 2.1 %collective-permute-start.18 = (f32[8,128,128]{2,1,0:T(8,128)S(1)}, f32[8,128,128]{2,1,0:T(8,128)S(1)}, u32[]{:S(2)}, u32[]{:S(2)}) collective-permute-start(f32[8,128,128]{2,1,0:T(8,128)S(1)} %shard_map.95), channel_id=1, source_target_pairs={{0,3},{1,2},{2,1},{3,0},{4,7},{5,6},{6,5},{7,4},{8,11},{9,10},{10,... | collective-permute-start | bytes 1572872 | tf_op jit(solution)/shard_map/ppermute | solution.py:26
  121.5 2.3 %collective-permute-done.18 = f32[8,128,128]{2,1,0:T(8,128)S(1)} collective-permute-done((f32[8,128,128]{2,1,0:T(8,128)S(1)}, f32[8,128,128]{2,1,0:T(8,128)S(1)}, u32[]{:S(2)}, u32[]{:S(2)}) %collective-permute-start.18) | collective-permute-done | bytes 524320 | tf_op jit(solution)/shard_map/ppermute | solution.py:26
  124.6 2.1 %collective-permute-start.22 = (f32[4,128,128]{2,1,0:T(8,128)S(1)}, f32[4,128,128]{2,1,0:T(8,128)S(1)}, u32[]{:S(2)}, u32[]{:S(2)}) collective-permute-start(f32[4,128,128]{2,1,0:T(8,128)S(1)} %slice.114), channel_id=1, source_target_pairs={{0,3},{1,2},{2,1},{3,0},{4,7},{5,6},{6,5},{7,4},{8,11},{9,10},{10,... | collective-permute-start | bytes 786440 | tf_op jit(solution)/shard_map/ppermute | solution.py:26
  127.9 2.9 %collective-permute-done.20 = f32[4,128,128]{2,1,0:T(8,128)S(1)} collective-permute-done((f32[4,128,128]{2,1,0:T(8,128)S(1)}, f32[4,128,128]{2,1,0:T(8,128)S(1)}, u32[]{:S(2)}, u32[]{:S(2)}) %collective-permute-start.20) | collective-permute-done | bytes 262176 | tf_op jit(solution)/shard_map/ppermute | solution.py:26
  133.8 3.6 %collective-permute-start.23 = (f32[520,128]{1,0:T(8,128)S(1)}, f32[520,128]{1,0:T(8,128)S(1)}, u32[]{:S(2)}, u32[]{:S(2)}) collective-permute-start(f32[520,128]{1,0:T(8,128)S(1)} %pad_maximum_fusion.5), channel_id=1, source_target_pairs={{0,8},{1,9},{2,10},{3,11},{4,12},{5,13},{6,14},{7,15},{8,0},{9,1},... | collective-permute-start | bytes 798728 | tf_op jit(solution)/shard_map/ppermute | solution.py:26
  137.4 2.7 %collective-permute-done.25.four = f32[520,128]{1,0:T(8,128)S(1)} collective-permute-done((f32[520,128]{1,0:T(8,128)S(1)}, f32[520,128]{1,0:T(8,128)S(1)}, u32[]{:S(2)}, u32[]{:S(2)}) %collective-permute-start.25) | collective-permute-done | bytes 266272 | tf_op jit(solution)/shard_map/ppermute | solution.py:26
  140.2 4.4 %collective-permute-done.23.two = f32[520,128]{1,0:T(8,128)S(1)} collective-permute-done((f32[520,128]{1,0:T(8,128)S(1)}, f32[520,128]{1,0:T(8,128)S(1)}, u32[]{:S(2)}, u32[]{:S(2)}) %collective-permute-start.23) | collective-permute-done | bytes 266272 | tf_op jit(solution)/shard_map/ppermute | solution.py:26
  (93 shorter events, 38.6 us)
Async XLA Ops:
  0.6 24.8 %collective-permute-start = (f32[128,2048]{1,0:T(8,128)}, f32[128,2048]{1,0:T(8,128)}, u32[]{:S(2)}, u32[]{:S(2)}) collective-permute-start(f32[128,2048]{1,0:T(8,128)} %refs_0_.1), channel_id=1, source_target_pairs={{0,32},{1,33},{2,34},{3,35},{4,36},{5,37},{6,38},{7,39},{8,40},{9,... | collective-permute-start | bytes 3145736 | tf_op jit(solution)/shard_map/ppermute | solution.py:35
  5.4 9.0 %collective-permute-start.3 = (f32[32,1024]{1,0:T(8,128)S(1)}, f32[32,1024]{1,0:T(8,128)S(1)}, u32[]{:S(2)}, u32[]{:S(2)}) collective-permute-start(f32[32,1024]{1,0:T(8,128)S(1)} %get-tuple-element.160), channel_id=1, source_target_pairs={{0,12},{1,13},{2,14},{3,15},{4,8},{5,9},{6,10},{7,11},{8,4},{9,5},... | collective-permute-start | bytes 393224 | tf_op jit(solution)/shard_map/ppermute | solution.py:26
  8.8 7.7 %collective-permute-start.2 = (f32[64,1024]{1,0:T(8,128)S(1)}, f32[64,1024]{1,0:T(8,128)S(1)}, u32[]{:S(2)}, u32[]{:S(2)}) collective-permute-start(f32[64,1024]{1,0:T(8,128)S(1)} %pad_maximum_fusion.8), channel_id=1, source_target_pairs={{0,12},{1,13},{2,14},{3,15},{4,8},{5,9},{6,10},{7,11},{8,4},{9,5},... | collective-permute-start | bytes 786440 | tf_op jit(solution)/shard_map/ppermute | solution.py:26
  11.9 21.2 %collective-permute-start.9 = (f32[128,2048]{1,0:T(8,128)}, f32[128,2048]{1,0:T(8,128)}, u32[]{:S(2)}, u32[]{:S(2)}) collective-permute-start(f32[128,2048]{1,0:T(8,128)} %refs_0_.1), channel_id=1, source_target_pairs={{0,96},{1,97},{2,98},{3,99},{4,100},{5,101},{6,102},{7,103},{8,104... | collective-permute-start | bytes 3145736 | tf_op jit(solution)/shard_map/ppermute | solution.py:35
  14.5 8.1 %collective-permute-start.4 = (f32[64,1024]{1,0:T(8,128)S(1)}, f32[64,1024]{1,0:T(8,128)S(1)}, u32[]{:S(2)}, u32[]{:S(2)}) collective-permute-start(f32[64,1024]{1,0:T(8,128)S(1)} %pad_maximum_fusion.9), channel_id=1, source_target_pairs={{0,4},{1,5},{2,6},{3,7},{4,0},{5,1},{6,2},{7,3},{8,12},{9,13},{10,... | collective-permute-start | bytes 786440 | tf_op jit(solution)/shard_map/ppermute | solution.py:26
  14.7 20.0 %collective-permute-start.7 = (f32[128,2048]{1,0:T(8,128)}, f32[128,2048]{1,0:T(8,128)S(1)}, u32[]{:S(2)}, u32[]{:S(2)}) collective-permute-start(f32[128,2048]{1,0:T(8,128)} %refs_0_.1), channel_id=1, source_target_pairs={{0,16},{16,0},{32,48},{48,32},{64,80},{80,64},{96,112},{112,96},{1... | collective-permute-start | bytes 3145736 | tf_op jit(solution)/shard_map/ppermute | solution.py:39
  16.5 10.2 %collective-permute-start.11 = (f32[128,1024]{1,0:T(8,128)S(1)}, f32[128,1024]{1,0:T(8,128)S(1)}, u32[]{:S(2)}, u32[]{:S(2)}) collective-permute-start(f32[128,1024]{1,0:T(8,128)S(1)} %pad_maximum_fusion.2), channel_id=1, source_target_pairs={{0,1},{1,0},{2,3},{3,2},{4,5},{5,4},{6,7},{7,6},{8,9},{9,8},{10,11... | collective-permute-start | bytes 1572872 | tf_op jit(solution)/shard_map/ppermute | solution.py:26
  22.6 10.5 %collective-permute-start.13 = (f32[128,1024]{1,0:T(8,128)S(1)}, f32[128,1024]{1,0:T(8,128)S(1)}, u32[]{:S(2)}, u32[]{:S(2)}) collective-permute-start(f32[128,1024]{1,0:T(8,128)S(1)} %pad_maximum_fusion.3), channel_id=1, source_target_pairs={{0,3},{1,2},{2,1},{3,0},{4,7},{5,6},{6,5},{7,4},{8,11},{9,10},{10,... | collective-permute-start | bytes 1572872 | tf_op jit(solution)/shard_map/ppermute | solution.py:26
  25.5 16.2 %collective-permute-start.5 = (f32[128,2048]{1,0:T(8,128)}, f32[128,2048]{1,0:T(8,128)S(1)}, u32[]{:S(2)}, u32[]{:S(2)}) collective-permute-start(f32[128,2048]{1,0:T(8,128)} %collective-permute-done.refs_2_), channel_id=1, source_target_pairs={{0,96},{1,97},{2,98},{3,99},{4,100},{5,101},{6,102},{7,103},{8,104... | collective-permute-start | bytes 3145736 | tf_op jit(solution)/shard_map/ppermute | solution.py:35
  26.8 20.5 %collective-permute-start.12 = (f32[256,1024]{1,0:T(8,128)S(1)}, f32[256,1024]{1,0:T(8,128)}, u32[]{:S(2)}, u32[]{:S(2)}) collective-permute-start(f32[256,1024]{1,0:T(8,128)S(1)} %pad_maximum_fusion.refs_3_), channel_id=1, source_target_pairs={{0,3},{1,2},{2,1},{3,0},{4,7},{5,6},{6,5},{7,4},{8,11},{9,10},{10,... | collective-permute-start | bytes 3145736 | tf_op jit(solution)/shard_map/ppermute | solution.py:26
  33.1 8.7 %collective-permute-start.8 = (f32[128,2048]{1,0:T(8,128)}, f32[128,2048]{1,0:T(8,128)}, u32[]{:S(2)}, u32[]{:S(2)}) collective-permute-start(f32[128,2048]{1,0:T(8,128)} %collective-permute-done.refs_2_), channel_id=1, source_target_pairs={{0,16},{16,0},{32,48},{48,32},{64,80},{80,64},{96,112},{112,96},{1... | collective-permute-start | bytes 3145736 | tf_op jit(solution)/shard_map/ppermute | solution.py:39
  33.1 8.7 %collective-permute-start.10 = (f32[128,2048]{1,0:T(8,128)}, f32[128,2048]{1,0:T(8,128)}, u32[]{:S(2)}, u32[]{:S(2)}) collective-permute-start(f32[128,2048]{1,0:T(8,128)} %collective-permute-done.9.refs_4_), channel_id=1, source_target_pairs={{0,16},{16,0},{32,48},{48,32},{64,80},{80,64},{96,112},{112,96},{1... | collective-permute-start | bytes 3145736 | tf_op jit(solution)/shard_map/ppermute | solution.py:39
  35.7 15.1 %collective-permute-start.14 = (f32[256,1024]{1,0:T(8,128)}, f32[256,1024]{1,0:T(8,128)}, u32[]{:S(2)}, u32[]{:S(2)}) collective-permute-start(f32[256,1024]{1,0:T(8,128)} %pad_maximum_fusion.1.refs_5_), channel_id=1, source_target_pairs={{0,1},{1,0},{2,3},{3,2},{4,5},{5,4},{6,7},{7,6},{8,9},{9,8},{10,11... | collective-permute-start | bytes 3145736 | tf_op jit(solution)/shard_map/ppermute | solution.py:26
  41.7 17.8 %collective-permute-start.6 = (f32[128,2048]{1,0:T(8,128)S(1)}, f32[128,2048]{1,0:T(8,128)S(1)}, u32[]{:S(2)}, u32[]{:S(2)}) collective-permute-start(f32[128,2048]{1,0:T(8,128)S(1)} %collective-permute-done.5.refs_1_), channel_id=1, source_target_pairs={{0,16},{16,0},{32,48},{48,32},{64,80},{80,64},{96,112},{112,96},{1... | collective-permute-start | bytes 3145736 | tf_op jit(solution)/shard_map/ppermute | solution.py:39
  107.3 10.8 %collective-permute-start.15 = (f32[8,136,128]{2,1,0:T(8,128)S(1)}, f32[8,136,128]{2,1,0:T(8,128)S(1)}, u32[]{:S(2)}, u32[]{:S(2)}) collective-permute-start(f32[8,136,128]{2,1,0:T(8,128)S(1)} %shard_map.93), channel_id=1, source_target_pairs={{0,3},{1,2},{2,1},{3,0},{4,7},{5,6},{6,5},{7,4},{8,11},{9,10},{10,... | collective-permute-start | bytes 1671176 | tf_op jit(solution)/shard_map/ppermute | solution.py:26
  109.5 10.6 %collective-permute-start.19 = (f32[8,128,128]{2,1,0:T(8,128)S(1)}, f32[8,128,128]{2,1,0:T(8,128)S(1)}, u32[]{:S(2)}, u32[]{:S(2)}) collective-permute-start(f32[8,128,128]{2,1,0:T(8,128)S(1)} %shard_map.94), channel_id=1, source_target_pairs={{0,1},{1,0},{2,3},{3,2},{4,5},{5,4},{6,7},{7,6},{8,9},{9,8},{10,11... | collective-permute-start | bytes 1572872 | tf_op jit(solution)/shard_map/ppermute | solution.py:26
  110.7 13.0 %collective-permute-start.18 = (f32[8,128,128]{2,1,0:T(8,128)S(1)}, f32[8,128,128]{2,1,0:T(8,128)S(1)}, u32[]{:S(2)}, u32[]{:S(2)}) collective-permute-start(f32[8,128,128]{2,1,0:T(8,128)S(1)} %shard_map.95), channel_id=1, source_target_pairs={{0,3},{1,2},{2,1},{3,0},{4,7},{5,6},{6,5},{7,4},{8,11},{9,10},{10,... | collective-permute-start | bytes 1572872 | tf_op jit(solution)/shard_map/ppermute | solution.py:26
  113.8 10.7 %collective-permute-start.17 = (f32[8,128,128]{2,1,0:T(8,128)S(1)}, f32[8,128,128]{2,1,0:T(8,128)S(1)}, u32[]{:S(2)}, u32[]{:S(2)}) collective-permute-start(f32[8,128,128]{2,1,0:T(8,128)S(1)} %shard_map.96), channel_id=1, source_target_pairs={{0,1},{1,0},{2,3},{3,2},{4,5},{5,4},{6,7},{7,6},{8,9},{9,8},{10,11... | collective-permute-start | bytes 1572872 | tf_op jit(solution)/shard_map/ppermute | solution.py:26
  118.2 9.2 %collective-permute-start.16 = (f32[4,136,128]{2,1,0:T(8,128)S(1)}, f32[4,136,128]{2,1,0:T(8,128)S(1)}, u32[]{:S(2)}, u32[]{:S(2)}) collective-permute-start(f32[4,136,128]{2,1,0:T(8,128)S(1)} %slice.105), channel_id=1, source_target_pairs={{0,1},{1,0},{2,3},{3,2},{4,5},{5,4},{6,7},{7,6},{8,9},{9,8},{10,11... | collective-permute-start | bytes 835592 | tf_op jit(solution)/shard_map/ppermute | solution.py:26
  120.2 7.7 %collective-permute-start.21 = (f32[4,128,128]{2,1,0:T(8,128)S(1)}, f32[4,128,128]{2,1,0:T(8,128)S(1)}, u32[]{:S(2)}, u32[]{:S(2)}) collective-permute-start(f32[4,128,128]{2,1,0:T(8,128)S(1)} %slice.110), channel_id=1, source_target_pairs={{0,3},{1,2},{2,1},{3,0},{4,7},{5,6},{6,5},{7,4},{8,11},{9,10},{10,... | collective-permute-start | bytes 786440 | tf_op jit(solution)/shard_map/ppermute | solution.py:26
  124.6 7.7 %collective-permute-start.22 = (f32[4,128,128]{2,1,0:T(8,128)S(1)}, f32[4,128,128]{2,1,0:T(8,128)S(1)}, u32[]{:S(2)}, u32[]{:S(2)}) collective-permute-start(f32[4,128,128]{2,1,0:T(8,128)S(1)} %slice.114), channel_id=1, source_target_pairs={{0,3},{1,2},{2,1},{3,0},{4,7},{5,6},{6,5},{7,4},{8,11},{9,10},{10,... | collective-permute-start | bytes 786440 | tf_op jit(solution)/shard_map/ppermute | solution.py:26
  132.4 7.7 %collective-permute-start.25 = (f32[520,128]{1,0:T(8,128)S(1)}, f32[520,128]{1,0:T(8,128)S(1)}, u32[]{:S(2)}, u32[]{:S(2)}) collective-permute-start(f32[520,128]{1,0:T(8,128)S(1)} %pad_maximum_fusion.7), channel_id=1, source_target_pairs={{0,12},{1,13},{2,14},{3,15},{4,8},{5,9},{6,10},{7,11},{8,4},{9,5},... | collective-permute-start | bytes 798728 | tf_op jit(solution)/shard_map/ppermute | solution.py:26
  133.7 6.5 %collective-permute-start.24 = (f32[520,128]{1,0:T(8,128)S(1)}, f32[520,128]{1,0:T(8,128)S(1)}, u32[]{:S(2)}, u32[]{:S(2)}) collective-permute-start(f32[520,128]{1,0:T(8,128)S(1)} %pad_maximum_fusion.6), channel_id=1, source_target_pairs={{0,4},{1,5},{2,6},{3,7},{4,0},{5,1},{6,2},{7,3},{8,12},{9,13},{10,... | collective-permute-start | bytes 798728 | tf_op jit(solution)/shard_map/ppermute | solution.py:26
  133.8 10.7 %collective-permute-start.23 = (f32[520,128]{1,0:T(8,128)S(1)}, f32[520,128]{1,0:T(8,128)S(1)}, u32[]{:S(2)}, u32[]{:S(2)}) collective-permute-start(f32[520,128]{1,0:T(8,128)S(1)} %pad_maximum_fusion.5), channel_id=1, source_target_pairs={{0,8},{1,9},{2,10},{3,11},{4,12},{5,13},{6,14},{7,15},{8,0},{9,1},... | collective-permute-start | bytes 798728 | tf_op jit(solution)/shard_map/ppermute | solution.py:26
  (11 other events, 158.3 us)
